TPU v7x, 128 devices: a whole 4x4x4 slice. The times are simulated.
128 devices in a mesh: node: 8 (over y, core), local: 4 (over z), cuts: 4 (over x).
Axes of the slice: x: 4, y: 4, z: 4, core: 2. Of those that a mesh axis runs over, the one named last changes fastest.
Arguments:
- tokens: bfloat16 [4096, 2048], P(('node', 'local'), 'cuts'), may hold values from -6 to 6
- routes: int32 [4096, 8], P(('node', 'local')), may hold values from 0 to 127, all different within a row; in each aligned block of 128 rows (0 to 127, 128 to 255, ...) at most 12 rows name the same one
- gates: bfloat16 [4096, 8], P(('node', 'local')), may hold values from 0.049804688 to 0.29882812
- cotangent: bfloat16 [4096, 2048], P(('node', 'local'), 'cuts'), may hold values from -6 to 6
- w_gate: bfloat16 [128, 768, 2048], P(('node', 'local'), 'cuts'), may hold values from -0.125 to 0.125
- w_up: bfloat16 [128, 768, 2048], P(('node', 'local'), 'cuts'), may hold values from -0.125 to 0.125
- w_down: bfloat16 [128, 768, 2048], P(('node', 'local'), 'cuts'), may hold values from -0.21875 to 0.21875
Outputs:
- mixed: bfloat16 [4096, 2048], P(('node', 'local'), 'cuts')
- grad_tokens: bfloat16 [4096, 2048], P(('node', 'local'), 'cuts')
- grad_gate: bfloat16 [128, 768, 2048], P(('node', 'local'), 'cuts')
- grad_up: bfloat16 [128, 768, 2048], P(('node', 'local'), 'cuts')
- grad_down: bfloat16 [128, 768, 2048], P(('node', 'local'), 'cuts')
Inputs may be any that keep to these rules, and one draw needn't show every extreme that they name: `routes`: each row names 8 different experts. Within each aligned block of 128 rows (the tokens of one index of node and local) no expert is named more than 12 times, and in every draw some expert is named exactly 12 times in some block.
All inputs are finite; a program needn't handle non-finite values.
Results may differ from a plain program's by a relative error of at most 0.015.
Values may be sent and summed in bfloat16 or wider, within the bound.
No kernel may reach another device: no remote copies, remote signals or barrier semaphores. Data moves between devices by JAX's collectives and lax.ppermute only.
A program may use at most 128 MiB of HBM per device.

v0:
```python
import functools

import jax
import jax.numpy as jnp
from jax import lax
from jax.experimental import pallas as pl
from jax.experimental.pallas import tpu as pltpu
from jax.sharding import Mesh
from jax.sharding import PartitionSpec as P

BF = jnp.bfloat16
F32 = jnp.float32
CAP = 12
GROUP = ("y", "c", "z")
VMEM_LIMIT = 52 * 1024 * 1024


def fetch(a, axis, r):
    n = lax.axis_size(axis)
    return lax.ppermute(a, axis, [((i + r) % n, i) for i in range(n)])


def add(*terms):
    total = terms[0].astype(F32)
    for term in terms[1:]:
        total = total + term.astype(F32)
    return total.astype(BF)


def nt(a, b):
    return lax.dot_general(a, b, (((1,), (1,)), ((), ())), preferred_element_type=F32)


def tn(a, b):
    return lax.dot_general(a, b, (((0,), (0,)), ((), ())), preferred_element_type=F32)


def nn(a, b):
    return jnp.dot(a, b, preferred_element_type=F32)


def slot_map(ids_ref, meta, n_exp):
    tok = meta[0].shape[1]
    y, z, c = ids_ref[0], ids_ref[1], ids_ref[2]
    top = meta[0].shape[0] // 2
    both = 2 * n_exp
    line = lax.broadcasted_iota(jnp.int32, (both, tok), 0)
    core = jnp.where(line < n_exp, c, 1 - c)
    expert = (y * 2 + core) * 4 + z
    expert = (expert * n_exp + lax.rem(line, n_exp)).astype(F32)
    earlier = (
        lax.broadcasted_iota(jnp.int32, (tok, tok), 0) < lax.broadcasted_iota(jnp.int32, (tok, tok), 1)
    ).astype(BF)
    widen = (
        lax.broadcasted_iota(jnp.int32, (both * 4, both), 0) // 4
        == lax.broadcasted_iota(jnp.int32, (both * 4, both), 1)
    ).astype(BF)
    owner = lax.rem(lax.broadcasted_iota(jnp.int32, (both * 4, tok), 0), 4)
    slots = both * 4 * CAP
    repeat = (
        lax.broadcasted_iota(jnp.int32, (slots, both * 4), 0) // CAP
        == lax.broadcasted_iota(jnp.int32, (slots, both * 4), 1)
    ).astype(BF)
    slot = lax.rem(lax.broadcasted_iota(jnp.int32, (slots, tok), 0), CAP).astype(F32)
    columns = []
    for zz in range(4):
        data = meta[zz].astype(F32)
        named = jnp.zeros((both, tok), F32)
        gate = jnp.zeros((both, tok), F32)
        for k in range(top):
            same = data[k : k + 1] == expert
            named = jnp.where(same, 1.0, named)
            gate = jnp.where(same, data[top + k : top + k + 1], gate)
        rank = jnp.where(named > 0, nn(named.astype(BF), earlier), -1.0)
        here = owner == zz
        rank = jnp.where(here, nn(widen, rank.astype(BF)), -1.0).astype(BF)
        gate = nn(widen, gate.astype(BF)).astype(BF)
        columns.append(jnp.where(nn(repeat, rank) == slot, nn(repeat, gate), 0.0).astype(BF))
    return jnp.concatenate(columns, axis=1)


def pick_kernel(ids_ref, whole_ref, own_ref, sib_ref, maps_ref):
    n_exp, span = own_ref.shape[:2]
    tok, width = 128, whole_ref.shape[2]
    n = own_ref.shape[2] // width
    slots = slot_map(ids_ref, [whole_ref[z, n * tok :, :tok] for z in range(4)], n_exp)
    maps_ref[0] = slots
    for r in range(n):
        block = jnp.concatenate([whole_ref[z, r * tok : (r + 1) * tok] for z in range(4)], axis=0)
        picked = nn(slots, block).astype(BF)
        cols = slice(r * width, (r + 1) * width)
        for e in range(n_exp):
            own_ref[e, :, cols] = picked[e * span : (e + 1) * span]
            lo = (n_exp + e) * span
            sib_ref[e, :, cols] = picked[lo : lo + span]


def pick(ids, whole, n_exp):
    width = whole.shape[2]
    span = 4 * CAP
    rows = jax.ShapeDtypeStruct((n_exp, 4 * span, 4 * width), BF)
    maps = jax.ShapeDtypeStruct((4, 2 * n_exp * span, 4 * 128), BF)
    rows_spec = pl.BlockSpec((n_exp, span, 4 * width), lambda i: (0, i, 0))
    return pl.pallas_call(
        pick_kernel,
        grid=(4,),
        out_shape=(rows, rows, maps),
        in_specs=[
            pl.BlockSpec(memory_space=pltpu.SMEM),
            pl.BlockSpec((4,) + whole.shape[1:], lambda i: (i, 0, 0)),
        ],
        out_specs=(rows_spec, rows_spec, pl.BlockSpec((1,) + maps.shape[1:], lambda i: (i, 0, 0))),
        compiler_params=pltpu.CompilerParams(vmem_limit_bytes=VMEM_LIMIT),
        cost_estimate=pl.CostEstimate(flops=4 << 30, bytes_accessed=18 << 20, transcendentals=0),
    )(ids, whole)


def sum_kernel(ids_ref, map_ref, own_ref, sib_ref, *outs):
    by_y, by_z = outs[:5], outs[5:]
    yr = pl.program_id(0)
    z = ids_ref[1]
    n_exp = own_ref.shape[0]
    tok, width = 128, own_ref.shape[2] // 4
    rows = jnp.concatenate(
        [ref[e] for ref in (own_ref, sib_ref) for e in range(n_exp)], axis=0
    )
    for zr in range(4):
        there = pl.multiple_of(lax.rem(z + zr, 4) * tok, tok)
        total = tn(map_ref[0, :, pl.ds(there, tok)], rows).astype(BF)
        cut = [total[:, r * width : (r + 1) * width] for r in range(4)]
        y_dest = (by_y[0], by_y[1], by_y[2 + zr // 2], by_y[4])
        for i in range(4):

            @pl.when(yr == i)
            def _(i=i):
                at = zr % 2 if i == 2 else zr
                y_dest[i][at, 0], y_dest[i][at, 1] = cut[0], cut[1]

        if zr == 2:
            for part in range(2):

                @pl.when(yr // 2 == part)
                def _(part=part):
                    at = yr - 2 * part
                    by_z[2 + part][at, 0], by_z[2 + part][at, 1] = cut[2], cut[3]

        else:
            ref = by_z[(0, 1, None, 4)[zr]]
            ref[yr, 0], ref[yr, 1] = cut[2], cut[3]


def sum_tokens(ids, maps, own, sib):
    n_exp, rows, cols = own.shape
    whole = jax.ShapeDtypeStruct((4, 2, 128, cols // 4), BF)
    half = jax.ShapeDtypeStruct((2,) + whole.shape[1:], BF)
    outs = (whole, whole, half, half, whole) * 2
    at = lambda i, ids: lax.rem(ids[0] + i, 4)
    rows_spec = pl.BlockSpec((n_exp, rows // 4, cols), lambda i, ids: (0, at(i, ids), 0))
    keep = lambda a: pl.BlockSpec(a.shape, lambda i, ids: (0,) * 4)
    return pl.pallas_call(
        sum_kernel,
        grid_spec=pltpu.PrefetchScalarGridSpec(
            num_scalar_prefetch=1,
            grid=(4,),
            in_specs=[
                pl.BlockSpec((1,) + maps.shape[1:], lambda i, ids: (at(i, ids), 0, 0)),
                rows_spec,
                rows_spec,
            ],
            out_specs=tuple(keep(a) for a in outs),
        ),
        out_shape=outs,
        compiler_params=pltpu.CompilerParams(vmem_limit_bytes=VMEM_LIMIT),
        cost_estimate=pl.CostEstimate(flops=4 << 30, bytes_accessed=16 << 20, transcendentals=0),
    )(ids, maps, own, sib)


def moved_columns(me, n, width):
    return [pl.ds(pl.multiple_of(lax.rem(me + r, n) * width, width), width) for r in range(n)]


def x_rows_of(c, refs):
    x0, x1, lo, hi, x3 = refs
    both = lambda ref: jnp.concatenate([ref[0, c], ref[0, 1 - c]], axis=0)
    far = jnp.where(pl.program_id(0) < 2, both(lo), both(hi))
    return [both(x0), both(x1), far, both(x3)]


def forward_kernel(ids_ref, *refs):
    x_refs, refs = refs[:5], refs[5:]
    own, sib, wg, wu, wd, oo, os, hid_ref, da_ref, db_ref = refs
    half, cols = own.shape[1:]
    n, width = 4, cols // 4
    fixed = [slice(r * width, (r + 1) * width) for r in range(n)]
    moved = moved_columns(ids_ref[3], n, width)
    x_rows = x_rows_of(ids_ref[2], x_refs)
    g_rows = [jnp.concatenate([own[0, :, f], sib[0, :, f]], axis=0) for f in fixed]
    a = sum(nt(x_rows[r], wg[0, :, moved[r]]) for r in range(n))
    b = sum(nt(x_rows[r], wu[0, :, moved[r]]) for r in range(n))
    gh = sum(nt(g_rows[r], wd[0, :, moved[r]]) for r in range(n))
    s = jax.nn.sigmoid(a)
    act = a * s
    hidden = (act * b).astype(BF)
    hid_ref[0] = hidden
    da_ref[0] = (gh * b * s * (1.0 + a * (1.0 - s))).astype(BF)
    db_ref[0] = (gh * act).astype(BF)
    for r in range(n):
        out = nn(hidden, wd[0, :, moved[r]]).astype(BF)
        oo[0, :, fixed[r]] = out[:half]
        os[0, :, fixed[r]] = out[half:]


def back_kernel(ids_ref, da_ref, db_ref, wg, wu, back_ref):
    c = ids_ref[2]
    n = back_ref.shape[0]
    half, width = back_ref.shape[3:]
    da, db = da_ref[0], db_ref[0]
    for r in range(n):
        cols = slice(r * width, (r + 1) * width)
        back = (nn(da, wg[0, :, cols]) + nn(db, wu[0, :, cols])).astype(BF)
        back_ref[r, 0, c] = back[:half]
        back_ref[r, 0, 1 - c] = back[half:]


def weights_kernel(ids_ref, *refs):
    x_refs, refs = refs[:5], refs[5:]
    own, sib, hid_ref, da_ref, db_ref, dwg, dwu, dwd = refs
    cols = own.shape[2]
    n, width = 4, cols // 4
    fixed = [slice(r * width, (r + 1) * width) for r in range(n)]
    moved = moved_columns(ids_ref[3], n, width)
    x_rows = x_rows_of(ids_ref[2], x_refs)
    hidden, da, db = hid_ref[0], da_ref[0], db_ref[0]
    for r in range(n):
        g_rows = jnp.concatenate([own[0, :, fixed[r]], sib[0, :, fixed[r]]], axis=0)
        dwg[0, :, moved[r]] = tn(da, x_rows[r]).astype(BF)
        dwu[0, :, moved[r]] = tn(db, x_rows[r]).astype(BF)
        dwd[0, :, moved[r]] = tn(hidden, g_rows).astype(BF)


def each(a):
    return pl.BlockSpec((1,) + a.shape[1:], lambda i: (i,) + (0,) * (a.ndim - 1))


def each_x(blocks):
    specs = [each(a) for a in blocks]
    lo, hi = blocks[2], blocks[3]
    specs[2] = pl.BlockSpec((1,) + lo.shape[1:], lambda i: (jnp.minimum(i, 1), 0, 0, 0))
    specs[3] = pl.BlockSpec((1,) + hi.shape[1:], lambda i: (jnp.maximum(i - 2, 0), 0, 0, 0))
    return specs


def per_expert(kernel, ids, in_specs, args, outs, out_specs, products, mebibytes):
    n_exp = 4
    return pl.pallas_call(
        kernel,
        grid=(n_exp,),
        out_shape=outs,
        in_specs=[pl.BlockSpec(memory_space=pltpu.SMEM)] + in_specs,
        out_specs=out_specs,
        compiler_params=pltpu.CompilerParams(vmem_limit_bytes=VMEM_LIMIT),
        cost_estimate=pl.CostEstimate(
            flops=products * (1536 * 192 * 2048 * 3), bytes_accessed=mebibytes << 20, transcendentals=0
        ),
    )(ids, *args)


def forward(ids, x, g, weights):
    n_exp, rows, _ = g[0].shape
    mid = jax.ShapeDtypeStruct((n_exp, 2 * rows, weights[0].shape[1]), BF)
    out = jax.ShapeDtypeStruct(g[0].shape, BF)
    outs = (out, out, mid, mid, mid)
    args = tuple(x) + tuple(g) + tuple(weights)
    specs = each_x(x) + [each(a) for a in tuple(g) + tuple(weights)]
    return per_expert(forward_kernel, ids, specs, args, outs, tuple(each(a) for a in outs), 4, 30)


def backward(ids, mids, weights, shape):
    back = jax.ShapeDtypeStruct((4,) + shape, BF)
    args = tuple(mids) + tuple(weights)
    spec = pl.BlockSpec((4, 1) + shape[1:], lambda i: (0, i, 0, 0, 0))
    return per_expert(back_kernel, ids, [each(a) for a in args], args, back, spec, 2, 14)


def weight_grads(ids, x, g, mids, like):
    outs = (jax.ShapeDtypeStruct(like.shape, BF),) * 3
    args = tuple(x) + tuple(g) + tuple(mids)
    specs = each_x(x) + [each(a) for a in tuple(g) + tuple(mids)]
    return per_expert(weights_kernel, ids, specs, args, outs, tuple(each(a) for a in outs), 3, 24)


def collect_far(parts, axis):
    own, up, far_lo, far_hi, down = parts
    half = far_lo.shape[0]
    got_lo, got_hi = fetch(far_lo, axis, -1), fetch(far_hi, axis, 1)
    up = jnp.concatenate([add(up[:half], got_lo), up[half:]])
    down = jnp.concatenate([down[:half], add(down[half:], got_hi)])
    return own, up, down


def collect_near(parts, axis):
    own, up, down = parts
    return add(own, fetch(up, axis, -1), fetch(down, axis, 1))


def collect_small(parts, axis):
    return add(parts[0], *[fetch(parts[r], axis, -r) for r in (1, 2, 3)])


def ranks(named):
    tok = named.shape[-1]
    earlier = jnp.arange(tok)[:, None] < jnp.arange(tok)[None, :]
    count = jnp.dot(named.astype(BF), earlier.astype(BF), preferred_element_type=F32)
    return jnp.where(named > 0, count, -1.0)


def body(tokens, routes, gates, cotangent, w_gate, w_up, w_down):
    y, c, z, x = (lax.axis_index(a) for a in ("y", "c", "z", "x"))
    ids = jnp.stack([y, z, c, x]).astype(jnp.int32)
    n_exp = w_gate.shape[0]
    total_exp = n_exp * 32
    tok, width = tokens.shape
    weights = (w_gate, w_up, w_down)

    cot = [cotangent] + [fetch(cotangent, "x", r) for r in (1, 2, 3)]
    routes_t = routes.T
    meta = jnp.concatenate([routes_t.astype(BF), gates.T], axis=0)
    meta = jnp.pad(meta, ((0, 0), (0, width - tok)))
    whole = lax.all_gather(jnp.concatenate(cot + [meta]), ("y", "z"))

    experts_all = jnp.arange(total_exp, dtype=jnp.int32)
    named = jnp.sum((routes_t[:, None, :] == experts_all[None, :, None]).astype(F32), axis=0)
    place = ranks(named).astype(BF)
    slots = total_exp * CAP
    slot = jnp.arange(slots, dtype=jnp.int32)
    repeat = (slot[:, None] // CAP == experts_all[None, :]).astype(BF)
    place_rep = jnp.dot(repeat, place, preferred_element_type=F32)
    own_map = (place_rep == (slot % CAP).astype(F32)[:, None]).astype(BF)

    def exchange(a):
        return lax.all_to_all(a, GROUP, split_axis=0, concat_axis=0, tiled=True)

    came = exchange(jnp.dot(own_map, tokens, preferred_element_type=F32).astype(BF))
    came = came.reshape(4, 2, 4, n_exp, CAP, width).transpose(3, 1, 0, 2, 4, 5)
    came = came.reshape(n_exp, 2, 16 * CAP, width)
    up, down = fetch(came, "x", 1), fetch(came, "x", -1)
    whole, up, down = lax.optimization_barrier((whole, up, down))
    pair = n_exp // 2
    x_blocks = (came, up, fetch(down[:pair], "x", -1), fetch(up[pair:], "x", 1), down)

    own, sib, maps = pick(ids, whole, n_exp)
    sib, far_lo, far_hi = lax.optimization_barrier((sib, x_blocks[2], x_blocks[3]))
    x_blocks = (came, up, far_lo, far_hi, down)
    g_blocks = (own, fetch(sib, "c", 1))
    out_own, out_sib, hidden, grad_a, grad_b = forward(ids, x_blocks, g_blocks, weights)
    out_sib = fetch(out_sib, "c", 1)
    back = backward(ids, (grad_a, grad_b), weights[:2], came.shape)
    back = lax.psum_scatter(back.reshape(-1, width), "x", scatter_dimension=0, tiled=True)

    sums = sum_tokens(ids, maps, out_own, out_sib)
    ends_y, ends_z = collect_far(sums[:5], "y"), collect_far(sums[5:], "z")
    hidden, ends_y, ends_z = lax.optimization_barrier((hidden, ends_y, ends_z))
    grads = weight_grads(ids, x_blocks, g_blocks, (hidden, grad_a, grad_b), w_gate)
    part1, part2 = collect_near(ends_y, "y"), collect_near(ends_z, "z")

    back = back.reshape(n_exp, 2, 4, 4, CAP, width).transpose(2, 1, 3, 0, 4, 5)
    back = back.reshape(slots, width)
    grads, back, part1, part2 = lax.optimization_barrier((grads, back, part1, part2))
    back = exchange(back)
    part1, part2 = collect_small(part1, "z"), collect_small(part2, "y")
    back, part1, part2 = lax.optimization_barrier((back, part1, part2))
    mixed = collect_small((part1[0], part1[1], part2[0], part2[1]), "x")
    grad_tokens = tn(own_map, back).astype(BF)
    return (mixed, grad_tokens) + tuple(grads)


def solution(mesh):
    split = Mesh(mesh.devices.reshape(4, 2, 4, 4), ("y", "c", "z", "x"))
    acts = P(GROUP, "x")
    rows = P(GROUP, None)
    wts = P(GROUP, "x", None)
    return jax.shard_map(
        body,
        mesh=split,
        in_specs=(acts, rows, rows, acts, wts, wts, wts),
        out_specs=(acts, acts, wts, wts, wts),
        check_vma=False,
    )
```

profile of v0, /device:TPU:0, one launch (start us, length us, event | category | flops | bytes accessed | tf_op | source)
XLA Modules:
  0.0 297.4 jit_solution(291031679174972200)
XLA Ops:
  7.2 3.2 %collective-permute-start.1 = (bf16[128,512]{1,0:T(8,128)(2,1)}, bf16[128,512]{1,0:T(8,128)(2,1)S(1)}, u32[]{:S(2)}, u32[]{:S(2)}) collective-permute-start(bf16[128,512]{1,0:T(8,128)(2,1)} %param.10), channel_id=1, source_target_pairs={{2,0},{3,1},{0,2},{1,3},{6,4},{7,5},{4,6},{5,7},{10,8},{11,9},{8,1... | collective-permute-start | bytes 393224 | tf_op jit(solution)/shard_map/ppermute | solution.py:20
  14.0 3.2 %collective-permute-done = bf16[128,512]{1,0:T(8,128)(2,1)S(1)} collective-permute-done((bf16[128,512]{1,0:T(8,128)(2,1)}, bf16[128,512]{1,0:T(8,128)(2,1)S(1)}, u32[]{:S(2)}, u32[]{:S(2)}) %collective-permute-start) | collective-permute-done | bytes 131104 | tf_op jit(solution)/shard_map/ppermute | solution.py:20
  21.4 39.8 %all_to_all.21 = bf16[32,48,512]{2,1,0:T(8,128)(2,1)S(1)} all-to-all(bf16[32,48,512]{2,1,0:T(8,128)(2,1)S(1)} %bitcast.53), channel_id=1, replica_groups=mesh['y'=4,'c'=2,'z'=4,'x'=4] {'y','c','z'}, dimensions={0} | all-to-all | bytes 3145728 | tf_op jit(solution)/shard_map/all_to_all | solution.py:341
  65.2 2.5 collective-permute-start.3
  67.7 33.8 %collective-permute-done.4.refs_4_ = bf16[4,2,192,512]{3,2,1,0:T(8,128)(2,1)S(1)} collective-permute-done((bf16[4,2,192,512]{3,2,1,0:T(8,128)(2,1)S(1)}, bf16[4,2,192,512]{3,2,1,0:T(8,128)(2,1)S(1)}, u32[]{:S(2)}, u32[]{:S(2)}) %collective-permute-start.4) | collective-permute-done | bytes 1572896 | tf_op jit(solution)/shard_map/ppermute | solution.py:20
  101.5 3.3 %all-gather.3.cloned.1.call-done = bf16[8448,512]{1,0:T(8,128)(2,1)} async-done(((bf16[528,512]{1,0:T(8,128)(2,1)}), bf16[8448,512]{1,0:T(8,128)(2,1)}) %all-gather.3.cloned.1.call-update) | async-done | bytes 8650768 | tf_op jit(solution)/shard_map/all_gather | solution.py:329
  104.8 2.1 slice.67
  111.2 11.5 %shard_map.110 = (bf16[4,192,2048]{2,1,0:T(8,128)(2,1)}, bf16[4,192,2048]{2,1,0:T(8,128)(2,1)}, bf16[4,384,512]{2,1,0:T(8,128)(2,1)S(1)}) custom-call(s32[4]{0:T(128)S(1)} %pad_add_fusion.ids_ref, bf16[16,528,512]{2,1,0:T(8,128)(2,1)} %bitcast.56), custom_call_target="tpu_custom_call" | custom-call | flops 4294967296 | bytes 18874368 | tf_op jit(solution)/shard_map/pallas_call | solution.py:104
  123.8 4.8 %collective-permute-done.5.refs_2_ = bf16[2,2,192,512]{3,2,1,0:T(8,128)(2,1)S(1)} collective-permute-done((bf16[2,2,192,512]{3,2,1,0:T(8,128)(2,1)}, bf16[2,2,192,512]{3,2,1,0:T(8,128)(2,1)S(1)}, u32[]{:S(2)}, u32[]{:S(2)}) %collective-permute-start.5) | collective-permute-done | bytes 786464 | tf_op jit(solution)/shard_map/ppermute | solution.py:20
  128.7 5.9 %collective-permute-done.7.refs_6_ = bf16[4,192,2048]{2,1,0:T(8,128)(2,1)S(1)} collective-permute-done((bf16[4,192,2048]{2,1,0:T(8,128)(2,1)}, bf16[4,192,2048]{2,1,0:T(8,128)(2,1)S(1)}, u32[]{:S(2)}, u32[]{:S(2)}) %collective-permute-start.7) | collective-permute-done | bytes 3145760 | tf_op jit(solution)/shard_map/ppermute | solution.py:20
  136.2 13.2 %shard_map.111 = (bf16[4,192,2048]{2,1,0:T(8,128)(2,1)}, bf16[4,192,2048]{2,1,0:T(8,128)(2,1)}, bf16[4,384,192]{2,1,0:T(8,128)(2,1)S(1)}, bf16[4,384,192]{2,1,0:T(8,128)(2,1)S(1)}, bf16[4,384,192]{2,1,0:T(8,128)(2,1)}) custom-call(s32[4]{0:T(128)S(1)} %pad_add_fusion.ids_ref, bf16[4,2,192,512]{3,2,1,0:T(8,128)(2,1)} %copy-done.10, ...), custom_call_target="tpu_custom_call" | custom-call | flops 7247757312 | bytes 31457280 | tf_op jit(solution)/shard_map/pallas_call | solution.py:255
  151.7 7.6 %shard_map.114 = bf16[4,4,2,192,512]{4,3,2,1,0:T(8,128)(2,1)} custom-call(s32[4]{0:T(128)S(1)} %pad_add_fusion.ids_ref, bf16[4,384,192]{2,1,0:T(8,128)(2,1)S(1)} %get-tuple-element.71.refs_8_.da_ref, bf16[4,384,192]{2,1,0:T(8,128)(2,1)S(1)} %copy-done.3, bf16[4,192,2048]{2,1,0:T(8,128)(2,1)} %wg.1, bf16[4,192,2048]{2,1,0:T(8,128)(2,1)} %wu.1), custom_call_target="tpu_custom_call" | custom-call | flops 3623878656 | bytes 14680064 | tf_op jit(solution)/shard_map/pallas_call | solution.py:255
  159.3 1.9 copy-done.20
  161.3 5.5 %collective-permute-done.8.sib_ref = bf16[4,192,2048]{2,1,0:T(8,128)(2,1)S(1)} collective-permute-done((bf16[4,192,2048]{2,1,0:T(8,128)(2,1)S(1)}, bf16[4,192,2048]{2,1,0:T(8,128)(2,1)S(1)}, u32[]{:S(2)}, u32[]{:S(2)}) %collective-permute-start.8) | collective-permute-done | bytes 3145760 | tf_op jit(solution)/shard_map/ppermute | solution.py:20
  166.8 2.1 copy-done.21
  168.9 13.4 %shard_map.112 = (bf16[4,2,128,512]{3,2,1,0:T(8,128)(2,1)}, bf16[4,2,128,512]{3,2,1,0:T(8,128)(2,1)}, bf16[2,2,128,512]{3,2,1,0:T(8,128)(2,1)S(1)}, bf16[2,2,128...) custom-call(s32[4]{0:T(128)S(1)} %pad_add_fusion.ids_ref, ...), custom_call_target="tpu_custom_call" | custom-call | flops 4294967296 | bytes 16777216 | tf_op jit(solution)/shard_map/pallas_call | solution.py:160
  189.4 1.9 collective-permute-start.12
  191.3 6.2 %collective-permute-done.9 = bf16[2,2,128,512]{3,2,1,0:T(8,128)(2,1)S(1)} collective-permute-done((bf16[2,2,128,512]{3,2,1,0:T(8,128)(2,1)S(1)}, bf16[2,2,128,512]{3,2,1,0:T(8,128)(2,1)S(1)}, u32[]{:S(2)}, u32[]{:S(2)}) %collective-permute-start.9) | collective-permute-done | bytes 524320 | tf_op jit(solution)/shard_map/ppermute | solution.py:20
  198.1 4.6 %collective-permute-done.11 = bf16[2,2,128,512]{3,2,1,0:T(8,128)(2,1)S(1)} collective-permute-done((bf16[2,2,128,512]{3,2,1,0:T(8,128)(2,1)S(1)}, bf16[2,2,128,512]{3,2,1,0:T(8,128)(2,1)S(1)}, u32[]{:S(2)}, u32[]{:S(2)}) %collective-permute-start.11) | collective-permute-done | bytes 524320 | tf_op jit(solution)/shard_map/ppermute | solution.py:20
  203.6 3.0 collective-permute-start.14
  207.6 2.2 collective-permute-start.16
  209.8 10.9 %shard_map.113 = (bf16[4,192,2048]{2,1,0:T(8,128)(2,1)}, bf16[4,192,2048]{2,1,0:T(8,128)(2,1)}, bf16[4,192,2048]{2,1,0:T(8,128)(2,1)}) custom-call(s32[4]{0:T(128)S(1)} %pad_add_fusion.ids_ref, bf16[4,2,192,512]{3,2,1,0:T(8,128)(2,1)} %copy-done.10, bf16[4,2,192,512]{3,2,1,0:T(8,128)(2,1)} %collective-permute-done.3.refs_1_, ...), custom_call_target="tpu_custom_call" | custom-call | flops 5435817984 | bytes 25165824 | tf_op jit(solution)/shard_map/pallas_call | solution.py:255
  220.7 7.6 %collective-permute-done.13 = bf16[4,2,128,512]{3,2,1,0:T(8,128)(2,1)S(1)} collective-permute-done((bf16[4,2,128,512]{3,2,1,0:T(8,128)(2,1)S(1)}, bf16[4,2,128,512]{3,2,1,0:T(8,128)(2,1)S(1)}, u32[]{:S(2)}, u32[]{:S(2)}) %collective-permute-start.13) | collective-permute-done | bytes 1048608 | tf_op jit(solution)/shard_map/ppermute | solution.py:20
  231.5 2.4 reshape.70
  235.4 3.7 %reshape.71 = bf16[1536,512]{1,0:T(8,128)(2,1)} reshape(bf16[4,2,4,4,12,512]{5,4,3,2,1,0:T(8,128)(2,1)} %copy.32) | data formatting | bytes 3145728 | tf_op jit(solution)/shard_map/reshape | solution.py:367
  239.1 5.3 %all-to-all-start.1 = ((bf16[32,48,512]{2,1,0:T(8,128)(2,1)}), bf16[32,48,512]{2,1,0:T(8,128)(2,1)S(1)}, u32[]{:S(2)}, u32[]{:S(2)}) async-start(bf16[32,48,512]{2,1,0:T(8,128)(2,1)} %bitcast.12), calls=%async_computation.2 | async-start | bytes 3145728 | tf_op jit(solution)/shard_map/all_to_all | solution.py:341
  248.9 2.1 collective-permute-start.18
  254.3 16.8 %collective-permute-done.17 = bf16[2,128,512]{2,1,0:T(8,128)(2,1)S(1)} collective-permute-done((bf16[2,128,512]{2,1,0:T(8,128)(2,1)S(1)}, bf16[2,128,512]{2,1,0:T(8,128)(2,1)S(1)}, u32[]{:S(2)}, u32[]{:S(2)}) %collective-permute-start.17) | collective-permute-done | bytes 262176 | tf_op jit(solution)/shard_map/ppermute | solution.py:20
  271.1 3.0 collective-permute-start.21
  274.1 2.8 collective-permute-done.18
  278.1 2.3 collective-permute-done.21
  281.8 3.1 %collective-permute-start.24 = (bf16[128,512]{1,0:T(8,128)(2,1)S(1)}, bf16[128,512]{1,0:T(8,128)(2,1)S(1)}, u32[]{:S(2)}, u32[]{:S(2)}) collective-permute-start(bf16[128,512]{1,0:T(8,128)(2,1)S(1)} %get-tuple-element.97), channel_id=1, source_target_pairs={{2,0},{3,1},{0,2},{1,3},{6,4},{7,5},{4,6},{5,7},{10,8},{11,9},{8,1... | collective-permute-start | bytes 393224 | tf_op jit(solution)/shard_map/ppermute | solution.py:20
  (122 shorter events, 51.5 us)
Async XLA Ops:
  7.2 97.6 %all-gather.3.cloned.1.call-start = ((), (), s32[]{:S(2)}) async-start(), calls=%async_computation.4 | async-start | bytes 9191424 | tf_op jit(solution)/shard_map/all_gather | solution.py:329
  7.2 10.0 %collective-permute-start.1 = (bf16[128,512]{1,0:T(8,128)(2,1)}, bf16[128,512]{1,0:T(8,128)(2,1)S(1)}, u32[]{:S(2)}, u32[]{:S(2)}) collective-permute-start(bf16[128,512]{1,0:T(8,128)(2,1)} %param.10), channel_id=1, source_target_pairs={{2,0},{3,1},{0,2},{1,3},{6,4},{7,5},{4,6},{5,7},{10,8},{11,9},{8,1... | collective-permute-start | bytes 393224 | tf_op jit(solution)/shard_map/ppermute | solution.py:20
  10.4 6.8 %collective-permute-start = (bf16[128,512]{1,0:T(8,128)(2,1)}, bf16[128,512]{1,0:T(8,128)(2,1)S(1)}, u32[]{:S(2)}, u32[]{:S(2)}) collective-permute-start(bf16[128,512]{1,0:T(8,128)(2,1)} %param.10), channel_id=1, source_target_pairs={{1,0},{2,1},{3,2},{0,3},{5,4},{6,5},{7,6},{4,7},{9,8},{10,9},{11,1... | collective-permute-start | bytes 393224 | tf_op jit(solution)/shard_map/ppermute | solution.py:20
  11.6 6.4 %collective-permute-start.2 = (bf16[128,512]{1,0:T(8,128)(2,1)}, bf16[128,512]{1,0:T(8,128)(2,1)S(1)}, u32[]{:S(2)}, u32[]{:S(2)}) collective-permute-start(bf16[128,512]{1,0:T(8,128)(2,1)} %param.10), channel_id=1, source_target_pairs={{3,0},{0,1},{1,2},{2,3},{7,4},{4,5},{5,6},{6,7},{11,8},{8,9},{9,10... | collective-permute-start | bytes 393224 | tf_op jit(solution)/shard_map/ppermute | solution.py:20
  19.5 212.0 %reduce-scatter.2.cloned.1.call-start = ((), (), s32[]{:S(2)}) async-start(), calls=%async_computation.3 | async-start | bytes 7864320 | tf_op jit(solution)/shard_map/reduce_scatter | solution.py:358
  64.4 58.3 %copy-start.10 = (bf16[4,2,192,512]{3,2,1,0:T(8,128)(2,1)}, bf16[4,2,192,512]{3,2,1,0:T(8,128)(2,1)S(1)}, u32[]{:S(2)}) copy-start(bf16[4,2,192,512]{3,2,1,0:T(8,128)(2,1)S(1)} %copy.31.refs_0_) | copy-start | bytes 4718596
  64.4 37.1 %collective-permute-start.4 = (bf16[4,2,192,512]{3,2,1,0:T(8,128)(2,1)S(1)}, bf16[4,2,192,512]{3,2,1,0:T(8,128)(2,1)S(1)}, u32[]{:S(2)}, u32[]{:S(2)}) collective-permute-start(bf16[4,2,192,512]{3,2,1,0:T(8,128)(2,1)S(1)} %copy.31.refs_0_), channel_id=1, source_target_pairs={{3,0},{0,1},{1,2},{2,3},{7,4},{4,5},{5,6},{6,7},{11,8},{8,9},{9,10... | collective-permute-start | bytes 4718600 | tf_op jit(solution)/shard_map/ppermute | solution.py:20
  65.2 36.3 %collective-permute-start.3 = (bf16[4,2,192,512]{3,2,1,0:T(8,128)(2,1)S(1)}, bf16[4,2,192,512]{3,2,1,0:T(8,128)(2,1)}, u32[]{:S(2)}, u32[]{:S(2)}) collective-permute-start(bf16[4,2,192,512]{3,2,1,0:T(8,128)(2,1)S(1)} %copy.31.refs_0_), channel_id=1, source_target_pairs={{1,0},{2,1},{3,2},{0,3},{5,4},{6,5},{7,6},{4,7},{9,8},{10,9},{11,1... | collective-permute-start | bytes 4718600 | tf_op jit(solution)/shard_map/ppermute | solution.py:20
  107.9 20.7 %collective-permute-start.5 = (bf16[2,2,192,512]{3,2,1,0:T(8,128)(2,1)}, bf16[2,2,192,512]{3,2,1,0:T(8,128)(2,1)S(1)}, u32[]{:S(2)}, u32[]{:S(2)}) collective-permute-start(bf16[2,2,192,512]{3,2,1,0:T(8,128)(2,1)} %slice.66), channel_id=1, source_target_pairs={{3,0},{0,1},{1,2},{2,3},{7,4},{4,5},{5,6},{6,7},{11,8},{8,9},{9,10... | collective-permute-start | bytes 2359304 | tf_op jit(solution)/shard_map/ppermute | solution.py:20
  109.3 19.2 %collective-permute-start.6 = (bf16[2,2,192,512]{3,2,1,0:T(8,128)(2,1)}, bf16[2,2,192,512]{3,2,1,0:T(8,128)(2,1)S(1)}, u32[]{:S(2)}, u32[]{:S(2)}) collective-permute-start(bf16[2,2,192,512]{3,2,1,0:T(8,128)(2,1)} %slice.67), channel_id=1, source_target_pairs={{1,0},{2,1},{3,2},{0,3},{5,4},{6,5},{7,6},{4,7},{9,8},{10,9},{11,1... | collective-permute-start | bytes 2359304 | tf_op jit(solution)/shard_map/ppermute | solution.py:20
  128.6 5.9 %collective-permute-start.7 = (bf16[4,192,2048]{2,1,0:T(8,128)(2,1)}, bf16[4,192,2048]{2,1,0:T(8,128)(2,1)S(1)}, u32[]{:S(2)}, u32[]{:S(2)}) collective-permute-start(bf16[4,192,2048]{2,1,0:T(8,128)(2,1)} %get-tuple-element.55), channel_id=1, source_target_pairs={{16,0},{0,16},{17,1},{1,17},{18,2},{2,18},{19,3},{3,19},{20,4},{4,... | collective-permute-start | bytes 9437192 | tf_op jit(solution)/shard_map/ppermute | solution.py:20
  161.2 5.7 %collective-permute-start.8 = (bf16[4,192,2048]{2,1,0:T(8,128)(2,1)S(1)}, bf16[4,192,2048]{2,1,0:T(8,128)(2,1)S(1)}, u32[]{:S(2)}, u32[]{:S(2)}) collective-permute-start(bf16[4,192,2048]{2,1,0:T(8,128)(2,1)S(1)} %copy-done.20), channel_id=1, source_target_pairs={{16,0},{0,16},{17,1},{1,17},{18,2},{2,18},{19,3},{3,19},{20,4},{4,... | collective-permute-start | bytes 9437192 | tf_op jit(solution)/shard_map/ppermute | solution.py:20
  182.3 15.2 %collective-permute-start.9 = (bf16[2,2,128,512]{3,2,1,0:T(8,128)(2,1)S(1)}, bf16[2,2,128,512]{3,2,1,0:T(8,128)(2,1)S(1)}, u32[]{:S(2)}, u32[]{:S(2)}) collective-permute-start(bf16[2,2,128,512]{3,2,1,0:T(8,128)(2,1)S(1)} %get-tuple-element.62), channel_id=1, source_target_pairs={{96,0},{0,32},{32,64},{64,96},{97,1},{1,33},{33,65},{65,97},{98,2}... | collective-permute-start | bytes 1572872 | tf_op jit(solution)/shard_map/ppermute | solution.py:20
  183.8 14.0 %collective-permute-start.10 = (bf16[2,2,128,512]{3,2,1,0:T(8,128)(2,1)S(1)}, bf16[2,2,128,512]{3,2,1,0:T(8,128)(2,1)S(1)}, u32[]{:S(2)}, u32[]{:S(2)}) collective-permute-start(bf16[2,2,128,512]{3,2,1,0:T(8,128)(2,1)S(1)} %get-tuple-element.64), channel_id=1, source_target_pairs={{32,0},{64,32},{96,64},{0,96},{33,1},{65,33},{97,65},{1,97},{34,2}... | collective-permute-start | bytes 1572872 | tf_op jit(solution)/shard_map/ppermute | solution.py:20
  188.0 14.7 %collective-permute-start.11 = (bf16[2,2,128,512]{3,2,1,0:T(8,128)(2,1)S(1)}, bf16[2,2,128,512]{3,2,1,0:T(8,128)(2,1)S(1)}, u32[]{:S(2)}, u32[]{:S(2)}) collective-permute-start(bf16[2,2,128,512]{3,2,1,0:T(8,128)(2,1)S(1)} %get-tuple-element.67), channel_id=1, source_target_pairs={{12,0},{0,4},{4,8},{8,12},{13,1},{1,5},{5,9},{9,13},{14,2},{2,6},{... | collective-permute-start | bytes 1572872 | tf_op jit(solution)/shard_map/ppermute | solution.py:20
  189.4 13.6 %collective-permute-start.12 = (bf16[2,2,128,512]{3,2,1,0:T(8,128)(2,1)S(1)}, bf16[2,2,128,512]{3,2,1,0:T(8,128)(2,1)S(1)}, u32[]{:S(2)}, u32[]{:S(2)}) collective-permute-start(bf16[2,2,128,512]{3,2,1,0:T(8,128)(2,1)S(1)} %copy-done.22), channel_id=1, source_target_pairs={{4,0},{8,4},{12,8},{0,12},{5,1},{9,5},{13,9},{1,13},{6,2},{10,6},{... | collective-permute-start | bytes 1572872 | tf_op jit(solution)/shard_map/ppermute | solution.py:20
  203.2 25.1 %copy-start.16 = (bf16[4,2,128,512]{3,2,1,0:T(8,128)(2,1)S(1)}, bf16[4,2,128,512]{3,2,1,0:T(8,128)(2,1)}, u32[]{:S(2)}) copy-start(bf16[4,2,128,512]{3,2,1,0:T(8,128)(2,1)} %get-tuple-element.76) | copy-start | bytes 3145732
  203.2 25.1 %collective-permute-start.13 = (bf16[4,2,128,512]{3,2,1,0:T(8,128)(2,1)S(1)}, bf16[4,2,128,512]{3,2,1,0:T(8,128)(2,1)S(1)}, u32[]{:S(2)}, u32[]{:S(2)}) collective-permute-start(bf16[4,2,128,512]{3,2,1,0:T(8,128)(2,1)S(1)} %pad_maximum_fusion), channel_id=1, source_target_pairs={{96,0},{0,32},{32,64},{64,96},{97,1},{1,33},{33,65},{65,97},{98,2}... | collective-permute-start | bytes 3145736 | tf_op jit(solution)/shard_map/ppermute | solution.py:20
  203.6 24.8 %collective-permute-start.14 = (bf16[4,2,128,512]{3,2,1,0:T(8,128)(2,1)S(1)}, bf16[4,2,128,512]{3,2,1,0:T(8,128)(2,1)S(1)}, u32[]{:S(2)}, u32[]{:S(2)}) collective-permute-start(bf16[4,2,128,512]{3,2,1,0:T(8,128)(2,1)S(1)} %pad_maximum_fusion.1), channel_id=1, source_target_pairs={{32,0},{64,32},{96,64},{0,96},{33,1},{65,33},{97,65},{1,97},{34,2}... | collective-permute-start | bytes 3145736 | tf_op jit(solution)/shard_map/ppermute | solution.py:20
  206.5 24.5 %collective-permute-start.15 = (bf16[4,2,128,512]{3,2,1,0:T(8,128)(2,1)S(1)}, bf16[4,2,128,512]{3,2,1,0:T(8,128)(2,1)S(1)}, u32[]{:S(2)}, u32[]{:S(2)}) collective-permute-start(bf16[4,2,128,512]{3,2,1,0:T(8,128)(2,1)S(1)} %pad_maximum_fusion.2), channel_id=1, source_target_pairs={{12,0},{0,4},{4,8},{8,12},{13,1},{1,5},{5,9},{9,13},{14,2},{2,6},{... | collective-permute-start | bytes 3145736 | tf_op jit(solution)/shard_map/ppermute | solution.py:20
  207.6 23.4 %collective-permute-start.16 = (bf16[4,2,128,512]{3,2,1,0:T(8,128)(2,1)S(1)}, bf16[4,2,128,512]{3,2,1,0:T(8,128)(2,1)S(1)}, u32[]{:S(2)}, u32[]{:S(2)}) collective-permute-start(bf16[4,2,128,512]{3,2,1,0:T(8,128)(2,1)S(1)} %pad_maximum_fusion.3), channel_id=1, source_target_pairs={{4,0},{8,4},{12,8},{0,12},{5,1},{9,5},{13,9},{1,13},{6,2},{10,6},{... | collective-permute-start | bytes 3145736 | tf_op jit(solution)/shard_map/ppermute | solution.py:20
  239.1 41.4 %all-to-all-start.1 = ((bf16[32,48,512]{2,1,0:T(8,128)(2,1)}), bf16[32,48,512]{2,1,0:T(8,128)(2,1)S(1)}, u32[]{:S(2)}, u32[]{:S(2)}) async-start(bf16[32,48,512]{2,1,0:T(8,128)(2,1)} %bitcast.12), calls=%async_computation.2 | async-start | bytes 3145728 | tf_op jit(solution)/shard_map/all_to_all | solution.py:341
  245.6 25.5 %collective-permute-start.17 = (bf16[2,128,512]{2,1,0:T(8,128)(2,1)S(1)}, bf16[2,128,512]{2,1,0:T(8,128)(2,1)S(1)}, u32[]{:S(2)}, u32[]{:S(2)}) collective-permute-start(bf16[2,128,512]{2,1,0:T(8,128)(2,1)S(1)} %get-tuple-element.94), channel_id=1, source_target_pairs={{12,0},{0,4},{4,8},{8,12},{13,1},{1,5},{5,9},{9,13},{14,2},{2,6},{... | collective-permute-start | bytes 786440 | tf_op jit(solution)/shard_map/ppermute | solution.py:20
  247.4 26.6 %collective-permute-start.19 = (bf16[2,128,512]{2,1,0:T(8,128)(2,1)S(1)}, bf16[2,128,512]{2,1,0:T(8,128)(2,1)S(1)}, u32[]{:S(2)}, u32[]{:S(2)}) collective-permute-start(bf16[2,128,512]{2,1,0:T(8,128)(2,1)S(1)} %get-tuple-element.95), channel_id=1, source_target_pairs={{4,0},{8,4},{12,8},{0,12},{5,1},{9,5},{13,9},{1,13},{6,2},{10,6},{... | collective-permute-start | bytes 786440 | tf_op jit(solution)/shard_map/ppermute | solution.py:20
  248.9 28.0 %collective-permute-start.18 = (bf16[2,128,512]{2,1,0:T(8,128)(2,1)S(1)}, bf16[2,128,512]{2,1,0:T(8,128)(2,1)S(1)}, u32[]{:S(2)}, u32[]{:S(2)}) collective-permute-start(bf16[2,128,512]{2,1,0:T(8,128)(2,1)S(1)} %get-tuple-element.96), channel_id=1, source_target_pairs={{8,0},{12,4},{0,8},{4,12},{9,1},{13,5},{1,9},{5,13},{10,2},{14,6},... | collective-permute-start | bytes 786440 | tf_op jit(solution)/shard_map/ppermute | solution.py:20
  251.0 27.0 %collective-permute-start.20 = (bf16[2,128,512]{2,1,0:T(8,128)(2,1)S(1)}, bf16[2,128,512]{2,1,0:T(8,128)(2,1)S(1)}, u32[]{:S(2)}, u32[]{:S(2)}) collective-permute-start(bf16[2,128,512]{2,1,0:T(8,128)(2,1)S(1)} %get-tuple-element.91), channel_id=1, source_target_pairs={{96,0},{0,32},{32,64},{64,96},{97,1},{1,33},{33,65},{65,97},{98,2}... | collective-permute-start | bytes 786440 | tf_op jit(solution)/shard_map/ppermute | solution.py:20
  252.6 25.5 %collective-permute-start.22 = (bf16[2,128,512]{2,1,0:T(8,128)(2,1)S(1)}, bf16[2,128,512]{2,1,0:T(8,128)(2,1)S(1)}, u32[]{:S(2)}, u32[]{:S(2)}) collective-permute-start(bf16[2,128,512]{2,1,0:T(8,128)(2,1)S(1)} %get-tuple-element.92), channel_id=1, source_target_pairs={{32,0},{64,32},{96,64},{0,96},{33,1},{65,33},{97,65},{1,97},{34,2}... | collective-permute-start | bytes 786440 | tf_op jit(solution)/shard_map/ppermute | solution.py:20
  271.1 9.2 %collective-permute-start.21 = (bf16[2,128,512]{2,1,0:T(8,128)(2,1)S(1)}, bf16[2,128,512]{2,1,0:T(8,128)(2,1)S(1)}, u32[]{:S(2)}, u32[]{:S(2)}) collective-permute-start(bf16[2,128,512]{2,1,0:T(8,128)(2,1)S(1)} %get-tuple-element.93), channel_id=1, source_target_pairs={{64,0},{96,32},{0,64},{32,96},{65,1},{97,33},{1,65},{33,97},{66,2}... | collective-permute-start | bytes 786440 | tf_op jit(solution)/shard_map/ppermute | solution.py:20
  276.9 13.7 %copy-start.1 = (bf16[128,512]{1,0:T(8,128)(2,1)S(1)}, bf16[128,512]{1,0:T(8,128)(2,1)}, u32[]{:S(2)}) copy-start(bf16[128,512]{1,0:T(8,128)(2,1)} %param.7) | copy-start | bytes 393220
  280.5 7.7 %collective-permute-start.23 = (bf16[128,512]{1,0:T(8,128)(2,1)S(1)}, bf16[128,512]{1,0:T(8,128)(2,1)S(1)}, u32[]{:S(2)}, u32[]{:S(2)}) collective-permute-start(bf16[128,512]{1,0:T(8,128)(2,1)S(1)} %slice_bitcast_fusion.8), channel_id=1, source_target_pairs={{3,0},{0,1},{1,2},{2,3},{7,4},{4,5},{5,6},{6,7},{11,8},{8,9},{9,10... | collective-permute-start | bytes 393224 | tf_op jit(solution)/shard_map/ppermute | solution.py:20
  281.8 7.9 %collective-permute-start.24 = (bf16[128,512]{1,0:T(8,128)(2,1)S(1)}, bf16[128,512]{1,0:T(8,128)(2,1)S(1)}, u32[]{:S(2)}, u32[]{:S(2)}) collective-permute-start(bf16[128,512]{1,0:T(8,128)(2,1)S(1)} %get-tuple-element.97), channel_id=1, source_target_pairs={{2,0},{3,1},{0,2},{1,3},{6,4},{7,5},{4,6},{5,7},{10,8},{11,9},{8,1... | collective-permute-start | bytes 393224 | tf_op jit(solution)/shard_map/ppermute | solution.py:20
  284.9 5.0 %collective-permute-start.25 = (bf16[128,512]{1,0:T(8,128)(2,1)S(1)}, bf16[128,512]{1,0:T(8,128)(2,1)S(1)}, u32[]{:S(2)}, u32[]{:S(2)}) collective-permute-start(bf16[128,512]{1,0:T(8,128)(2,1)S(1)} %get-tuple-element.98), channel_id=1, source_target_pairs={{1,0},{2,1},{3,2},{0,3},{5,4},{6,5},{7,6},{4,7},{9,8},{10,9},{11,1... | collective-permute-start | bytes 393224 | tf_op jit(solution)/shard_map/ppermute | solution.py:20
  (20 other events, 110.5 us)
Sparse Core Ops, SparseCore 0:
  19.6 85.1 all-gather.2
  159.4 63.3 reduce-scatter.1
where the time goes:
time: 299 us; the launch traced here: 297 us
  waiting for transfers between devices  102 us (34%)
  Pallas kernels  56.6 us (19%)
  starting transfers between devices  47.2 us (16%)
  blocking collectives  39.8 us (13%)
  local copies, waits for them, and re-layouts  28.2 us (9%)
  between operations  14.4 us (5%)
  other arithmetic  7.05 us (2%)
    ppermute x26, waiting for transfers between devices, fetch(): return lax.ppermute(a, axis, [((i + r) % n, i) for i in range(n)])  98.5 us
    ppermute x26, starting transfers between devices, fetch(): return lax.ppermute(a, axis, [((i + r) % n, i) for i in range(n)])  41.8 us
    all_to_all x1, blocking collectives, exchange(): return lax.all_to_all(a, GROUP, split_axis=0, concat_axis=0, tiled=True)  39.8 us
    pallas_call x3, Pallas kernels, per_expert(): pl.pallas_call(kernel, grid=(n_exp,), out_shape=outs, in_specs=[pl.BlockS...  31.7 us
    pallas_call x1, Pallas kernels, sum_tokens(): pl.pallas_call(sum_kernel, grid_spec=pltpu.PrefetchScalarGridSpec(num_sca...  13.4 us
    pallas_call x1, Pallas kernels, pick(): pl.pallas_call(pick_kernel, grid=(4,), out_shape=(rows, rows, maps), in_s...  11.5 us
    unnamed x50, local copies, waits for them, and re-layouts  10.8 us
  transfers between devices with their start and end apart: 29, of which 17 were waited for; matrix products, arithmetic and copies ran while one was open for 5% of the time, Pallas kernels for 12%

commit v1 on v0

--- a/solution.py
+++ b/solution.py
@@ -121,32 +121,30 @@
     z = ids_ref[1]
     n_exp = own_ref.shape[0]
     tok, width = 128, own_ref.shape[2] // 4
-    rows = jnp.concatenate(
-        [ref[e] for ref in (own_ref, sib_ref) for e in range(n_exp)], axis=0
-    )
-    for zr in range(4):
-        there = pl.multiple_of(lax.rem(z + zr, 4) * tok, tok)
-        total = tn(map_ref[0, :, pl.ds(there, tok)], rows).astype(BF)
-        cut = [total[:, r * width : (r + 1) * width] for r in range(4)]
-        y_dest = (by_y[0], by_y[1], by_y[2 + zr // 2], by_y[4])
-        for i in range(4):
-
-            @pl.when(yr == i)
-            def _(i=i):
-                at = zr % 2 if i == 2 else zr
-                y_dest[i][at, 0], y_dest[i][at, 1] = cut[0], cut[1]
-
-        if zr == 2:
-            for part in range(2):
-
-                @pl.when(yr // 2 == part)
-                def _(part=part):
-                    at = yr - 2 * part
-                    by_z[2 + part][at, 0], by_z[2 + part][at, 1] = cut[2], cut[3]
-
-        else:
-            ref = by_z[(0, 1, None, 4)[zr]]
-            ref[yr, 0], ref[yr, 1] = cut[2], cut[3]
+    there = [pl.multiple_of(lax.rem(z + zr, 4) * tok, tok) for zr in range(4)]
+    gates = jnp.concatenate([map_ref[0, :, pl.ds(t, tok)] for t in there], axis=1)
+    for r in range(4):
+        cols = slice(r * width, (r + 1) * width)
+        rows = [ref[e, :, cols] for ref in (own_ref, sib_ref) for e in range(n_exp)]
+        total = tn(gates, jnp.concatenate(rows, axis=0)).astype(BF)
+        for zr in range(4):
+            block = total[zr * tok : (zr + 1) * tok]
+            if r >= 2:
+                if zr != 2:
+                    by_z[(0, 1, None, 4)[zr]][0, r - 2] = block
+                for part in range(2 if zr == 2 else 0):
+
+                    @pl.when(yr // 2 == part)
+                    def _(part=part, block=block):
+                        by_z[2 + part][0, r - 2] = block
+
+                continue
+            dest = (by_y[0], by_y[1], by_y[2 + zr // 2], by_y[4])
+            for i in range(4):
+
+                @pl.when(yr == i)
+                def _(i=i, block=block):
+                    dest[i][zr % 2 if i == 2 else zr, r] = block
 
 
 def sum_tokens(ids, maps, own, sib):
@@ -157,6 +155,10 @@
     at = lambda i, ids: lax.rem(ids[0] + i, 4)
     rows_spec = pl.BlockSpec((n_exp, rows // 4, cols), lambda i, ids: (0, at(i, ids), 0))
     keep = lambda a: pl.BlockSpec(a.shape, lambda i, ids: (0,) * 4)
+    block = (1,) + whole.shape[1:]
+    each_y = pl.BlockSpec(block, lambda i, ids: (i, 0, 0, 0))
+    first = pl.BlockSpec(block, lambda i, ids: (jnp.minimum(i, 1), 0, 0, 0))
+    last = pl.BlockSpec(block, lambda i, ids: (jnp.maximum(i - 2, 0), 0, 0, 0))
     return pl.pallas_call(
         sum_kernel,
         grid_spec=pltpu.PrefetchScalarGridSpec(
@@ -167,7 +169,7 @@
                 rows_spec,
                 rows_spec,
             ],
-            out_specs=tuple(keep(a) for a in outs),
+            out_specs=tuple(keep(a) for a in outs[:5]) + (each_y, each_y, first, last, each_y),
         ),
         out_shape=outs,
         compiler_params=pltpu.CompilerParams(vmem_limit_bytes=VMEM_LIMIT),
@@ -188,36 +190,39 @@
 
 def forward_kernel(ids_ref, *refs):
     x_refs, refs = refs[:5], refs[5:]
-    own, sib, wg, wu, wd, oo, os, hid_ref, da_ref, db_ref = refs
-    half, cols = own.shape[1:]
+    wg, wu, wd, oo, os, hid_ref, slope_ref, act_ref = refs
+    half, cols = oo.shape[1:]
     n, width = 4, cols // 4
-    fixed = [slice(r * width, (r + 1) * width) for r in range(n)]
     moved = moved_columns(ids_ref[3], n, width)
     x_rows = x_rows_of(ids_ref[2], x_refs)
-    g_rows = [jnp.concatenate([own[0, :, f], sib[0, :, f]], axis=0) for f in fixed]
     a = sum(nt(x_rows[r], wg[0, :, moved[r]]) for r in range(n))
     b = sum(nt(x_rows[r], wu[0, :, moved[r]]) for r in range(n))
-    gh = sum(nt(g_rows[r], wd[0, :, moved[r]]) for r in range(n))
     s = jax.nn.sigmoid(a)
     act = a * s
     hidden = (act * b).astype(BF)
     hid_ref[0] = hidden
-    da_ref[0] = (gh * b * s * (1.0 + a * (1.0 - s))).astype(BF)
-    db_ref[0] = (gh * act).astype(BF)
+    slope_ref[0] = b * s * (1.0 + a * (1.0 - s))
+    act_ref[0] = act
     for r in range(n):
         out = nn(hidden, wd[0, :, moved[r]]).astype(BF)
-        oo[0, :, fixed[r]] = out[:half]
-        os[0, :, fixed[r]] = out[half:]
-
-
-def back_kernel(ids_ref, da_ref, db_ref, wg, wu, back_ref):
+        oo[0, :, r * width : (r + 1) * width] = out[:half]
+        os[0, :, r * width : (r + 1) * width] = out[half:]
+
+
+def back_kernel(ids_ref, own, sib, slope_ref, act_ref, wg, wu, wd, da_ref, db_ref, back_ref):
     c = ids_ref[2]
     n = back_ref.shape[0]
     half, width = back_ref.shape[3:]
-    da, db = da_ref[0], db_ref[0]
+    moved = moved_columns(ids_ref[3], n, width)
+    fixed = [slice(r * width, (r + 1) * width) for r in range(n)]
+    g_rows = [jnp.concatenate([own[0, :, f], sib[0, :, f]], axis=0) for f in fixed]
+    gh = sum(nt(g_rows[r], wd[0, :, moved[r]]) for r in range(n))
+    da = (gh * slope_ref[0]).astype(BF)
+    db = (gh * act_ref[0]).astype(BF)
+    da_ref[0] = da
+    db_ref[0] = db
     for r in range(n):
-        cols = slice(r * width, (r + 1) * width)
-        back = (nn(da, wg[0, :, cols]) + nn(db, wu[0, :, cols])).astype(BF)
+        back = (nn(da, wg[0, :, fixed[r]]) + nn(db, wu[0, :, fixed[r]])).astype(BF)
         back_ref[r, 0, c] = back[:half]
         back_ref[r, 0, 1 - c] = back[half:]
 
@@ -265,21 +270,23 @@
     )(ids, *args)
 
 
-def forward(ids, x, g, weights):
-    n_exp, rows, _ = g[0].shape
+def forward(ids, x, weights):
+    n_exp, _, rows, width = x[0].shape
     mid = jax.ShapeDtypeStruct((n_exp, 2 * rows, weights[0].shape[1]), BF)
-    out = jax.ShapeDtypeStruct(g[0].shape, BF)
-    outs = (out, out, mid, mid, mid)
-    args = tuple(x) + tuple(g) + tuple(weights)
-    specs = each_x(x) + [each(a) for a in tuple(g) + tuple(weights)]
-    return per_expert(forward_kernel, ids, specs, args, outs, tuple(each(a) for a in outs), 4, 30)
-
-
-def backward(ids, mids, weights, shape):
-    back = jax.ShapeDtypeStruct((4,) + shape, BF)
-    args = tuple(mids) + tuple(weights)
+    wide = jax.ShapeDtypeStruct(mid.shape, F32)
+    out = jax.ShapeDtypeStruct((n_exp, rows, 4 * width), BF)
+    outs = (out, out, mid, wide, wide)
+    args = tuple(x) + tuple(weights)
+    specs = each_x(x) + [each(a) for a in weights]
+    return per_expert(forward_kernel, ids, specs, args, outs, tuple(each(a) for a in outs), 3, 26)
+
+
+def backward(ids, g, slope, act, weights, mid, shape):
+    outs = (mid, mid, jax.ShapeDtypeStruct((4,) + shape, BF))
+    args = tuple(g) + (slope, act) + tuple(weights)
     spec = pl.BlockSpec((4, 1) + shape[1:], lambda i: (0, i, 0, 0, 0))
-    return per_expert(back_kernel, ids, [each(a) for a in args], args, back, spec, 2, 14)
+    out_specs = (each(mid), each(mid), spec)
+    return per_expert(back_kernel, ids, [each(a) for a in args], args, outs, out_specs, 3, 26)
 
 
 def weight_grads(ids, x, g, mids, like):
@@ -324,10 +331,6 @@
 
     cot = [cotangent] + [fetch(cotangent, "x", r) for r in (1, 2, 3)]
     routes_t = routes.T
-    meta = jnp.concatenate([routes_t.astype(BF), gates.T], axis=0)
-    meta = jnp.pad(meta, ((0, 0), (0, width - tok)))
-    whole = lax.all_gather(jnp.concatenate(cot + [meta]), ("y", "z"))
-
     experts_all = jnp.arange(total_exp, dtype=jnp.int32)
     named = jnp.sum((routes_t[:, None, :] == experts_all[None, :, None]).astype(F32), axis=0)
     place = ranks(named).astype(BF)
@@ -341,35 +344,40 @@
         return lax.all_to_all(a, GROUP, split_axis=0, concat_axis=0, tiled=True)
 
     came = exchange(jnp.dot(own_map, tokens, preferred_element_type=F32).astype(BF))
+
+    meta = jnp.concatenate([routes_t.astype(BF), gates.T], axis=0)
+    meta = jnp.pad(meta, ((0, 0), (0, width - tok)))
+    whole = jnp.concatenate(cot + [meta])
+    came, whole = lax.optimization_barrier((came, whole))
+    whole = lax.all_gather(whole, ("y", "z"))
+
     came = came.reshape(4, 2, 4, n_exp, CAP, width).transpose(3, 1, 0, 2, 4, 5)
     came = came.reshape(n_exp, 2, 16 * CAP, width)
     up, down = fetch(came, "x", 1), fetch(came, "x", -1)
-    whole, up, down = lax.optimization_barrier((whole, up, down))
     pair = n_exp // 2
     x_blocks = (came, up, fetch(down[:pair], "x", -1), fetch(up[pair:], "x", 1), down)
-
+    out_own, out_sib, hidden, slope, act = forward(ids, x_blocks, weights)
+
+    whole, out_sib = lax.optimization_barrier((whole, out_sib))
     own, sib, maps = pick(ids, whole, n_exp)
-    sib, far_lo, far_hi = lax.optimization_barrier((sib, x_blocks[2], x_blocks[3]))
-    x_blocks = (came, up, far_lo, far_hi, down)
-    g_blocks = (own, fetch(sib, "c", 1))
-    out_own, out_sib, hidden, grad_a, grad_b = forward(ids, x_blocks, g_blocks, weights)
-    out_sib = fetch(out_sib, "c", 1)
-    back = backward(ids, (grad_a, grad_b), weights[:2], came.shape)
+    sib, out_sib = lax.optimization_barrier((sib, fetch(out_sib, "c", 1)))
+
+    sums = sum_tokens(ids, maps, out_own, out_sib)
+    sib, sums = lax.optimization_barrier((fetch(sib, "c", 1), sums))
+    ends_y, ends_z = collect_far(sums[:5], "y"), collect_far(sums[5:], "z")
+    g_blocks = (own, sib)
+    mid = jax.ShapeDtypeStruct(hidden.shape, BF)
+    grad_a, grad_b, back = backward(ids, g_blocks, slope, act, weights, mid, came.shape)
     back = lax.psum_scatter(back.reshape(-1, width), "x", scatter_dimension=0, tiled=True)
-
-    sums = sum_tokens(ids, maps, out_own, out_sib)
-    ends_y, ends_z = collect_far(sums[:5], "y"), collect_far(sums[5:], "z")
-    hidden, ends_y, ends_z = lax.optimization_barrier((hidden, ends_y, ends_z))
+    grad_a, ends_y, ends_z = lax.optimization_barrier((grad_a, ends_y, ends_z))
     grads = weight_grads(ids, x_blocks, g_blocks, (hidden, grad_a, grad_b), w_gate)
     part1, part2 = collect_near(ends_y, "y"), collect_near(ends_z, "z")
+    grads, part1, part2 = lax.optimization_barrier((grads, part1, part2))
+    part1, part2 = collect_small(part1, "z"), collect_small(part2, "y")
+    mixed = collect_small((part1[0], part1[1], part2[0], part2[1]), "x")
 
     back = back.reshape(n_exp, 2, 4, 4, CAP, width).transpose(2, 1, 3, 0, 4, 5)
-    back = back.reshape(slots, width)
-    grads, back, part1, part2 = lax.optimization_barrier((grads, back, part1, part2))
-    back = exchange(back)
-    part1, part2 = collect_small(part1, "z"), collect_small(part2, "y")
-    back, part1, part2 = lax.optimization_barrier((back, part1, part2))
-    mixed = collect_small((part1[0], part1[1], part2[0], part2[1]), "x")
+    back = exchange(back.reshape(slots, width))
     grad_tokens = tn(own_map, back).astype(BF)
     return (mixed, grad_tokens) + tuple(grads)
 

time: 299 us -> 292 us (0.977)
  blocking collectives: 39.8 us -> 0 us
  waiting for transfers between devices: 102 us -> 127 us
  starting transfers between devices: 47.2 us -> 52.3 us
  Pallas kernels: 56.6 us -> 59.6 us
    all_to_all x1 -> x0, blocking collectives: 39.8 us -> none  [exchange(): return lax.all_to_all(a, GROUP, split_axis=0, concat_axis=0, tiled=True)]
    all_to_all x1 -> x2, starting transfers between devices: 5.28 us -> 16 us  [exchange(): return lax.all_to_all(a, GROUP, split_axis=0, concat_axis=0, tiled=True)]
    all_to_all x1 -> x2, waiting for transfers between devices: 0.01 us -> 10.1 us  [exchange(): return lax.all_to_all(a, GROUP, split_axis=0, concat_axis=0, tiled=True)]
    reduce_scatter x1, waiting for transfers between devices: 0.02 us -> 9.47 us  [body(): lax.psum_scatter(back.reshape(-1, width), 'x', scatter_dimension=0, tiled...]
    ppermute x26, waiting for transfers between devices: 98.5 us -> 108 us  [fetch(): return lax.ppermute(a, axis, [((i + r) % n, i) for i in range(n)])]
    ppermute x26, starting transfers between devices: 41.8 us -> 36.3 us  [fetch(): return lax.ppermute(a, axis, [((i + r) % n, i) for i in range(n)])]
    all_to_all x1 -> x2, local copies, waits for them, and re-layouts: 0.87 us -> 5.23 us  [exchange(): return lax.all_to_all(a, GROUP, split_axis=0, concat_axis=0, tiled=True)]
    pallas_call x3, Pallas kernels: 31.7 us -> 35.8 us  [per_expert(): pl.pallas_call(kernel, grid=(n_exp,), out_shape=outs, in_specs=[pl.BlockS...]
  transfers between devices with their start and end apart: 29 -> 30, of which waited for: 17 -> 17; matrix products, arithmetic and copies ran while one was open for 5% -> 7% of each run, Pallas kernels for 12% -> 16%
where the time goes in v1:
time: 292 us; the launch traced here: 291 us
  waiting for transfers between devices  127 us (43%)
  Pallas kernels  59.6 us (20%)
  starting transfers between devices  52.3 us (18%)
  local copies, waits for them, and re-layouts  27 us (9%)
  between operations  14.4 us (5%)
  other arithmetic  5.88 us (2%)
  matrix products  4.23 us (1%)
    ppermute x26, waiting for transfers between devices, fetch(): return lax.ppermute(a, axis, [((i + r) % n, i) for i in range(n)])  108 us
    ppermute x26, starting transfers between devices, fetch(): return lax.ppermute(a, axis, [((i + r) % n, i) for i in range(n)])  36.3 us
    pallas_call x3, Pallas kernels, per_expert(): pl.pallas_call(kernel, grid=(n_exp,), out_shape=outs, in_specs=[pl.BlockS...  35.8 us
    all_to_all x2, starting transfers between devices, exchange(): return lax.all_to_all(a, GROUP, split_axis=0, concat_axis=0, tiled=True)  16 us
    pallas_call x1, Pallas kernels, sum_tokens(): pl.pallas_call(sum_kernel, grid_spec=pltpu.PrefetchScalarGridSpec(num_sca...  12.3 us
    pallas_call x1, Pallas kernels, pick(): pl.pallas_call(pick_kernel, grid=(4,), out_shape=(rows, rows, maps), in_s...  11.5 us
    unnamed x60, local copies, waits for them, and re-layouts  11.1 us
    all_to_all x2, waiting for transfers between devices, exchange(): return lax.all_to_all(a, GROUP, split_axis=0, concat_axis=0, tiled=True)  10.1 us
  transfers between devices with their start and end apart: 30, of which 17 were waited for; matrix products, arithmetic and copies ran while one was open for 7% of the time, Pallas kernels for 16%

profile of v1, /device:TPU:0, one launch (start us, length us, event | category | flops | bytes accessed | tf_op | source)
XLA Modules:
  0.0 290.8 jit_solution(6261293296117039548)
XLA Ops:
  10.2 8.5 %all-to-all-start = ((bf16[32,48,512]{2,1,0:T(8,128)(2,1)}), bf16[32,48,512]{2,1,0:T(8,128)(2,1)S(1)}, u32[]{:S(2)}, u32[]{:S(2)}) async-start(bf16[32,48,512]{2,1,0:T(8,128)(2,1)} %bitcast.54), calls=%async_computation | async-start | bytes 3145728 | tf_op jit(solution)/shard_map/all_to_all | solution.py:344
  18.9 2.8 collective-permute-start
  23.4 4.3 %collective-permute-done = bf16[128,512]{1,0:T(8,128)(2,1)S(1)} collective-permute-done((bf16[128,512]{1,0:T(8,128)(2,1)S(1)}, bf16[128,512]{1,0:T(8,128)(2,1)S(1)}, u32[]{:S(2)}, u32[]{:S(2)}) %collective-permute-start) | collective-permute-done | bytes 131104 | tf_op jit(solution)/shard_map/ppermute | solution.py:20
  27.7 1.8 collective-permute-done.1
  31.4 10.1 %all-to-all-done = bf16[32,48,512]{2,1,0:T(8,128)(2,1)S(1)} async-done(((bf16[32,48,512]{2,1,0:T(8,128)(2,1)}), bf16[32,48,512]{2,1,0:T(8,128)(2,1)S(1)}, u32[]{:S(2)}, u32[]{:S(2)}) %all-to-all-start) | async-done | bytes 1572896 | tf_op jit(solution)/shard_map/all_to_all | solution.py:344
  42.7 2.4 reshape.65
  50.2 33.3 %collective-permute-done.4.refs_4_ = bf16[4,2,192,512]{3,2,1,0:T(8,128)(2,1)S(1)} collective-permute-done((bf16[4,2,192,512]{3,2,1,0:T(8,128)(2,1)S(1)}, bf16[4,2,192,512]{3,2,1,0:T(8,128)(2,1)S(1)}, u32[]{:S(2)}, u32[]{:S(2)}) %collective-permute-start.4) | collective-permute-done | bytes 1572896 | tf_op jit(solution)/shard_map/ppermute | solution.py:20
  86.4 2.9 collective-permute-start.6
  89.3 14.4 %collective-permute-done.5.refs_2_ = bf16[2,2,192,512]{3,2,1,0:T(8,128)(2,1)S(1)} collective-permute-done((bf16[2,2,192,512]{3,2,1,0:T(8,128)(2,1)}, bf16[2,2,192,512]{3,2,1,0:T(8,128)(2,1)S(1)}, u32[]{:S(2)}, u32[]{:S(2)}) %collective-permute-start.5) | collective-permute-done | bytes 786464 | tf_op jit(solution)/shard_map/ppermute | solution.py:20
  105.4 11.5 %shard_map.110 = (bf16[4,192,2048]{2,1,0:T(8,128)(2,1)}, bf16[4,192,2048]{2,1,0:T(8,128)(2,1)}, bf16[4,384,192]{2,1,0:T(8,128)(2,1)S(1)}, f32[4,384,192]{2,1,0:T(8,128)}, f32[4,384,192]{2,1,0:T(8,128)}) custom-call(s32[4]{0:T(128)S(1)} %pad_add_fusion.ids_ref, bf16[4,2,192,512]{3,2,1,0:T(8,128)(2,1)} %copy-done.11, bf16[4,2,192,512]{3,2,1,0:T(8,128)(2,1)} %copy-done.21, ...), custom_call_target="tpu_custom_call" | custom-call | flops 5435817984 | bytes 27262976 | tf_op jit(solution)/shard_map/pallas_call | solution.py:260
  117.7 11.5 %shard_map.111 = (bf16[4,192,2048]{2,1,0:T(8,128)(2,1)}, bf16[4,192,2048]{2,1,0:T(8,128)(2,1)}, bf16[4,384,512]{2,1,0:T(8,128)(2,1)S(1)}) custom-call(s32[4]{0:T(128)S(1)} %pad_add_fusion.ids_ref, bf16[16,528,512]{2,1,0:T(8,128)(2,1)} %bitcast.57), custom_call_target="tpu_custom_call" | custom-call | flops 4294967296 | bytes 18874368 | tf_op jit(solution)/shard_map/pallas_call | solution.py:104
  132.0 12.3 %shard_map.112 = (bf16[4,2,128,512]{3,2,1,0:T(8,128)(2,1)}, bf16[4,2,128,512]{3,2,1,0:T(8,128)(2,1)}, bf16[2,2,128,512]{3,2,1,0:T(8,128)(2,1)S(1)}, bf16[2,2,128...) custom-call(s32[4]{0:T(128)S(1)} %pad_add_fusion.ids_ref, ...), custom_call_target="tpu_custom_call" | custom-call | flops 4294967296 | bytes 16777216 | tf_op jit(solution)/shard_map/pallas_call | solution.py:162
  146.0 13.4 %shard_map.113 = (bf16[4,384,192]{2,1,0:T(8,128)(2,1)S(1)}, bf16[4,384,192]{2,1,0:T(8,128)(2,1)S(1)}, bf16[4,4,2,192,512]{4,3,2,1,0:T(8,128)(2,1)}) custom-call(s32[4]{0:T(128)S(1)} %pad_add_fusion.ids_ref, bf16[4,192,2048]{2,1,0:T(8,128)(2,1)} %get-tuple-element.62.own.refs_5_, bf16[4,192,2048]{2,1,0:T(8,128)(2,1)} %copy-done.26, ...), custom_call_target="tpu_custom_call" | custom-call | flops 5435817984 | bytes 27262976 | tf_op jit(solution)/shard_map/pallas_call | solution.py:260
  161.2 2.6 collective-permute-start.12
  167.3 8.8 %collective-permute-done.12 = bf16[2,2,128,512]{3,2,1,0:T(8,128)(2,1)S(1)} collective-permute-done((bf16[2,2,128,512]{3,2,1,0:T(8,128)(2,1)}, bf16[2,2,128,512]{3,2,1,0:T(8,128)(2,1)S(1)}, u32[]{:S(2)}, u32[]{:S(2)}) %collective-permute-start.12) | collective-permute-done | bytes 524320 | tf_op jit(solution)/shard_map/ppermute | solution.py:20
  176.3 2.8 collective-permute-done.11
  179.7 1.8 collective-permute-done.9
  182.6 2.4 collective-permute-start.16
  185.0 3.2 %collective-permute-start.14 = (bf16[4,2,128,512]{3,2,1,0:T(8,128)(2,1)S(1)}, bf16[4,2,128,512]{3,2,1,0:T(8,128)(2,1)S(1)}, u32[]{:S(2)}, u32[]{:S(2)}) collective-permute-start(bf16[4,2,128,512]{3,2,1,0:T(8,128)(2,1)S(1)} %pad_maximum_fusion.1), channel_id=1, source_target_pairs={{32,0},{64,32},{96,64},{0,96},{33,1},{65,33},{97,65},{1,97},{34,2}... | collective-permute-start | bytes 3145736 | tf_op jit(solution)/shard_map/ppermute | solution.py:20
  188.3 11.0 %shard_map.114 = (bf16[4,192,2048]{2,1,0:T(8,128)(2,1)}, bf16[4,192,2048]{2,1,0:T(8,128)(2,1)}, bf16[4,192,2048]{2,1,0:T(8,128)(2,1)}) custom-call(s32[4]{0:T(128)S(1)} %pad_add_fusion.ids_ref, bf16[4,2,192,512]{3,2,1,0:T(8,128)(2,1)} %copy-done.11, bf16[4,2,192,512]{3,2,1,0:T(8,128)(2,1)} %copy-done.21, ...), custom_call_target="tpu_custom_call" | custom-call | flops 5435817984 | bytes 25165824 | tf_op jit(solution)/shard_map/pallas_call | solution.py:260
  199.3 7.9 %collective-permute-done.15 = bf16[4,2,128,512]{3,2,1,0:T(8,128)(2,1)S(1)} collective-permute-done((bf16[4,2,128,512]{3,2,1,0:T(8,128)(2,1)S(1)}, bf16[4,2,128,512]{3,2,1,0:T(8,128)(2,1)S(1)}, u32[]{:S(2)}, u32[]{:S(2)}) %collective-permute-start.15) | collective-permute-done | bytes 1048608 | tf_op jit(solution)/shard_map/ppermute | solution.py:20
  212.2 3.2 %collective-permute-start.18 = (bf16[2,128,512]{2,1,0:T(8,128)(2,1)}, bf16[2,128,512]{2,1,0:T(8,128)(2,1)S(1)}, u32[]{:S(2)}, u32[]{:S(2)}) collective-permute-start(bf16[2,128,512]{2,1,0:T(8,128)(2,1)} %get-tuple-element.113), channel_id=1, source_target_pairs={{8,0},{12,4},{0,8},{4,12},{9,1},{13,5},{1,9},{5,13},{10,2},{14,6},... | collective-permute-start | bytes 786440 | tf_op jit(solution)/shard_map/ppermute | solution.py:20
  216.4 9.5 %reduce-scatter.2.cloned.1.call-done = bf16[1536,512]{1,0:T(8,128)(2,1)} async-done(((bf16[6144,512]{1,0:T(8,128)(2,1)}), bf16[1536,512]{1,0:T(8,128)(2,1)}) %reduce-scatter.2.cloned.1.call-update) | async-done | bytes 1572880 | tf_op jit(solution)/shard_map/reduce_scatter | solution.py:371
  225.9 2.4 reshape.68
  229.8 3.7 %reshape.73 = bf16[32,48,512]{2,1,0:T(8,128)(2,1)} reshape(bf16[4,2,4,4,12,512]{5,4,3,2,1,0:T(8,128)(2,1)} %copy.39) | data formatting | bytes 3145728 | tf_op jit(solution)/shard_map/all_to_all | solution.py:344
  233.5 7.4 %all-to-all-start.1 = ((bf16[32,48,512]{2,1,0:T(8,128)(2,1)}), bf16[32,48,512]{2,1,0:T(8,128)(2,1)S(1)}, u32[]{:S(2)}, u32[]{:S(2)}) async-start(bf16[32,48,512]{2,1,0:T(8,128)(2,1)} %reshape.73), calls=%async_computation.2 | async-start | bytes 3145728 | tf_op jit(solution)/shard_map/all_to_all | solution.py:344
  240.9 1.9 collective-permute-start.21
  242.8 2.7 collective-permute-start.22
  249.3 18.4 %collective-permute-done.21 = bf16[2,128,512]{2,1,0:T(8,128)(2,1)S(1)} collective-permute-done((bf16[2,128,512]{2,1,0:T(8,128)(2,1)S(1)}, bf16[2,128,512]{2,1,0:T(8,128)(2,1)S(1)}, u32[]{:S(2)}, u32[]{:S(2)}) %collective-permute-start.21) | collective-permute-done | bytes 262176 | tf_op jit(solution)/shard_map/ppermute | solution.py:20
  267.6 5.8 %collective-permute-done.22 = bf16[2,128,512]{2,1,0:T(8,128)(2,1)S(1)} collective-permute-done((bf16[2,128,512]{2,1,0:T(8,128)(2,1)S(1)}, bf16[2,128,512]{2,1,0:T(8,128)(2,1)S(1)}, u32[]{:S(2)}, u32[]{:S(2)}) %collective-permute-start.22) | collective-permute-done | bytes 262176 | tf_op jit(solution)/shard_map/ppermute | solution.py:20
  276.6 3.6 %collective-permute-done.24 = bf16[128,512]{1,0:T(8,128)(2,1)S(1)} collective-permute-done((bf16[128,512]{1,0:T(8,128)(2,1)S(1)}, bf16[128,512]{1,0:T(8,128)(2,1)S(1)}, u32[]{:S(2)}, u32[]{:S(2)}) %collective-permute-start.24) | collective-permute-done | bytes 131104 | tf_op jit(solution)/shard_map/ppermute | solution.py:20
  282.0 2.0 convolution_convert_fusion.1
  (132 shorter events, 46.2 us)
Async XLA Ops:
  10.2 31.3 %all-to-all-start = ((bf16[32,48,512]{2,1,0:T(8,128)(2,1)}), bf16[32,48,512]{2,1,0:T(8,128)(2,1)S(1)}, u32[]{:S(2)}, u32[]{:S(2)}) async-start(bf16[32,48,512]{2,1,0:T(8,128)(2,1)} %bitcast.54), calls=%async_computation | async-start | bytes 3145728 | tf_op jit(solution)/shard_map/all_to_all | solution.py:344
  18.8 98.9 %all-gather.3.cloned.1.call-start = ((), (), s32[]{:S(2)}) async-start(), calls=%async_computation.4 | async-start | bytes 9191424 | tf_op jit(solution)/shard_map/all_gather | solution.py:352
  18.9 8.9 %collective-permute-start = (bf16[128,512]{1,0:T(8,128)(2,1)S(1)}, bf16[128,512]{1,0:T(8,128)(2,1)S(1)}, u32[]{:S(2)}, u32[]{:S(2)}) collective-permute-start(bf16[128,512]{1,0:T(8,128)(2,1)S(1)} %copy-done.23), channel_id=1, source_target_pairs={{1,0},{2,1},{3,2},{0,3},{5,4},{6,5},{7,6},{4,7},{9,8},{10,9},{11,1... | collective-permute-start | bytes 393224 | tf_op jit(solution)/shard_map/ppermute | solution.py:20
  21.7 7.9 %collective-permute-start.1 = (bf16[128,512]{1,0:T(8,128)(2,1)S(1)}, bf16[128,512]{1,0:T(8,128)(2,1)S(1)}, u32[]{:S(2)}, u32[]{:S(2)}) collective-permute-start(bf16[128,512]{1,0:T(8,128)(2,1)S(1)} %copy-done.23), channel_id=1, source_target_pairs={{2,0},{3,1},{0,2},{1,3},{6,4},{7,5},{4,6},{5,7},{10,8},{11,9},{8,1... | collective-permute-start | bytes 393224 | tf_op jit(solution)/shard_map/ppermute | solution.py:20
  22.5 8.9 %collective-permute-start.2 = (bf16[128,512]{1,0:T(8,128)(2,1)S(1)}, bf16[128,512]{1,0:T(8,128)(2,1)S(1)}, u32[]{:S(2)}, u32[]{:S(2)}) collective-permute-start(bf16[128,512]{1,0:T(8,128)(2,1)S(1)} %copy-done.23), channel_id=1, source_target_pairs={{3,0},{0,1},{1,2},{2,3},{7,4},{4,5},{5,6},{6,7},{11,8},{8,9},{9,10... | collective-permute-start | bytes 393224 | tf_op jit(solution)/shard_map/ppermute | solution.py:20
  42.7 183.2 %reduce-scatter.2.cloned.1.call-start = ((), (), s32[]{:S(2)}) async-start(), calls=%async_computation.3 | async-start | bytes 7864320 | tf_op jit(solution)/shard_map/reduce_scatter | solution.py:371
  46.9 57.6 %copy-start.11 = (bf16[4,2,192,512]{3,2,1,0:T(8,128)(2,1)}, bf16[4,2,192,512]{3,2,1,0:T(8,128)(2,1)S(1)}, u32[]{:S(2)}) copy-start(bf16[4,2,192,512]{3,2,1,0:T(8,128)(2,1)S(1)} %copy.36.refs_0_) | copy-start | bytes 4718596
  46.9 36.6 %collective-permute-start.4 = (bf16[4,2,192,512]{3,2,1,0:T(8,128)(2,1)S(1)}, bf16[4,2,192,512]{3,2,1,0:T(8,128)(2,1)S(1)}, u32[]{:S(2)}, u32[]{:S(2)}) collective-permute-start(bf16[4,2,192,512]{3,2,1,0:T(8,128)(2,1)S(1)} %copy.36.refs_0_), channel_id=1, source_target_pairs={{3,0},{0,1},{1,2},{2,3},{7,4},{4,5},{5,6},{6,7},{11,8},{8,9},{9,10... | collective-permute-start | bytes 4718600 | tf_op jit(solution)/shard_map/ppermute | solution.py:20
  48.5 36.4 %collective-permute-start.3 = (bf16[4,2,192,512]{3,2,1,0:T(8,128)(2,1)S(1)}, bf16[4,2,192,512]{3,2,1,0:T(8,128)(2,1)S(1)}, u32[]{:S(2)}, u32[]{:S(2)}) collective-permute-start(bf16[4,2,192,512]{3,2,1,0:T(8,128)(2,1)S(1)} %copy.36.refs_0_), channel_id=1, source_target_pairs={{1,0},{2,1},{3,2},{0,3},{5,4},{6,5},{7,6},{4,7},{9,8},{10,9},{11,1... | collective-permute-start | bytes 4718600 | tf_op jit(solution)/shard_map/ppermute | solution.py:20
  84.6 19.1 %collective-permute-start.5 = (bf16[2,2,192,512]{3,2,1,0:T(8,128)(2,1)}, bf16[2,2,192,512]{3,2,1,0:T(8,128)(2,1)S(1)}, u32[]{:S(2)}, u32[]{:S(2)}) collective-permute-start(bf16[2,2,192,512]{3,2,1,0:T(8,128)(2,1)} %slice.88), channel_id=1, source_target_pairs={{3,0},{0,1},{1,2},{2,3},{7,4},{4,5},{5,6},{6,7},{11,8},{8,9},{9,10... | collective-permute-start | bytes 2359304 | tf_op jit(solution)/shard_map/ppermute | solution.py:20
  86.4 18.1 %collective-permute-start.6 = (bf16[2,2,192,512]{3,2,1,0:T(8,128)(2,1)}, bf16[2,2,192,512]{3,2,1,0:T(8,128)(2,1)S(1)}, u32[]{:S(2)}, u32[]{:S(2)}) collective-permute-start(bf16[2,2,192,512]{3,2,1,0:T(8,128)(2,1)} %slice.89), channel_id=1, source_target_pairs={{1,0},{2,1},{3,2},{0,3},{5,4},{6,5},{7,6},{4,7},{9,8},{10,9},{11,1... | collective-permute-start | bytes 2359304 | tf_op jit(solution)/shard_map/ppermute | solution.py:20
  117.7 12.7 %collective-permute-start.7 = (bf16[4,192,2048]{2,1,0:T(8,128)(2,1)}, bf16[4,192,2048]{2,1,0:T(8,128)(2,1)S(1)}, u32[]{:S(2)}, u32[]{:S(2)}) collective-permute-start(bf16[4,192,2048]{2,1,0:T(8,128)(2,1)} %get-tuple-element.64), channel_id=1, source_target_pairs={{16,0},{0,16},{17,1},{1,17},{18,2},{2,18},{19,3},{3,19},{20,4},{4,... | collective-permute-start | bytes 9437192 | tf_op jit(solution)/shard_map/ppermute | solution.py:20
  130.4 13.9 %collective-permute-start.8 = (bf16[4,192,2048]{2,1,0:T(8,128)(2,1)}, bf16[4,192,2048]{2,1,0:T(8,128)(2,1)S(1)}, u32[]{:S(2)}, u32[]{:S(2)}) collective-permute-start(bf16[4,192,2048]{2,1,0:T(8,128)(2,1)} %get-tuple-element.65), channel_id=1, source_target_pairs={{16,0},{0,16},{17,1},{1,17},{18,2},{2,18},{19,3},{3,19},{20,4},{4,... | collective-permute-start | bytes 9437192 | tf_op jit(solution)/shard_map/ppermute | solution.py:20
  161.2 14.8 %collective-permute-start.12 = (bf16[2,2,128,512]{3,2,1,0:T(8,128)(2,1)}, bf16[2,2,128,512]{3,2,1,0:T(8,128)(2,1)S(1)}, u32[]{:S(2)}, u32[]{:S(2)}) collective-permute-start(bf16[2,2,128,512]{3,2,1,0:T(8,128)(2,1)} %get-tuple-element.93), channel_id=1, source_target_pairs={{4,0},{8,4},{12,8},{0,12},{5,1},{9,5},{13,9},{1,13},{6,2},{10,6},{... | collective-permute-start | bytes 1572872 | tf_op jit(solution)/shard_map/ppermute | solution.py:20
  163.9 15.3 %collective-permute-start.11 = (bf16[2,2,128,512]{3,2,1,0:T(8,128)(2,1)S(1)}, bf16[2,2,128,512]{3,2,1,0:T(8,128)(2,1)S(1)}, u32[]{:S(2)}, u32[]{:S(2)}) collective-permute-start(bf16[2,2,128,512]{3,2,1,0:T(8,128)(2,1)S(1)} %get-tuple-element.91), channel_id=1, source_target_pairs={{12,0},{0,4},{4,8},{8,12},{13,1},{1,5},{5,9},{9,13},{14,2},{2,6},{... | collective-permute-start | bytes 1572872 | tf_op jit(solution)/shard_map/ppermute | solution.py:20
  165.0 14.4 %collective-permute-start.10 = (bf16[2,2,128,512]{3,2,1,0:T(8,128)(2,1)S(1)}, bf16[2,2,128,512]{3,2,1,0:T(8,128)(2,1)S(1)}, u32[]{:S(2)}, u32[]{:S(2)}) collective-permute-start(bf16[2,2,128,512]{3,2,1,0:T(8,128)(2,1)S(1)} %get-tuple-element.88), channel_id=1, source_target_pairs={{32,0},{64,32},{96,64},{0,96},{33,1},{65,33},{97,65},{1,97},{34,2}... | collective-permute-start | bytes 1572872 | tf_op jit(solution)/shard_map/ppermute | solution.py:20
  166.5 14.9 %collective-permute-start.9 = (bf16[2,2,128,512]{3,2,1,0:T(8,128)(2,1)S(1)}, bf16[2,2,128,512]{3,2,1,0:T(8,128)(2,1)S(1)}, u32[]{:S(2)}, u32[]{:S(2)}) collective-permute-start(bf16[2,2,128,512]{3,2,1,0:T(8,128)(2,1)S(1)} %get-tuple-element.86), channel_id=1, source_target_pairs={{96,0},{0,32},{32,64},{64,96},{97,1},{1,33},{33,65},{65,97},{98,2}... | collective-permute-start | bytes 1572872 | tf_op jit(solution)/shard_map/ppermute | solution.py:20
  181.7 25.4 %collective-permute-start.15 = (bf16[4,2,128,512]{3,2,1,0:T(8,128)(2,1)S(1)}, bf16[4,2,128,512]{3,2,1,0:T(8,128)(2,1)S(1)}, u32[]{:S(2)}, u32[]{:S(2)}) collective-permute-start(bf16[4,2,128,512]{3,2,1,0:T(8,128)(2,1)S(1)} %pad_maximum_fusion.2), channel_id=1, source_target_pairs={{12,0},{0,4},{4,8},{8,12},{13,1},{1,5},{5,9},{9,13},{14,2},{2,6},{... | collective-permute-start | bytes 3145736 | tf_op jit(solution)/shard_map/ppermute | solution.py:20
  182.6 24.5 %collective-permute-start.16 = (bf16[4,2,128,512]{3,2,1,0:T(8,128)(2,1)S(1)}, bf16[4,2,128,512]{3,2,1,0:T(8,128)(2,1)S(1)}, u32[]{:S(2)}, u32[]{:S(2)}) collective-permute-start(bf16[4,2,128,512]{3,2,1,0:T(8,128)(2,1)S(1)} %pad_maximum_fusion.3), channel_id=1, source_target_pairs={{4,0},{8,4},{12,8},{0,12},{5,1},{9,5},{13,9},{1,13},{6,2},{10,6},{... | collective-permute-start | bytes 3145736 | tf_op jit(solution)/shard_map/ppermute | solution.py:20
  185.0 24.8 %collective-permute-start.13 = (bf16[4,2,128,512]{3,2,1,0:T(8,128)(2,1)S(1)}, bf16[4,2,128,512]{3,2,1,0:T(8,128)(2,1)S(1)}, u32[]{:S(2)}, u32[]{:S(2)}) collective-permute-start(bf16[4,2,128,512]{3,2,1,0:T(8,128)(2,1)S(1)} %pad_maximum_fusion), channel_id=1, source_target_pairs={{96,0},{0,32},{32,64},{64,96},{97,1},{1,33},{33,65},{65,97},{98,2}... | collective-permute-start | bytes 3145736 | tf_op jit(solution)/shard_map/ppermute | solution.py:20
  185.0 24.8 %collective-permute-start.14 = (bf16[4,2,128,512]{3,2,1,0:T(8,128)(2,1)S(1)}, bf16[4,2,128,512]{3,2,1,0:T(8,128)(2,1)S(1)}, u32[]{:S(2)}, u32[]{:S(2)}) collective-permute-start(bf16[4,2,128,512]{3,2,1,0:T(8,128)(2,1)S(1)} %pad_maximum_fusion.1), channel_id=1, source_target_pairs={{32,0},{64,32},{96,64},{0,96},{33,1},{65,33},{97,65},{1,97},{34,2}... | collective-permute-start | bytes 3145736 | tf_op jit(solution)/shard_map/ppermute | solution.py:20
  212.2 33.3 %collective-permute-start.17 = (bf16[2,128,512]{2,1,0:T(8,128)(2,1)}, bf16[2,128,512]{2,1,0:T(8,128)(2,1)S(1)}, u32[]{:S(2)}, u32[]{:S(2)}) collective-permute-start(bf16[2,128,512]{2,1,0:T(8,128)(2,1)} %get-tuple-element.111), channel_id=1, source_target_pairs={{12,0},{0,4},{4,8},{8,12},{13,1},{1,5},{5,9},{9,13},{14,2},{2,6},{... | collective-permute-start | bytes 786440 | tf_op jit(solution)/shard_map/ppermute | solution.py:20
  212.2 34.7 %collective-permute-start.18 = (bf16[2,128,512]{2,1,0:T(8,128)(2,1)}, bf16[2,128,512]{2,1,0:T(8,128)(2,1)S(1)}, u32[]{:S(2)}, u32[]{:S(2)}) collective-permute-start(bf16[2,128,512]{2,1,0:T(8,128)(2,1)} %get-tuple-element.113), channel_id=1, source_target_pairs={{8,0},{12,4},{0,8},{4,12},{9,1},{13,5},{1,9},{5,13},{10,2},{14,6},... | collective-permute-start | bytes 786440 | tf_op jit(solution)/shard_map/ppermute | solution.py:20
  215.5 32.2 %collective-permute-start.19 = (bf16[2,128,512]{2,1,0:T(8,128)(2,1)}, bf16[2,128,512]{2,1,0:T(8,128)(2,1)}, u32[]{:S(2)}, u32[]{:S(2)}) collective-permute-start(bf16[2,128,512]{2,1,0:T(8,128)(2,1)} %get-tuple-element.112), channel_id=1, source_target_pairs={{4,0},{8,4},{12,8},{0,12},{5,1},{9,5},{13,9},{1,13},{6,2},{10,6},{... | collective-permute-start | bytes 786440 | tf_op jit(solution)/shard_map/ppermute | solution.py:20
  233.5 48.5 %all-to-all-start.1 = ((bf16[32,48,512]{2,1,0:T(8,128)(2,1)}), bf16[32,48,512]{2,1,0:T(8,128)(2,1)S(1)}, u32[]{:S(2)}, u32[]{:S(2)}) async-start(bf16[32,48,512]{2,1,0:T(8,128)(2,1)} %reshape.73), calls=%async_computation.2 | async-start | bytes 3145728 | tf_op jit(solution)/shard_map/all_to_all | solution.py:344
  240.9 26.7 %collective-permute-start.21 = (bf16[2,128,512]{2,1,0:T(8,128)(2,1)S(1)}, bf16[2,128,512]{2,1,0:T(8,128)(2,1)S(1)}, u32[]{:S(2)}, u32[]{:S(2)}) collective-permute-start(bf16[2,128,512]{2,1,0:T(8,128)(2,1)S(1)} %get-tuple-element.114), channel_id=1, source_target_pairs={{96,0},{0,32},{32,64},{64,96},{97,1},{1,33},{33,65},{65,97},{98,2}... | collective-permute-start | bytes 786440 | tf_op jit(solution)/shard_map/ppermute | solution.py:20
  242.8 30.6 %collective-permute-start.22 = (bf16[2,128,512]{2,1,0:T(8,128)(2,1)S(1)}, bf16[2,128,512]{2,1,0:T(8,128)(2,1)S(1)}, u32[]{:S(2)}, u32[]{:S(2)}) collective-permute-start(bf16[2,128,512]{2,1,0:T(8,128)(2,1)S(1)} %get-tuple-element.116), channel_id=1, source_target_pairs={{64,0},{96,32},{0,64},{32,96},{65,1},{97,33},{1,65},{33,97},{66,2}... | collective-permute-start | bytes 786440 | tf_op jit(solution)/shard_map/ppermute | solution.py:20
  245.5 27.9 %collective-permute-start.23 = (bf16[2,128,512]{2,1,0:T(8,128)(2,1)S(1)}, bf16[2,128,512]{2,1,0:T(8,128)(2,1)S(1)}, u32[]{:S(2)}, u32[]{:S(2)}) collective-permute-start(bf16[2,128,512]{2,1,0:T(8,128)(2,1)S(1)} %get-tuple-element.115), channel_id=1, source_target_pairs={{32,0},{64,32},{96,64},{0,96},{33,1},{65,33},{97,65},{1,97},{34,2}... | collective-permute-start | bytes 786440 | tf_op jit(solution)/shard_map/ppermute | solution.py:20
  248.9 35.1 %copy-start.1 = (bf16[128,512]{1,0:T(8,128)(2,1)S(1)}, bf16[128,512]{1,0:T(8,128)(2,1)}, u32[]{:S(2)}) copy-start(bf16[128,512]{1,0:T(8,128)(2,1)} %param.7) | copy-start | bytes 393220
  248.9 27.7 %collective-permute-start.20 = (bf16[128,512]{1,0:T(8,128)(2,1)S(1)}, bf16[128,512]{1,0:T(8,128)(2,1)S(1)}, u32[]{:S(2)}, u32[]{:S(2)}) collective-permute-start(bf16[128,512]{1,0:T(8,128)(2,1)S(1)} %slice_bitcast_fusion.8), channel_id=1, source_target_pairs={{3,0},{0,1},{1,2},{2,3},{7,4},{4,5},{5,6},{6,7},{11,8},{8,9},{9,10... | collective-permute-start | bytes 393224 | tf_op jit(solution)/shard_map/ppermute | solution.py:20
  273.6 6.6 %collective-permute-start.24 = (bf16[128,512]{1,0:T(8,128)(2,1)S(1)}, bf16[128,512]{1,0:T(8,128)(2,1)S(1)}, u32[]{:S(2)}, u32[]{:S(2)}) collective-permute-start(bf16[128,512]{1,0:T(8,128)(2,1)S(1)} %get-tuple-element.117), channel_id=1, source_target_pairs={{2,0},{3,1},{0,2},{1,3},{6,4},{7,5},{4,6},{5,7},{10,8},{11,9},{8,1... | collective-permute-start | bytes 393224 | tf_op jit(solution)/shard_map/ppermute | solution.py:20
  275.1 6.1 %collective-permute-start.25 = (bf16[128,512]{1,0:T(8,128)(2,1)S(1)}, bf16[128,512]{1,0:T(8,128)(2,1)S(1)}, u32[]{:S(2)}, u32[]{:S(2)}) collective-permute-start(bf16[128,512]{1,0:T(8,128)(2,1)S(1)} %get-tuple-element.118), channel_id=1, source_target_pairs={{1,0},{2,1},{3,2},{0,3},{5,4},{6,5},{7,6},{4,7},{9,8},{10,9},{11,1... | collective-permute-start | bytes 393224 | tf_op jit(solution)/shard_map/ppermute | solution.py:20
  (26 other events, 148.7 us)
Sparse Core Ops, SparseCore 0:
  41.7 70.0 all-gather.2
  161.3 64.4 reduce-scatter.1

commit v2 on v1

--- a/solution.py
+++ b/solution.py
@@ -296,6 +296,46 @@
     return per_expert(weights_kernel, ids, specs, args, outs, tuple(each(a) for a in outs), 3, 24)
 
 
+def regroup_matrix(span):
+    n = 4 * span
+    line = lax.broadcasted_iota(jnp.int32, (n, n), 0)
+    col = lax.broadcasted_iota(jnp.int32, (n, n), 1)
+    swapped = (lax.rem(line // CAP, 4) * 4 + line // span) * CAP + lax.rem(line, CAP)
+    return (swapped == col).astype(BF)
+
+
+def by_expert_kernel(rows_ref, out_ref):
+    span = out_ref.shape[2]
+    rows = nn(regroup_matrix(span), rows_ref[0]).astype(BF)
+    for e in range(out_ref.shape[0]):
+        out_ref[e, 0] = rows[e * span : (e + 1) * span]
+
+
+def by_group_kernel(rows_ref, out_ref):
+    span = rows_ref.shape[2]
+    rows = jnp.concatenate([rows_ref[e, 0] for e in range(rows_ref.shape[0])], axis=0)
+    out_ref[0] = tn(regroup_matrix(span), rows).astype(BF)
+
+
+def regroup(rows, to_experts):
+    width = rows.shape[-1]
+    span = 4 * CAP
+    flat = pl.BlockSpec((1, 4 * span, width), lambda i: (i, 0, 0))
+    deep = pl.BlockSpec((4, 1, span, width), lambda i: (0, lax.rem(i, 2), i // 2, 0))
+    cost = pl.CostEstimate(flops=2 * 1536 * 192 * width, bytes_accessed=3 << 20, transcendentals=0)
+    if to_experts:
+        shape = jax.ShapeDtypeStruct((4, 2, 4 * span, width), BF)
+        return pl.pallas_call(
+            by_expert_kernel, grid=(8,), out_shape=shape, in_specs=[flat], out_specs=deep,
+            cost_estimate=cost,
+        )(rows.reshape(8, 4 * span, width))
+    shape = jax.ShapeDtypeStruct((8, 4 * span, width), BF)
+    return pl.pallas_call(
+        by_group_kernel, grid=(8,), out_shape=shape, in_specs=[deep], out_specs=flat,
+        cost_estimate=cost,
+    )(rows.reshape(4, 2, 4 * span, width)).reshape(-1, width)
+
+
 def collect_far(parts, axis):
     own, up, far_lo, far_hi, down = parts
     half = far_lo.shape[0]
@@ -329,7 +369,6 @@
     tok, width = tokens.shape
     weights = (w_gate, w_up, w_down)
 
-    cot = [cotangent] + [fetch(cotangent, "x", r) for r in (1, 2, 3)]
     routes_t = routes.T
     experts_all = jnp.arange(total_exp, dtype=jnp.int32)
     named = jnp.sum((routes_t[:, None, :] == experts_all[None, :, None]).astype(F32), axis=0)
@@ -343,41 +382,41 @@
     def exchange(a):
         return lax.all_to_all(a, GROUP, split_axis=0, concat_axis=0, tiled=True)
 
-    came = exchange(jnp.dot(own_map, tokens, preferred_element_type=F32).astype(BF))
-
+    sent = jnp.dot(own_map, tokens, preferred_element_type=F32).astype(BF)
+    sent, cotangent = lax.optimization_barrier((sent, cotangent))
+    came = regroup(exchange(sent), True)
+    up, down = fetch(came, "x", 1), fetch(came, "x", -1)
+    pair = n_exp // 2
+    far_lo, far_hi = fetch(down[:pair], "x", -1), fetch(up[pair:], "x", 1)
+
+    cot = [cotangent] + [fetch(cotangent, "x", r) for r in (1, 2, 3)]
     meta = jnp.concatenate([routes_t.astype(BF), gates.T], axis=0)
     meta = jnp.pad(meta, ((0, 0), (0, width - tok)))
-    whole = jnp.concatenate(cot + [meta])
-    came, whole = lax.optimization_barrier((came, whole))
-    whole = lax.all_gather(whole, ("y", "z"))
-
-    came = came.reshape(4, 2, 4, n_exp, CAP, width).transpose(3, 1, 0, 2, 4, 5)
-    came = came.reshape(n_exp, 2, 16 * CAP, width)
-    up, down = fetch(came, "x", 1), fetch(came, "x", -1)
-    pair = n_exp // 2
-    x_blocks = (came, up, fetch(down[:pair], "x", -1), fetch(up[pair:], "x", 1), down)
+    whole = lax.all_gather(jnp.concatenate(cot + [meta]), ("y", "z"))
+    whole, up, down = lax.optimization_barrier((whole, up, down))
+    own, sib, maps = pick(ids, whole, n_exp)
+
+    sib, far_lo, far_hi = lax.optimization_barrier((sib, far_lo, far_hi))
+    x_blocks = (came, up, far_lo, far_hi, down)
     out_own, out_sib, hidden, slope, act = forward(ids, x_blocks, weights)
-
-    whole, out_sib = lax.optimization_barrier((whole, out_sib))
-    own, sib, maps = pick(ids, whole, n_exp)
-    sib, out_sib = lax.optimization_barrier((sib, fetch(out_sib, "c", 1)))
-
-    sums = sum_tokens(ids, maps, out_own, out_sib)
-    sib, sums = lax.optimization_barrier((fetch(sib, "c", 1), sums))
-    ends_y, ends_z = collect_far(sums[:5], "y"), collect_far(sums[5:], "z")
+    out_sib, sib = lax.optimization_barrier((out_sib, fetch(sib, "c", 1)))
     g_blocks = (own, sib)
     mid = jax.ShapeDtypeStruct(hidden.shape, BF)
     grad_a, grad_b, back = backward(ids, g_blocks, slope, act, weights, mid, came.shape)
     back = lax.psum_scatter(back.reshape(-1, width), "x", scatter_dimension=0, tiled=True)
-    grad_a, ends_y, ends_z = lax.optimization_barrier((grad_a, ends_y, ends_z))
+
+    out_sib, grad_a = lax.optimization_barrier((fetch(out_sib, "c", 1), grad_a))
+    sums = sum_tokens(ids, maps, out_own, out_sib)
+    ends_y, ends_z = collect_far(sums[:5], "y"), collect_far(sums[5:], "z")
+    hidden, ends_y, ends_z = lax.optimization_barrier((hidden, ends_y, ends_z))
     grads = weight_grads(ids, x_blocks, g_blocks, (hidden, grad_a, grad_b), w_gate)
     part1, part2 = collect_near(ends_y, "y"), collect_near(ends_z, "z")
     grads, part1, part2 = lax.optimization_barrier((grads, part1, part2))
     part1, part2 = collect_small(part1, "z"), collect_small(part2, "y")
+
+    back, part1 = lax.optimization_barrier((back, part1))
+    back = exchange(regroup(back, False))
     mixed = collect_small((part1[0], part1[1], part2[0], part2[1]), "x")
-
-    back = back.reshape(n_exp, 2, 4, 4, CAP, width).transpose(2, 1, 3, 0, 4, 5)
-    back = exchange(back.reshape(slots, width))
     grad_tokens = tn(own_map, back).astype(BF)
     return (mixed, grad_tokens) + tuple(grads)
 

time: 292 us -> 301 us (1.031)
  blocking collectives: 0 us -> 40 us
  waiting for transfers between devices: 127 us -> 110 us
  Pallas kernels: 59.6 us -> 72.7 us
  local copies, waits for them, and re-layouts: 27 us -> 13.9 us
  starting transfers between devices: 52.3 us -> 43.4 us
    all_to_all x0 -> x1, blocking collectives: none -> 40 us  [exchange(): return lax.all_to_all(a, GROUP, split_axis=0, concat_axis=0, tiled=True)]
    pallas_call x0 -> x2, Pallas kernels: none -> 12.6 us  [the longest x1 6.48 us: regroup(): pl.pallas_call(by_group_kernel, grid=(8,), out_shape=shape, in_specs=[dee...]
    all_to_all x2 -> x1, starting transfers between devices: 16 us -> 4.19 us  [exchange(): return lax.all_to_all(a, GROUP, split_axis=0, concat_axis=0, tiled=True)]
    all_to_all x2 -> x1, waiting for transfers between devices: 10.1 us -> 0.01 us  [exchange(): return lax.all_to_all(a, GROUP, split_axis=0, concat_axis=0, tiled=True)]
    reduce_scatter x1, waiting for transfers between devices: 9.47 us -> 0.02 us  [body(): lax.psum_scatter(back.reshape(-1, width), 'x', scatter_dimension=0, tiled...]
    all_to_all x2 -> x0, local copies, waits for them, and re-layouts: 5.23 us -> none  [exchange(): return lax.all_to_all(a, GROUP, split_axis=0, concat_axis=0, tiled=True)]
    reshape x3 -> x0, local copies, waits for them, and re-layouts: 4.98 us -> none  [the longest x1 2.35 us: body(): came = came.reshape(4, 2, 4, n_exp, CAP, width).transpose(3, 1, 0, 2, 4, 5)]
    unnamed x60 -> x50, local copies, waits for them, and re-layouts: 11.1 us -> 10.3 us
  transfers between devices with their start and end apart: 30 -> 29, of which waited for: 17 -> 18; matrix products, arithmetic and copies ran while one was open for 7% -> 2% of each run, Pallas kernels for 16% -> 18%
where the time goes in v2:
time: 301 us; the launch traced here: 300 us
  waiting for transfers between devices  110 us (37%)
  Pallas kernels  72.7 us (24%)
  starting transfers between devices  43.4 us (14%)
  blocking collectives  40 us (13%)
  between operations  14.4 us (5%)
  local copies, waits for them, and re-layouts  13.9 us (5%)
  other arithmetic  3.69 us (1%)
    ppermute x26, waiting for transfers between devices, fetch(): return lax.ppermute(a, axis, [((i + r) % n, i) for i in range(n)])  110 us
    all_to_all x1, blocking collectives, exchange(): return lax.all_to_all(a, GROUP, split_axis=0, concat_axis=0, tiled=True)  40 us
    ppermute x26, starting transfers between devices, fetch(): return lax.ppermute(a, axis, [((i + r) % n, i) for i in range(n)])  39.1 us
    pallas_call x3, Pallas kernels, per_expert(): pl.pallas_call(kernel, grid=(n_exp,), out_shape=outs, in_specs=[pl.BlockS...  35.9 us
    pallas_call x1, Pallas kernels, sum_tokens(): pl.pallas_call(sum_kernel, grid_spec=pltpu.PrefetchScalarGridSpec(num_sca...  12.7 us
    pallas_call x1, Pallas kernels, pick(): pl.pallas_call(pick_kernel, grid=(4,), out_shape=(rows, rows, maps), in_s...  11.5 us
    unnamed x50, local copies, waits for them, and re-layouts  10.3 us
    pallas_call x1, Pallas kernels, regroup(): pl.pallas_call(by_group_kernel, grid=(8,), out_shape=shape, in_specs=[dee...  6.48 us
  transfers between devices with their start and end apart: 29, of which 18 were waited for; matrix products, arithmetic and copies ran while one was open for 2% of the time, Pallas kernels for 18%

profile of v2, /device:TPU:0, one launch (start us, length us, event | category | flops | bytes accessed | tf_op | source)
XLA Modules:
  0.0 300.3 jit_solution(13801494395327666870)
XLA Ops:
  10.8 2.7 collective-permute-start.1
  15.0 4.1 %collective-permute-done = bf16[128,512]{1,0:T(8,128)(2,1)S(1)} collective-permute-done((bf16[128,512]{1,0:T(8,128)(2,1)S(1)}, bf16[128,512]{1,0:T(8,128)(2,1)S(1)}, u32[]{:S(2)}, u32[]{:S(2)}) %collective-permute-start) | collective-permute-done | bytes 131104 | tf_op jit(solution)/shard_map/ppermute | solution.py:20
  20.5 40.0 %all_to_all.21 = bf16[32,48,512]{2,1,0:T(8,128)(2,1)} all-to-all(bf16[32,48,512]{2,1,0:T(8,128)(2,1)S(1)} %bitcast.49), channel_id=1, replica_groups=mesh['y'=4,'c'=2,'z'=4,'x'=4] {'y','c','z'}, dimensions={0} | all-to-all | bytes 3145728 | tf_op jit(solution)/shard_map/all_to_all | solution.py:383
  60.5 6.1 %shard_map.110.refs_0_ = bf16[4,2,192,512]{3,2,1,0:T(8,128)(2,1)} custom-call(bf16[8,192,512]{2,1,0:T(8,128)(2,1)} %bitcast.47), custom_call_target="tpu_custom_call" | custom-call | flops 301989888 | bytes 3145728 | tf_op jit(solution)/shard_map/pallas_call | solution.py:328
  68.0 1.9 collective-permute-start.3
  69.9 34.0 %collective-permute-done.4.refs_4_ = bf16[4,2,192,512]{3,2,1,0:T(8,128)(2,1)S(1)} collective-permute-done((bf16[4,2,192,512]{3,2,1,0:T(8,128)(2,1)}, bf16[4,2,192,512]{3,2,1,0:T(8,128)(2,1)S(1)}, u32[]{:S(2)}, u32[]{:S(2)}) %collective-permute-start.4) | collective-permute-done | bytes 1572896 | tf_op jit(solution)/shard_map/ppermute | solution.py:20
  106.4 2.2 collective-permute-start.6
  108.7 11.5 %shard_map.111 = (bf16[4,192,2048]{2,1,0:T(8,128)(2,1)}, bf16[4,192,2048]{2,1,0:T(8,128)(2,1)}, bf16[4,384,512]{2,1,0:T(8,128)(2,1)S(1)}) custom-call(s32[4]{0:T(128)S(1)} %pad_add_fusion.ids_ref, bf16[16,528,512]{2,1,0:T(8,128)(2,1)} %bitcast.53), custom_call_target="tpu_custom_call" | custom-call | flops 4294967296 | bytes 18874368 | tf_op jit(solution)/shard_map/pallas_call | solution.py:104
  121.3 2.0 collective-permute-done.5.refs_2_
  125.6 11.5 %shard_map.112 = (bf16[4,192,2048]{2,1,0:T(8,128)(2,1)}, bf16[4,192,2048]{2,1,0:T(8,128)(2,1)}, bf16[4,384,192]{2,1,0:T(8,128)(2,1)S(1)}, f32[4,384,192]{2,1,0:T(8,128)}, f32[4,384,192]{2,1,0:T(8,128)}) custom-call(s32[4]{0:T(128)S(1)} %pad_add_fusion.ids_ref, bf16[4,2,192,512]{3,2,1,0:T(8,128)(2,1)} %shard_map.110.refs_0_, ...), custom_call_target="tpu_custom_call" | custom-call | flops 5435817984 | bytes 27262976 | tf_op jit(solution)/shard_map/pallas_call | solution.py:260
  139.7 13.4 %shard_map.113 = (bf16[4,384,192]{2,1,0:T(8,128)(2,1)S(1)}, bf16[4,384,192]{2,1,0:T(8,128)(2,1)S(1)}, bf16[4,4,2,192,512]{4,3,2,1,0:T(8,128)(2,1)}) custom-call(s32[4]{0:T(128)S(1)} %pad_add_fusion.ids_ref, bf16[4,192,2048]{2,1,0:T(8,128)(2,1)} %get-tuple-element.58.own.refs_5_, bf16[4,192,2048]{2,1,0:T(8,128)(2,1)} %copy-done.20, ...), custom_call_target="tpu_custom_call" | custom-call | flops 5435817984 | bytes 27262976 | tf_op jit(solution)/shard_map/pallas_call | solution.py:260
  155.1 5.9 %collective-permute-done.8.sib_ref = bf16[4,192,2048]{2,1,0:T(8,128)(2,1)S(1)} collective-permute-done((bf16[4,192,2048]{2,1,0:T(8,128)(2,1)}, bf16[4,192,2048]{2,1,0:T(8,128)(2,1)S(1)}, u32[]{:S(2)}, u32[]{:S(2)}) %collective-permute-start.8) | collective-permute-done | bytes 3145760 | tf_op jit(solution)/shard_map/ppermute | solution.py:20
  162.6 12.7 %shard_map.114 = (bf16[4,2,128,512]{3,2,1,0:T(8,128)(2,1)}, bf16[4,2,128,512]{3,2,1,0:T(8,128)(2,1)}, bf16[2,2,128,512]{3,2,1,0:T(8,128)(2,1)S(1)}, bf16[2,2,128...) custom-call(s32[4]{0:T(128)S(1)} %pad_add_fusion.ids_ref, ...), custom_call_target="tpu_custom_call" | custom-call | flops 4294967296 | bytes 16777216 | tf_op jit(solution)/shard_map/pallas_call | solution.py:162
  181.1 2.5 collective-permute-start.11
  184.5 6.0 %collective-permute-done.9 = bf16[2,2,128,512]{3,2,1,0:T(8,128)(2,1)S(1)} collective-permute-done((bf16[2,2,128,512]{3,2,1,0:T(8,128)(2,1)S(1)}, bf16[2,2,128,512]{3,2,1,0:T(8,128)(2,1)S(1)}, u32[]{:S(2)}, u32[]{:S(2)}) %collective-permute-start.9) | collective-permute-done | bytes 524320 | tf_op jit(solution)/shard_map/ppermute | solution.py:20
  191.0 4.8 %collective-permute-done.11 = bf16[2,2,128,512]{3,2,1,0:T(8,128)(2,1)S(1)} collective-permute-done((bf16[2,2,128,512]{3,2,1,0:T(8,128)(2,1)S(1)}, bf16[2,2,128,512]{3,2,1,0:T(8,128)(2,1)S(1)}, u32[]{:S(2)}, u32[]{:S(2)}) %collective-permute-start.11) | collective-permute-done | bytes 524320 | tf_op jit(solution)/shard_map/ppermute | solution.py:20
  197.0 3.2 %collective-permute-start.14 = (bf16[4,2,128,512]{3,2,1,0:T(8,128)(2,1)S(1)}, bf16[4,2,128,512]{3,2,1,0:T(8,128)(2,1)S(1)}, u32[]{:S(2)}, u32[]{:S(2)}) collective-permute-start(bf16[4,2,128,512]{3,2,1,0:T(8,128)(2,1)S(1)} %pad_maximum_fusion.1), channel_id=1, source_target_pairs={{32,0},{64,32},{96,64},{0,96},{33,1},{65,33},{97,65},{1,97},{34,2}... | collective-permute-start | bytes 3145736 | tf_op jit(solution)/shard_map/ppermute | solution.py:20
  200.8 2.7 collective-permute-start.16
  203.4 10.9 %shard_map.115 = (bf16[4,192,2048]{2,1,0:T(8,128)(2,1)}, bf16[4,192,2048]{2,1,0:T(8,128)(2,1)}, bf16[4,192,2048]{2,1,0:T(8,128)(2,1)}) custom-call(s32[4]{0:T(128)S(1)} %pad_add_fusion.ids_ref, bf16[4,2,192,512]{3,2,1,0:T(8,128)(2,1)} %shard_map.110.refs_0_, bf16[4,2,192,512]{3,2,1,0:T(8,128)(2,1)} %copy-done.16, ...), custom_call_target="tpu_custom_call" | custom-call | flops 5435817984 | bytes 25165824 | tf_op jit(solution)/shard_map/pallas_call | solution.py:260
  214.4 7.3 %collective-permute-done.13 = bf16[4,2,128,512]{3,2,1,0:T(8,128)(2,1)S(1)} collective-permute-done((bf16[4,2,128,512]{3,2,1,0:T(8,128)(2,1)S(1)}, bf16[4,2,128,512]{3,2,1,0:T(8,128)(2,1)S(1)}, u32[]{:S(2)}, u32[]{:S(2)}) %collective-permute-start.13) | collective-permute-done | bytes 1048608 | tf_op jit(solution)/shard_map/ppermute | solution.py:20
  222.1 2.2 collective-permute-done.15
  225.4 2.9 collective-permute-start.19
  229.4 5.7 %collective-permute-done.17 = bf16[2,128,512]{2,1,0:T(8,128)(2,1)S(1)} collective-permute-done((bf16[2,128,512]{2,1,0:T(8,128)(2,1)S(1)}, bf16[2,128,512]{2,1,0:T(8,128)(2,1)S(1)}, u32[]{:S(2)}, u32[]{:S(2)}) %collective-permute-start.17) | collective-permute-done | bytes 262176 | tf_op jit(solution)/shard_map/ppermute | solution.py:20
  238.1 6.5 %shard_map.116 = bf16[8,192,512]{2,1,0:T(8,128)(2,1)} custom-call(bf16[4,2,192,512]{3,2,1,0:T(8,128)(2,1)} %bitcast.50), custom_call_target="tpu_custom_call" | custom-call | flops 301989888 | bytes 3145728 | tf_op jit(solution)/shard_map/pallas_call | solution.py:333
  244.6 4.2 %all-to-all-start.1 = ((bf16[32,48,512]{2,1,0:T(8,128)(2,1)}), bf16[32,48,512]{2,1,0:T(8,128)(2,1)S(1)}, u32[]{:S(2)}, u32[]{:S(2)}) async-start(bf16[32,48,512]{2,1,0:T(8,128)(2,1)} %bitcast.46), calls=%async_computation.2 | async-start | bytes 3145728 | tf_op jit(solution)/shard_map/all_to_all | solution.py:383
  248.8 1.9 collective-permute-start.21
  252.1 2.1 collective-permute-start.22
  254.2 21.3 %collective-permute-done.21 = bf16[2,128,512]{2,1,0:T(8,128)(2,1)S(1)} collective-permute-done((bf16[2,128,512]{2,1,0:T(8,128)(2,1)S(1)}, bf16[2,128,512]{2,1,0:T(8,128)(2,1)S(1)}, u32[]{:S(2)}, u32[]{:S(2)}) %collective-permute-start.21) | collective-permute-done | bytes 262176 | tf_op jit(solution)/shard_map/ppermute | solution.py:20
  275.5 5.8 %collective-permute-done.22 = bf16[2,128,512]{2,1,0:T(8,128)(2,1)S(1)} collective-permute-done((bf16[2,128,512]{2,1,0:T(8,128)(2,1)S(1)}, bf16[2,128,512]{2,1,0:T(8,128)(2,1)S(1)}, u32[]{:S(2)}, u32[]{:S(2)}) %collective-permute-start.22) | collective-permute-done | bytes 262176 | tf_op jit(solution)/shard_map/ppermute | solution.py:20
  281.5 2.1 collective-permute-start.24
  285.8 2.5 collective-permute-done.24
  288.4 3.3 %collective-permute-done.25 = bf16[128,512]{1,0:T(8,128)(2,1)S(1)} collective-permute-done((bf16[128,512]{1,0:T(8,128)(2,1)S(1)}, bf16[128,512]{1,0:T(8,128)(2,1)S(1)}, u32[]{:S(2)}, u32[]{:S(2)}) %collective-permute-start.25) | collective-permute-done | bytes 131104 | tf_op jit(solution)/shard_map/ppermute | solution.py:20
  (117 shorter events, 40.1 us)
Async XLA Ops:
  7.2 101.5 %all-gather.3.cloned.1.call-start = ((), (), s32[]{:S(2)}) async-start(), calls=%async_computation.4 | async-start | bytes 9191424 | tf_op jit(solution)/shard_map/all_gather | solution.py:395
  9.2 10.4 %collective-permute-start.2 = (bf16[128,512]{1,0:T(8,128)(2,1)S(1)}, bf16[128,512]{1,0:T(8,128)(2,1)S(1)}, u32[]{:S(2)}, u32[]{:S(2)}) collective-permute-start(bf16[128,512]{1,0:T(8,128)(2,1)S(1)} %copy-done.17), channel_id=1, source_target_pairs={{3,0},{0,1},{1,2},{2,3},{7,4},{4,5},{5,6},{6,7},{11,8},{8,9},{9,10... | collective-permute-start | bytes 393224 | tf_op jit(solution)/shard_map/ppermute | solution.py:20
  10.8 8.8 %collective-permute-start.1 = (bf16[128,512]{1,0:T(8,128)(2,1)S(1)}, bf16[128,512]{1,0:T(8,128)(2,1)S(1)}, u32[]{:S(2)}, u32[]{:S(2)}) collective-permute-start(bf16[128,512]{1,0:T(8,128)(2,1)S(1)} %copy-done.17), channel_id=1, source_target_pairs={{2,0},{3,1},{0,2},{1,3},{6,4},{7,5},{4,6},{5,7},{10,8},{11,9},{8,1... | collective-permute-start | bytes 393224 | tf_op jit(solution)/shard_map/ppermute | solution.py:20
  13.5 5.5 %collective-permute-start = (bf16[128,512]{1,0:T(8,128)(2,1)S(1)}, bf16[128,512]{1,0:T(8,128)(2,1)S(1)}, u32[]{:S(2)}, u32[]{:S(2)}) collective-permute-start(bf16[128,512]{1,0:T(8,128)(2,1)S(1)} %copy-done.17), channel_id=1, source_target_pairs={{1,0},{2,1},{3,2},{0,3},{5,4},{6,5},{7,6},{4,7},{9,8},{10,9},{11,1... | collective-permute-start | bytes 393224 | tf_op jit(solution)/shard_map/ppermute | solution.py:20
  20.4 217.6 %reduce-scatter.2.cloned.1.call-start = ((), (), s32[]{:S(2)}) async-start(), calls=%async_computation.3 | async-start | bytes 7864320 | tf_op jit(solution)/shard_map/reduce_scatter | solution.py:406
  66.6 37.2 %collective-permute-start.4 = (bf16[4,2,192,512]{3,2,1,0:T(8,128)(2,1)}, bf16[4,2,192,512]{3,2,1,0:T(8,128)(2,1)S(1)}, u32[]{:S(2)}, u32[]{:S(2)}) collective-permute-start(bf16[4,2,192,512]{3,2,1,0:T(8,128)(2,1)} %shard_map.110.refs_0_), channel_id=1, source_target_pairs={{3,0},{0,1},{1,2},{2,3},{7,4},{4,5},{5,6},{6,7},{11,8},{8,9},{9,10... | collective-permute-start | bytes 4718600 | tf_op jit(solution)/shard_map/ppermute | solution.py:20
  68.0 36.1 %collective-permute-start.3 = (bf16[4,2,192,512]{3,2,1,0:T(8,128)(2,1)}, bf16[4,2,192,512]{3,2,1,0:T(8,128)(2,1)S(1)}, u32[]{:S(2)}, u32[]{:S(2)}) collective-permute-start(bf16[4,2,192,512]{3,2,1,0:T(8,128)(2,1)} %shard_map.110.refs_0_), channel_id=1, source_target_pairs={{1,0},{2,1},{3,2},{0,3},{5,4},{6,5},{7,6},{4,7},{9,8},{10,9},{11,1... | collective-permute-start | bytes 4718600 | tf_op jit(solution)/shard_map/ppermute | solution.py:20
  103.9 19.4 %collective-permute-start.5 = (bf16[2,2,192,512]{3,2,1,0:T(8,128)(2,1)S(1)}, bf16[2,2,192,512]{3,2,1,0:T(8,128)(2,1)S(1)}, u32[]{:S(2)}, u32[]{:S(2)}) collective-permute-start(bf16[2,2,192,512]{3,2,1,0:T(8,128)(2,1)S(1)} %slice.88), channel_id=1, source_target_pairs={{3,0},{0,1},{1,2},{2,3},{7,4},{4,5},{5,6},{6,7},{11,8},{8,9},{9,10... | collective-permute-start | bytes 2359304 | tf_op jit(solution)/shard_map/ppermute | solution.py:20
  106.4 18.3 %collective-permute-start.6 = (bf16[2,2,192,512]{3,2,1,0:T(8,128)(2,1)}, bf16[2,2,192,512]{3,2,1,0:T(8,128)(2,1)S(1)}, u32[]{:S(2)}, u32[]{:S(2)}) collective-permute-start(bf16[2,2,192,512]{3,2,1,0:T(8,128)(2,1)} %slice.89), channel_id=1, source_target_pairs={{1,0},{2,1},{3,2},{0,3},{5,4},{6,5},{7,6},{4,7},{9,8},{10,9},{11,1... | collective-permute-start | bytes 2359304 | tf_op jit(solution)/shard_map/ppermute | solution.py:20
  124.7 13.4 %collective-permute-start.7 = (bf16[4,192,2048]{2,1,0:T(8,128)(2,1)}, bf16[4,192,2048]{2,1,0:T(8,128)(2,1)S(1)}, u32[]{:S(2)}, u32[]{:S(2)}) collective-permute-start(bf16[4,192,2048]{2,1,0:T(8,128)(2,1)} %get-tuple-element.65), channel_id=1, source_target_pairs={{16,0},{0,16},{17,1},{1,17},{18,2},{2,18},{19,3},{3,19},{20,4},{4,... | collective-permute-start | bytes 9437192 | tf_op jit(solution)/shard_map/ppermute | solution.py:20
  155.0 6.0 %collective-permute-start.8 = (bf16[4,192,2048]{2,1,0:T(8,128)(2,1)}, bf16[4,192,2048]{2,1,0:T(8,128)(2,1)S(1)}, u32[]{:S(2)}, u32[]{:S(2)}) collective-permute-start(bf16[4,192,2048]{2,1,0:T(8,128)(2,1)} %get-tuple-element.73), channel_id=1, source_target_pairs={{16,0},{0,16},{17,1},{1,17},{18,2},{2,18},{19,3},{3,19},{20,4},{4,... | collective-permute-start | bytes 9437192 | tf_op jit(solution)/shard_map/ppermute | solution.py:20
  175.3 15.2 %collective-permute-start.9 = (bf16[2,2,128,512]{3,2,1,0:T(8,128)(2,1)S(1)}, bf16[2,2,128,512]{3,2,1,0:T(8,128)(2,1)S(1)}, u32[]{:S(2)}, u32[]{:S(2)}) collective-permute-start(bf16[2,2,128,512]{3,2,1,0:T(8,128)(2,1)S(1)} %get-tuple-element.78), channel_id=1, source_target_pairs={{96,0},{0,32},{32,64},{64,96},{97,1},{1,33},{33,65},{65,97},{98,2}... | collective-permute-start | bytes 1572872 | tf_op jit(solution)/shard_map/ppermute | solution.py:20
  177.0 13.8 %collective-permute-start.10 = (bf16[2,2,128,512]{3,2,1,0:T(8,128)(2,1)S(1)}, bf16[2,2,128,512]{3,2,1,0:T(8,128)(2,1)S(1)}, u32[]{:S(2)}, u32[]{:S(2)}) collective-permute-start(bf16[2,2,128,512]{3,2,1,0:T(8,128)(2,1)S(1)} %get-tuple-element.80), channel_id=1, source_target_pairs={{32,0},{64,32},{96,64},{0,96},{33,1},{65,33},{97,65},{1,97},{34,2}... | collective-permute-start | bytes 1572872 | tf_op jit(solution)/shard_map/ppermute | solution.py:20
  178.6 11.9 %copy-start.11 = (bf16[4,2,128,512]{3,2,1,0:T(8,128)(2,1)S(1)}, bf16[4,2,128,512]{3,2,1,0:T(8,128)(2,1)}, u32[]{:S(2)}) copy-start(bf16[4,2,128,512]{3,2,1,0:T(8,128)(2,1)} %get-tuple-element.77) | copy-start | bytes 3145732
  181.1 14.8 %collective-permute-start.11 = (bf16[2,2,128,512]{3,2,1,0:T(8,128)(2,1)S(1)}, bf16[2,2,128,512]{3,2,1,0:T(8,128)(2,1)S(1)}, u32[]{:S(2)}, u32[]{:S(2)}) collective-permute-start(bf16[2,2,128,512]{3,2,1,0:T(8,128)(2,1)S(1)} %get-tuple-element.83), channel_id=1, source_target_pairs={{12,0},{0,4},{4,8},{8,12},{13,1},{1,5},{5,9},{9,13},{14,2},{2,6},{... | collective-permute-start | bytes 1572872 | tf_op jit(solution)/shard_map/ppermute | solution.py:20
  183.6 13.1 %collective-permute-start.12 = (bf16[2,2,128,512]{3,2,1,0:T(8,128)(2,1)S(1)}, bf16[2,2,128,512]{3,2,1,0:T(8,128)(2,1)S(1)}, u32[]{:S(2)}, u32[]{:S(2)}) collective-permute-start(bf16[2,2,128,512]{3,2,1,0:T(8,128)(2,1)S(1)} %copy-done.22), channel_id=1, source_target_pairs={{4,0},{8,4},{12,8},{0,12},{5,1},{9,5},{13,9},{1,13},{6,2},{10,6},{... | collective-permute-start | bytes 1572872 | tf_op jit(solution)/shard_map/ppermute | solution.py:20
  196.9 24.8 %collective-permute-start.13 = (bf16[4,2,128,512]{3,2,1,0:T(8,128)(2,1)S(1)}, bf16[4,2,128,512]{3,2,1,0:T(8,128)(2,1)S(1)}, u32[]{:S(2)}, u32[]{:S(2)}) collective-permute-start(bf16[4,2,128,512]{3,2,1,0:T(8,128)(2,1)S(1)} %pad_maximum_fusion), channel_id=1, source_target_pairs={{96,0},{0,32},{32,64},{64,96},{97,1},{1,33},{33,65},{65,97},{98,2}... | collective-permute-start | bytes 3145736 | tf_op jit(solution)/shard_map/ppermute | solution.py:20
  197.0 24.7 %collective-permute-start.14 = (bf16[4,2,128,512]{3,2,1,0:T(8,128)(2,1)S(1)}, bf16[4,2,128,512]{3,2,1,0:T(8,128)(2,1)S(1)}, u32[]{:S(2)}, u32[]{:S(2)}) collective-permute-start(bf16[4,2,128,512]{3,2,1,0:T(8,128)(2,1)S(1)} %pad_maximum_fusion.1), channel_id=1, source_target_pairs={{32,0},{64,32},{96,64},{0,96},{33,1},{65,33},{97,65},{1,97},{34,2}... | collective-permute-start | bytes 3145736 | tf_op jit(solution)/shard_map/ppermute | solution.py:20
  200.2 24.2 %collective-permute-start.15 = (bf16[4,2,128,512]{3,2,1,0:T(8,128)(2,1)S(1)}, bf16[4,2,128,512]{3,2,1,0:T(8,128)(2,1)S(1)}, u32[]{:S(2)}, u32[]{:S(2)}) collective-permute-start(bf16[4,2,128,512]{3,2,1,0:T(8,128)(2,1)S(1)} %pad_maximum_fusion.2), channel_id=1, source_target_pairs={{12,0},{0,4},{4,8},{8,12},{13,1},{1,5},{5,9},{9,13},{14,2},{2,6},{... | collective-permute-start | bytes 3145736 | tf_op jit(solution)/shard_map/ppermute | solution.py:20
  200.8 23.6 %collective-permute-start.16 = (bf16[4,2,128,512]{3,2,1,0:T(8,128)(2,1)S(1)}, bf16[4,2,128,512]{3,2,1,0:T(8,128)(2,1)S(1)}, u32[]{:S(2)}, u32[]{:S(2)}) collective-permute-start(bf16[4,2,128,512]{3,2,1,0:T(8,128)(2,1)S(1)} %pad_maximum_fusion.3), channel_id=1, source_target_pairs={{4,0},{8,4},{12,8},{0,12},{5,1},{9,5},{13,9},{1,13},{6,2},{10,6},{... | collective-permute-start | bytes 3145736 | tf_op jit(solution)/shard_map/ppermute | solution.py:20
  203.4 18.3 %copy-start.13 = (bf16[4,2,128,512]{3,2,1,0:T(8,128)(2,1)S(1)}, bf16[4,2,128,512]{3,2,1,0:T(8,128)(2,1)}, u32[]{:S(2)}) copy-start(bf16[4,2,128,512]{3,2,1,0:T(8,128)(2,1)} %get-tuple-element.92) | copy-start | bytes 3145732
  224.9 10.2 %collective-permute-start.17 = (bf16[2,128,512]{2,1,0:T(8,128)(2,1)S(1)}, bf16[2,128,512]{2,1,0:T(8,128)(2,1)S(1)}, u32[]{:S(2)}, u32[]{:S(2)}) collective-permute-start(bf16[2,128,512]{2,1,0:T(8,128)(2,1)S(1)} %get-tuple-element.105), channel_id=1, source_target_pairs={{12,0},{0,4},{4,8},{8,12},{13,1},{1,5},{5,9},{9,13},{14,2},{2,6},{... | collective-permute-start | bytes 786440 | tf_op jit(solution)/shard_map/ppermute | solution.py:20
  225.4 11.0 %collective-permute-start.19 = (bf16[2,128,512]{2,1,0:T(8,128)(2,1)S(1)}, bf16[2,128,512]{2,1,0:T(8,128)(2,1)S(1)}, u32[]{:S(2)}, u32[]{:S(2)}) collective-permute-start(bf16[2,128,512]{2,1,0:T(8,128)(2,1)S(1)} %get-tuple-element.106), channel_id=1, source_target_pairs={{4,0},{8,4},{12,8},{0,12},{5,1},{9,5},{13,9},{1,13},{6,2},{10,6},{... | collective-permute-start | bytes 786440 | tf_op jit(solution)/shard_map/ppermute | solution.py:20
  228.2 9.7 %collective-permute-start.18 = (bf16[2,128,512]{2,1,0:T(8,128)(2,1)S(1)}, bf16[2,128,512]{2,1,0:T(8,128)(2,1)S(1)}, u32[]{:S(2)}, u32[]{:S(2)}) collective-permute-start(bf16[2,128,512]{2,1,0:T(8,128)(2,1)S(1)} %get-tuple-element.107), channel_id=1, source_target_pairs={{8,0},{12,4},{0,8},{4,12},{9,1},{13,5},{1,9},{5,13},{10,2},{14,6},... | collective-permute-start | bytes 786440 | tf_op jit(solution)/shard_map/ppermute | solution.py:20
  244.6 47.8 %all-to-all-start.1 = ((bf16[32,48,512]{2,1,0:T(8,128)(2,1)}), bf16[32,48,512]{2,1,0:T(8,128)(2,1)S(1)}, u32[]{:S(2)}, u32[]{:S(2)}) async-start(bf16[32,48,512]{2,1,0:T(8,128)(2,1)} %bitcast.46), calls=%async_computation.2 | async-start | bytes 3145728 | tf_op jit(solution)/shard_map/all_to_all | solution.py:383
  248.8 26.7 %collective-permute-start.21 = (bf16[2,128,512]{2,1,0:T(8,128)(2,1)S(1)}, bf16[2,128,512]{2,1,0:T(8,128)(2,1)S(1)}, u32[]{:S(2)}, u32[]{:S(2)}) collective-permute-start(bf16[2,128,512]{2,1,0:T(8,128)(2,1)S(1)} %get-tuple-element.108), channel_id=1, source_target_pairs={{96,0},{0,32},{32,64},{64,96},{97,1},{1,33},{33,65},{65,97},{98,2}... | collective-permute-start | bytes 786440 | tf_op jit(solution)/shard_map/ppermute | solution.py:20
  250.7 24.8 %collective-permute-start.23 = (bf16[2,128,512]{2,1,0:T(8,128)(2,1)S(1)}, bf16[2,128,512]{2,1,0:T(8,128)(2,1)S(1)}, u32[]{:S(2)}, u32[]{:S(2)}) collective-permute-start(bf16[2,128,512]{2,1,0:T(8,128)(2,1)S(1)} %get-tuple-element.109), channel_id=1, source_target_pairs={{32,0},{64,32},{96,64},{0,96},{33,1},{65,33},{97,65},{1,97},{34,2}... | collective-permute-start | bytes 786440 | tf_op jit(solution)/shard_map/ppermute | solution.py:20
  252.1 41.3 %copy-start.1 = (bf16[128,512]{1,0:T(8,128)(2,1)S(1)}, bf16[128,512]{1,0:T(8,128)(2,1)}, u32[]{:S(2)}) copy-start(bf16[128,512]{1,0:T(8,128)(2,1)} %param.7) | copy-start | bytes 393220
  252.1 29.2 %collective-permute-start.22 = (bf16[2,128,512]{2,1,0:T(8,128)(2,1)S(1)}, bf16[2,128,512]{2,1,0:T(8,128)(2,1)S(1)}, u32[]{:S(2)}, u32[]{:S(2)}) collective-permute-start(bf16[2,128,512]{2,1,0:T(8,128)(2,1)S(1)} %get-tuple-element.110), channel_id=1, source_target_pairs={{64,0},{96,32},{0,64},{32,96},{65,1},{97,33},{1,65},{33,97},{66,2}... | collective-permute-start | bytes 786440 | tf_op jit(solution)/shard_map/ppermute | solution.py:20
  281.5 6.9 %collective-permute-start.24 = (bf16[128,512]{1,0:T(8,128)(2,1)S(1)}, bf16[128,512]{1,0:T(8,128)(2,1)S(1)}, u32[]{:S(2)}, u32[]{:S(2)}) collective-permute-start(bf16[128,512]{1,0:T(8,128)(2,1)S(1)} %get-tuple-element.111), channel_id=1, source_target_pairs={{2,0},{3,1},{0,2},{1,3},{6,4},{7,5},{4,6},{5,7},{10,8},{11,9},{8,1... | collective-permute-start | bytes 393224 | tf_op jit(solution)/shard_map/ppermute | solution.py:20
  283.6 8.0 %collective-permute-start.25 = (bf16[128,512]{1,0:T(8,128)(2,1)S(1)}, bf16[128,512]{1,0:T(8,128)(2,1)S(1)}, u32[]{:S(2)}, u32[]{:S(2)}) collective-permute-start(bf16[128,512]{1,0:T(8,128)(2,1)S(1)} %get-tuple-element.112), channel_id=1, source_target_pairs={{1,0},{2,1},{3,2},{0,3},{5,4},{6,5},{7,6},{4,7},{9,8},{10,9},{11,1... | collective-permute-start | bytes 393224 | tf_op jit(solution)/shard_map/ppermute | solution.py:20
  285.0 6.6 %collective-permute-start.20 = (bf16[128,512]{1,0:T(8,128)(2,1)S(1)}, bf16[128,512]{1,0:T(8,128)(2,1)S(1)}, u32[]{:S(2)}, u32[]{:S(2)}) collective-permute-start(bf16[128,512]{1,0:T(8,128)(2,1)S(1)} %slice_bitcast_fusion.8), channel_id=1, source_target_pairs={{3,0},{0,1},{1,2},{2,3},{7,4},{4,5},{5,6},{6,7},{11,8},{8,9},{9,10... | collective-permute-start | bytes 393224 | tf_op jit(solution)/shard_map/ppermute | solution.py:20
  (20 other events, 77.5 us)
Sparse Core Ops, SparseCore 0:
  20.6 83.7 all-gather.2
  155.1 62.8 reduce-scatter.1

commit v3 on v1

--- a/solution.py
+++ b/solution.py
@@ -115,66 +115,109 @@
     )(ids, whole)
 
 
-def sum_kernel(ids_ref, map_ref, own_ref, sib_ref, *outs):
-    by_y, by_z = outs[:5], outs[5:]
+def gates_of(ids_ref, map_ref, which):
+    tok = 128
+    there = [pl.multiple_of(lax.rem(ids_ref[1] + zr, 4) * tok, tok) for zr in which]
+    return jnp.concatenate([map_ref[0, :, pl.ds(t, tok)] for t in there], axis=1)
+
+
+def rows_of(own_ref, sib_ref):
+    return jnp.concatenate(
+        [ref[e] for ref in (own_ref, sib_ref) for e in range(own_ref.shape[0])], axis=0
+    )
+
+
+def sum_far_kernel(
+    ids_ref, map_ref, own_ref, sib_ref, map2_ref, own2_ref, sib2_ref, y_lo, y_hi, z_lo, z_hi
+):
     yr = pl.program_id(0)
-    z = ids_ref[1]
-    n_exp = own_ref.shape[0]
-    tok, width = 128, own_ref.shape[2] // 4
-    there = [pl.multiple_of(lax.rem(z + zr, 4) * tok, tok) for zr in range(4)]
-    gates = jnp.concatenate([map_ref[0, :, pl.ds(t, tok)] for t in there], axis=1)
-    for r in range(4):
-        cols = slice(r * width, (r + 1) * width)
-        rows = [ref[e, :, cols] for ref in (own_ref, sib_ref) for e in range(n_exp)]
-        total = tn(gates, jnp.concatenate(rows, axis=0)).astype(BF)
-        for zr in range(4):
-            block = total[zr * tok : (zr + 1) * tok]
-            if r >= 2:
-                if zr != 2:
-                    by_z[(0, 1, None, 4)[zr]][0, r - 2] = block
-                for part in range(2 if zr == 2 else 0):
-
-                    @pl.when(yr // 2 == part)
-                    def _(part=part, block=block):
-                        by_z[2 + part][0, r - 2] = block
-
-                continue
-            dest = (by_y[0], by_y[1], by_y[2 + zr // 2], by_y[4])
-            for i in range(4):
-
-                @pl.when(yr == i)
-                def _(i=i, block=block):
-                    dest[i][zr % 2 if i == 2 else zr, r] = block
-
-
-def sum_tokens(ids, maps, own, sib):
+    tok, width = y_lo.shape[2:]
+    gates = gates_of(ids_ref, map_ref, (2,))
+    total = tn(gates, rows_of(own_ref, sib_ref)).astype(BF)
+    for part, ref in enumerate((z_lo, z_hi)):
+
+        @pl.when(yr // 2 == part)
+        def _(ref=ref):
+            ref[0, 0], ref[0, 1] = total[:, :width], total[:, width:]
+
+    @pl.when(yr == 0)
+    def _():
+        rows = rows_of(own2_ref, sib2_ref)
+        for part, ref in enumerate((y_lo, y_hi)):
+            gates = gates_of(ids_ref, map2_ref, (2 * part, 2 * part + 1))
+            total = tn(gates, rows).astype(BF)
+            for i in range(2):
+                for f in range(2):
+                    ref[i, f] = total[i * tok : (i + 1) * tok, f * width : (f + 1) * width]
+
+
+def sum_near_kernel(ids_ref, map_ref, own_ref, sib_ref, y0, y1, y3, z0, z1, z3):
+    yr = pl.program_id(0)
+    tok, width = y0.shape[2:]
+    rows = rows_of(own_ref, sib_ref)
+    near = tn(gates_of(ids_ref, map_ref, (0, 1, 3)), rows[:, 2 * width :]).astype(BF)
+    for i, ref in enumerate((z0, z1, z3)):
+        for f in range(2):
+            ref[0, f] = near[i * tok : (i + 1) * tok, f * width : (f + 1) * width]
+
+    @pl.when(yr != 2)
+    def _():
+        total = tn(gates_of(ids_ref, map_ref, range(4)), rows[:, : 2 * width]).astype(BF)
+        for i, ref in ((0, y0), (1, y1), (3, y3)):
+
+            @pl.when(yr == i)
+            def _(ref=ref):
+                for zr in range(4):
+                    for f in range(2):
+                        ref[zr, f] = total[zr * tok : (zr + 1) * tok, f * width : (f + 1) * width]
+
+
+def sum_tokens(ids, maps, own, sib, far):
     n_exp, rows, cols = own.shape
     whole = jax.ShapeDtypeStruct((4, 2, 128, cols // 4), BF)
     half = jax.ShapeDtypeStruct((2,) + whole.shape[1:], BF)
-    outs = (whole, whole, half, half, whole) * 2
     at = lambda i, ids: lax.rem(ids[0] + i, 4)
-    rows_spec = pl.BlockSpec((n_exp, rows // 4, cols), lambda i, ids: (0, at(i, ids), 0))
+    block = (1,) + whole.shape[1:]
     keep = lambda a: pl.BlockSpec(a.shape, lambda i, ids: (0,) * 4)
-    block = (1,) + whole.shape[1:]
     each_y = pl.BlockSpec(block, lambda i, ids: (i, 0, 0, 0))
     first = pl.BlockSpec(block, lambda i, ids: (jnp.minimum(i, 1), 0, 0, 0))
     last = pl.BlockSpec(block, lambda i, ids: (jnp.maximum(i - 2, 0), 0, 0, 0))
-    return pl.pallas_call(
-        sum_kernel,
-        grid_spec=pltpu.PrefetchScalarGridSpec(
-            num_scalar_prefetch=1,
-            grid=(4,),
-            in_specs=[
-                pl.BlockSpec((1,) + maps.shape[1:], lambda i, ids: (at(i, ids), 0, 0)),
-                rows_spec,
-                rows_spec,
-            ],
-            out_specs=tuple(keep(a) for a in outs[:5]) + (each_y, each_y, first, last, each_y),
-        ),
-        out_shape=outs,
-        compiler_params=pltpu.CompilerParams(vmem_limit_bytes=VMEM_LIMIT),
-        cost_estimate=pl.CostEstimate(flops=4 << 30, bytes_accessed=16 << 20, transcendentals=0),
-    )(ids, maps, own, sib)
+    one_map = (1,) + maps.shape[1:]
+    map_y = pl.BlockSpec(one_map, lambda i, ids: (at(i, ids), 0, 0))
+    map_2 = pl.BlockSpec(one_map, lambda i, ids: (at(2, ids), 0, 0))
+    rows_y = pl.BlockSpec((n_exp, rows // 4, cols), lambda i, ids: (0, at(i, ids), 0))
+    some = (n_exp, rows // 4, cols // 2)
+    rows_z = pl.BlockSpec(some, lambda i, ids: (0, at(i, ids), 1))
+    rows_2 = pl.BlockSpec(some, lambda i, ids: (0, at(2, ids), 0))
+
+    def call(kernel, in_specs, args, outs, out_specs, flops):
+        return pl.pallas_call(
+            kernel,
+            grid_spec=pltpu.PrefetchScalarGridSpec(
+                num_scalar_prefetch=1, grid=(4,), in_specs=in_specs, out_specs=out_specs
+            ),
+            out_shape=outs,
+            compiler_params=pltpu.CompilerParams(vmem_limit_bytes=VMEM_LIMIT),
+            cost_estimate=pl.CostEstimate(flops=flops, bytes_accessed=flops >> 8, transcendentals=0),
+        )(ids, *args)
+
+    if far:
+        return call(
+            sum_far_kernel,
+            [map_y, rows_z, rows_z, map_2, rows_2, rows_2],
+            (maps, own, sib) * 2,
+            (half,) * 4,
+            (keep(half), keep(half), first, last),
+            1 << 30,
+        )
+    return call(
+        sum_near_kernel,
+        [map_y, rows_y, rows_y],
+        (maps, own, sib),
+        (whole,) * 6,
+        (keep(whole),) * 3 + (each_y,) * 3,
+        3 << 30,
+    )
 
 
 def moved_columns(me, n, width):
@@ -362,22 +405,27 @@
     own, sib, maps = pick(ids, whole, n_exp)
     sib, out_sib = lax.optimization_barrier((sib, fetch(out_sib, "c", 1)))
 
-    sums = sum_tokens(ids, maps, out_own, out_sib)
-    sib, sums = lax.optimization_barrier((fetch(sib, "c", 1), sums))
-    ends_y, ends_z = collect_far(sums[:5], "y"), collect_far(sums[5:], "z")
+    far = sum_tokens(ids, maps, out_own, out_sib, True)
+    sib, far = lax.optimization_barrier((fetch(sib, "c", 1), far))
     g_blocks = (own, sib)
     mid = jax.ShapeDtypeStruct(hidden.shape, BF)
     grad_a, grad_b, back = backward(ids, g_blocks, slope, act, weights, mid, came.shape)
     back = lax.psum_scatter(back.reshape(-1, width), "x", scatter_dimension=0, tiled=True)
-    grad_a, ends_y, ends_z = lax.optimization_barrier((grad_a, ends_y, ends_z))
+
+    out_sib, grad_a = lax.optimization_barrier((out_sib, grad_a))
+    near = sum_tokens(ids, maps, out_own, out_sib, False)
+    ends_y = collect_far((near[0], near[1], far[0], far[1], near[2]), "y")
+    ends_z = collect_far((near[3], near[4], far[2], far[3], near[5]), "z")
+    hidden, ends_y, ends_z = lax.optimization_barrier((hidden, ends_y, ends_z))
     grads = weight_grads(ids, x_blocks, g_blocks, (hidden, grad_a, grad_b), w_gate)
     part1, part2 = collect_near(ends_y, "y"), collect_near(ends_z, "z")
     grads, part1, part2 = lax.optimization_barrier((grads, part1, part2))
     part1, part2 = collect_small(part1, "z"), collect_small(part2, "y")
-    mixed = collect_small((part1[0], part1[1], part2[0], part2[1]), "x")
-
+
+    back, part1, part2 = lax.optimization_barrier((back, part1, part2))
     back = back.reshape(n_exp, 2, 4, 4, CAP, width).transpose(2, 1, 3, 0, 4, 5)
     back = exchange(back.reshape(slots, width))
+    mixed = collect_small((part1[0], part1[1], part2[0], part2[1]), "x")
     grad_tokens = tn(own_map, back).astype(BF)
     return (mixed, grad_tokens) + tuple(grads)
 

time: 292 us -> 279 us (0.955)
  waiting for transfers between devices: 127 us -> 116 us
  starting transfers between devices: 52.3 us -> 47.4 us
  Pallas kernels: 59.6 us -> 64.3 us
    ppermute x26, waiting for transfers between devices: 108 us -> 97.5 us  [fetch(): return lax.ppermute(a, axis, [((i + r) % n, i) for i in range(n)])]
    reduce_scatter x1, waiting for transfers between devices: 9.47 us -> 0.02 us  [body(): lax.psum_scatter(back.reshape(-1, width), 'x', scatter_dimension=0, tiled...]
    all_to_all x2, waiting for transfers between devices: 10.1 us -> 18.6 us  [exchange(): return lax.all_to_all(a, GROUP, split_axis=0, concat_axis=0, tiled=True)]
    pallas_call x1 -> x2, Pallas kernels: 12.3 us -> 17.1 us  [call(): pl.pallas_call(kernel, grid_spec=pltpu.PrefetchScalarGridSpec(num_scalar_...]
    ppermute x26, starting transfers between devices: 36.3 us -> 32.7 us  [fetch(): return lax.ppermute(a, axis, [((i + r) % n, i) for i in range(n)])]
    unnamed x60 -> x52, local copies, waits for them, and re-layouts: 11.1 us -> 10.4 us
  transfers between devices with their start and end apart: 30 -> 30, of which waited for: 17 -> 19; matrix products, arithmetic and copies ran while one was open for 7% -> 5% of each run, Pallas kernels for 16% -> 18%
where the time goes in v3:
time: 279 us; the launch traced here: 277 us
  waiting for transfers between devices  116 us (42%)
  Pallas kernels  64.3 us (23%)
  starting transfers between devices  47.4 us (17%)
  local copies, waits for them, and re-layouts  26.8 us (10%)
  between operations  14.5 us (5%)
  other arithmetic  4.88 us (2%)
  matrix products  3.29 us (1%)
    ppermute x26, waiting for transfers between devices, fetch(): return lax.ppermute(a, axis, [((i + r) % n, i) for i in range(n)])  97.5 us
    pallas_call x3, Pallas kernels, per_expert(): pl.pallas_call(kernel, grid=(n_exp,), out_shape=outs, in_specs=[pl.BlockS...  35.7 us
    ppermute x26, starting transfers between devices, fetch(): return lax.ppermute(a, axis, [((i + r) % n, i) for i in range(n)])  32.7 us
    all_to_all x2, waiting for transfers between devices, exchange(): return lax.all_to_all(a, GROUP, split_axis=0, concat_axis=0, tiled=True)  18.6 us
    pallas_call x2, Pallas kernels, call(): pl.pallas_call(kernel, grid_spec=pltpu.PrefetchScalarGridSpec(num_scalar_...  17.1 us
    all_to_all x2, starting transfers between devices, exchange(): return lax.all_to_all(a, GROUP, split_axis=0, concat_axis=0, tiled=True)  14.7 us
    pallas_call x1, Pallas kernels, pick(): pl.pallas_call(pick_kernel, grid=(4,), out_shape=(rows, rows, maps), in_s...  11.5 us
    unnamed x52, local copies, waits for them, and re-layouts  10.4 us
  transfers between devices with their start and end apart: 30, of which 19 were waited for; matrix products, arithmetic and copies ran while one was open for 5% of the time, Pallas kernels for 18%

profile of v3, /device:TPU:0, one launch (start us, length us, event | category | flops | bytes accessed | tf_op | source)
XLA Modules:
  0.0 277.3 jit_solution(7708620500804665091)
XLA Ops:
  10.2 8.5 %all-to-all-start = ((bf16[32,48,512]{2,1,0:T(8,128)(2,1)}), bf16[32,48,512]{2,1,0:T(8,128)(2,1)S(1)}, u32[]{:S(2)}, u32[]{:S(2)}) async-start(bf16[32,48,512]{2,1,0:T(8,128)(2,1)} %bitcast.5), calls=%async_computation | async-start | bytes 3145728 | tf_op jit(solution)/shard_map/all_to_all | solution.py:387
  18.8 2.8 %collective-permute-start = (bf16[128,512]{1,0:T(8,128)(2,1)S(1)}, bf16[128,512]{1,0:T(8,128)(2,1)S(1)}, u32[]{:S(2)}, u32[]{:S(2)}) collective-permute-start(bf16[128,512]{1,0:T(8,128)(2,1)S(1)} %copy-done.19), channel_id=1, source_target_pairs={{1,0},{2,1},{3,2},{0,3},{5,4},{6,5},{7,6},{4,7},{9,8},{10,9},{11,1... | collective-permute-start | bytes 393224 | tf_op jit(solution)/shard_map/ppermute | solution.py:20
  23.4 4.3 %collective-permute-done = bf16[128,512]{1,0:T(8,128)(2,1)S(1)} collective-permute-done((bf16[128,512]{1,0:T(8,128)(2,1)S(1)}, bf16[128,512]{1,0:T(8,128)(2,1)S(1)}, u32[]{:S(2)}, u32[]{:S(2)}) %collective-permute-start) | collective-permute-done | bytes 131104 | tf_op jit(solution)/shard_map/ppermute | solution.py:20
  27.7 1.8 collective-permute-done.1
  31.4 10.1 %all-to-all-done = bf16[32,48,512]{2,1,0:T(8,128)(2,1)S(1)} async-done(((bf16[32,48,512]{2,1,0:T(8,128)(2,1)}), bf16[32,48,512]{2,1,0:T(8,128)(2,1)S(1)}, u32[]{:S(2)}, u32[]{:S(2)}) %all-to-all-start) | async-done | bytes 1572896 | tf_op jit(solution)/shard_map/all_to_all | solution.py:387
  42.6 2.4 reshape.65
  50.2 33.3 %collective-permute-done.4.refs_4_ = bf16[4,2,192,512]{3,2,1,0:T(8,128)(2,1)S(1)} collective-permute-done((bf16[4,2,192,512]{3,2,1,0:T(8,128)(2,1)S(1)}, bf16[4,2,192,512]{3,2,1,0:T(8,128)(2,1)S(1)}, u32[]{:S(2)}, u32[]{:S(2)}) %collective-permute-start.4) | collective-permute-done | bytes 1572896 | tf_op jit(solution)/shard_map/ppermute | solution.py:20
  86.5 2.7 collective-permute-start.6
  89.3 14.4 %collective-permute-done.5.refs_2_ = bf16[2,2,192,512]{3,2,1,0:T(8,128)(2,1)S(1)} collective-permute-done((bf16[2,2,192,512]{3,2,1,0:T(8,128)(2,1)}, bf16[2,2,192,512]{3,2,1,0:T(8,128)(2,1)S(1)}, u32[]{:S(2)}, u32[]{:S(2)}) %collective-permute-start.5) | collective-permute-done | bytes 786464 | tf_op jit(solution)/shard_map/ppermute | solution.py:20
  105.3 11.4 %shard_map.110 = (bf16[4,192,2048]{2,1,0:T(8,128)(2,1)}, bf16[4,192,2048]{2,1,0:T(8,128)(2,1)}, bf16[4,384,192]{2,1,0:T(8,128)(2,1)S(1)}, f32[4,384,192]{2,1,0:T(8,128)}, f32[4,384,192]{2,1,0:T(8,128)}) custom-call(s32[4]{0:T(128)S(1)} %pad_add_fusion.ids_ref, bf16[4,2,192,512]{3,2,1,0:T(8,128)(2,1)} %copy-done.10, bf16[4,2,192,512]{3,2,1,0:T(8,128)(2,1)} %copy-done.18, ...), custom_call_target="tpu_custom_call" | custom-call | flops 5435817984 | bytes 27262976 | tf_op jit(solution)/shard_map/pallas_call | solution.py:303
  117.7 11.5 %shard_map.111 = (bf16[4,192,2048]{2,1,0:T(8,128)(2,1)}, bf16[4,192,2048]{2,1,0:T(8,128)(2,1)}, bf16[4,384,512]{2,1,0:T(8,128)(2,1)S(1)}) custom-call(s32[4]{0:T(128)S(1)} %pad_add_fusion.ids_ref, bf16[16,528,512]{2,1,0:T(8,128)(2,1)} %bitcast.54), custom_call_target="tpu_custom_call" | custom-call | flops 4294967296 | bytes 18874368 | tf_op jit(solution)/shard_map/pallas_call | solution.py:104
  132.0 6.3 %shard_map.112 = (bf16[2,2,128,512]{3,2,1,0:T(8,128)(2,1)S(1)}, bf16[2,2,128,512]{3,2,1,0:T(8,128)(2,1)S(1)}, bf16[2,2,128,512]{3,2,1,0:T(8,128)(2,1)S(1)}, bf16[2,2,128,512]{3,2,1,0:T(8,128)(2,1)}) custom-call(s32[4]{0:T(128)S(1)} %pad_add_fusion.ids_ref, bf16[4,384,512]{2,1,0:T(8,128)(2,1)} %copy-done.2, ...), custom_call_target="tpu_custom_call" | custom-call | flops 1073741824 | bytes 4194304 | tf_op jit(solution)/shard_map/pallas_call | solution.py:194
  139.9 13.5 %shard_map.113 = (bf16[4,384,192]{2,1,0:T(8,128)(2,1)S(1)}, bf16[4,384,192]{2,1,0:T(8,128)(2,1)S(1)}, bf16[4,4,2,192,512]{4,3,2,1,0:T(8,128)(2,1)}) custom-call(s32[4]{0:T(128)S(1)} %pad_add_fusion.ids_ref, bf16[4,192,2048]{2,1,0:T(8,128)(2,1)} %get-tuple-element.61.own.refs_5_, bf16[4,192,2048]{2,1,0:T(8,128)(2,1)} %copy-done.22, ...), custom_call_target="tpu_custom_call" | custom-call | flops 5435817984 | bytes 27262976 | tf_op jit(solution)/shard_map/pallas_call | solution.py:303
  156.6 1.9 collective-permute-start.10
  158.5 10.8 %shard_map.114 = (bf16[4,2,128,512]{3,2,1,0:T(8,128)(2,1)S(1)}, bf16[4,2,128,512]{3,2,1,0:T(8,128)(2,1)}, bf16[4,2,128,512]{3,2,1,0:T(8,128)(2,1)}, bf16[4,2,128...) custom-call(s32[4]{0:T(128)S(1)} %pad_add_fusion.ids_ref, ...), custom_call_target="tpu_custom_call" | custom-call | flops 3221225472 | bytes 12582912 | tf_op jit(solution)/shard_map/pallas_call | solution.py:194
  173.0 2.1 collective-permute-start.12
  176.5 10.2 %collective-permute-done.11 = bf16[2,2,128,512]{3,2,1,0:T(8,128)(2,1)S(1)} collective-permute-done((bf16[2,2,128,512]{3,2,1,0:T(8,128)(2,1)S(1)}, bf16[2,2,128,512]{3,2,1,0:T(8,128)(2,1)S(1)}, u32[]{:S(2)}, u32[]{:S(2)}) %collective-permute-start.11) | collective-permute-done | bytes 524320 | tf_op jit(solution)/shard_map/ppermute | solution.py:20
  187.4 1.9 collective-permute-start.13
  189.4 2.7 collective-permute-start.16
  192.1 10.8 %shard_map.115 = (bf16[4,192,2048]{2,1,0:T(8,128)(2,1)}, bf16[4,192,2048]{2,1,0:T(8,128)(2,1)}, bf16[4,192,2048]{2,1,0:T(8,128)(2,1)}) custom-call(s32[4]{0:T(128)S(1)} %pad_add_fusion.ids_ref, bf16[4,2,192,512]{3,2,1,0:T(8,128)(2,1)} %copy-done.10, bf16[4,2,192,512]{3,2,1,0:T(8,128)(2,1)} %copy-done.18, ...), custom_call_target="tpu_custom_call" | custom-call | flops 5435817984 | bytes 25165824 | tf_op jit(solution)/shard_map/pallas_call | solution.py:303
  202.9 8.7 %collective-permute-done.14 = bf16[4,2,128,512]{3,2,1,0:T(8,128)(2,1)S(1)} collective-permute-done((bf16[4,2,128,512]{3,2,1,0:T(8,128)(2,1)S(1)}, bf16[4,2,128,512]{3,2,1,0:T(8,128)(2,1)S(1)}, u32[]{:S(2)}, u32[]{:S(2)}) %collective-permute-start.14) | collective-permute-done | bytes 1048608 | tf_op jit(solution)/shard_map/ppermute | solution.py:20
  221.5 3.7 %collective-permute-done.19 = bf16[2,128,512]{2,1,0:T(8,128)(2,1)S(1)} collective-permute-done((bf16[2,128,512]{2,1,0:T(8,128)(2,1)S(1)}, bf16[2,128,512]{2,1,0:T(8,128)(2,1)S(1)}, u32[]{:S(2)}, u32[]{:S(2)}) %collective-permute-start.19) | collective-permute-done | bytes 262176 | tf_op jit(solution)/shard_map/ppermute | solution.py:20
  225.7 2.2 collective-permute-done.18
  227.9 2.4 collective-permute-done.17
  230.5 2.2 collective-permute-done.20
  232.9 2.4 reshape.68
  236.9 3.7 %reshape.73 = bf16[32,48,512]{2,1,0:T(8,128)(2,1)} reshape(bf16[4,2,4,4,12,512]{5,4,3,2,1,0:T(8,128)(2,1)} %copy.39) | data formatting | bytes 3145728 | tf_op jit(solution)/shard_map/all_to_all | solution.py:387
  240.5 6.1 %all-to-all-start.1 = ((bf16[32,48,512]{2,1,0:T(8,128)(2,1)}), bf16[32,48,512]{2,1,0:T(8,128)(2,1)S(1)}, u32[]{:S(2)}, u32[]{:S(2)}) async-start(bf16[32,48,512]{2,1,0:T(8,128)(2,1)} %reshape.73), calls=%async_computation.2 | async-start | bytes 3145728 | tf_op jit(solution)/shard_map/all_to_all | solution.py:387
  246.7 3.9 %collective-permute-start.25 = (bf16[128,512]{1,0:T(8,128)(2,1)S(1)}, bf16[128,512]{1,0:T(8,128)(2,1)S(1)}, u32[]{:S(2)}, u32[]{:S(2)}) collective-permute-start(bf16[128,512]{1,0:T(8,128)(2,1)S(1)} %get-tuple-element.116), channel_id=1, source_target_pairs={{1,0},{2,1},{3,2},{0,3},{5,4},{6,5},{7,6},{4,7},{9,8},{10,9},{11,1... | collective-permute-start | bytes 393224 | tf_op jit(solution)/shard_map/ppermute | solution.py:20
  251.6 5.0 %collective-permute-done.25 = bf16[128,512]{1,0:T(8,128)(2,1)S(1)} collective-permute-done((bf16[128,512]{1,0:T(8,128)(2,1)S(1)}, bf16[128,512]{1,0:T(8,128)(2,1)S(1)}, u32[]{:S(2)}, u32[]{:S(2)}) %collective-permute-start.25) | collective-permute-done | bytes 131104 | tf_op jit(solution)/shard_map/ppermute | solution.py:20
  256.6 1.9 collective-permute-done.24
  260.8 8.5 %all-to-all-done.1 = bf16[32,48,512]{2,1,0:T(8,128)(2,1)S(1)} async-done(((bf16[32,48,512]{2,1,0:T(8,128)(2,1)}), bf16[32,48,512]{2,1,0:T(8,128)(2,1)S(1)}, u32[]{:S(2)}, u32[]{:S(2)}) %all-to-all-start.1) | async-done | bytes 1572896 | tf_op jit(solution)/shard_map/all_to_all | solution.py:387
  (125 shorter events, 48.7 us)
Async XLA Ops:
  10.2 31.3 %all-to-all-start = ((bf16[32,48,512]{2,1,0:T(8,128)(2,1)}), bf16[32,48,512]{2,1,0:T(8,128)(2,1)S(1)}, u32[]{:S(2)}, u32[]{:S(2)}) async-start(bf16[32,48,512]{2,1,0:T(8,128)(2,1)} %bitcast.5), calls=%async_computation | async-start | bytes 3145728 | tf_op jit(solution)/shard_map/all_to_all | solution.py:387
  18.8 98.9 %all-gather.3.cloned.1.call-start = ((), (), s32[]{:S(2)}) async-start(), calls=%async_computation.4 | async-start | bytes 9191424 | tf_op jit(solution)/shard_map/all_gather | solution.py:395
  18.8 8.9 %collective-permute-start = (bf16[128,512]{1,0:T(8,128)(2,1)S(1)}, bf16[128,512]{1,0:T(8,128)(2,1)S(1)}, u32[]{:S(2)}, u32[]{:S(2)}) collective-permute-start(bf16[128,512]{1,0:T(8,128)(2,1)S(1)} %copy-done.19), channel_id=1, source_target_pairs={{1,0},{2,1},{3,2},{0,3},{5,4},{6,5},{7,6},{4,7},{9,8},{10,9},{11,1... | collective-permute-start | bytes 393224 | tf_op jit(solution)/shard_map/ppermute | solution.py:20
  21.7 7.9 %collective-permute-start.1 = (bf16[128,512]{1,0:T(8,128)(2,1)S(1)}, bf16[128,512]{1,0:T(8,128)(2,1)S(1)}, u32[]{:S(2)}, u32[]{:S(2)}) collective-permute-start(bf16[128,512]{1,0:T(8,128)(2,1)S(1)} %copy-done.19), channel_id=1, source_target_pairs={{2,0},{3,1},{0,2},{1,3},{6,4},{7,5},{4,6},{5,7},{10,8},{11,9},{8,1... | collective-permute-start | bytes 393224 | tf_op jit(solution)/shard_map/ppermute | solution.py:20
  22.5 8.9 %collective-permute-start.2 = (bf16[128,512]{1,0:T(8,128)(2,1)S(1)}, bf16[128,512]{1,0:T(8,128)(2,1)S(1)}, u32[]{:S(2)}, u32[]{:S(2)}) collective-permute-start(bf16[128,512]{1,0:T(8,128)(2,1)S(1)} %copy-done.19), channel_id=1, source_target_pairs={{3,0},{0,1},{1,2},{2,3},{7,4},{4,5},{5,6},{6,7},{11,8},{8,9},{9,10... | collective-permute-start | bytes 393224 | tf_op jit(solution)/shard_map/ppermute | solution.py:20
  42.6 190.2 %reduce-scatter.2.cloned.1.call-start = ((), (), s32[]{:S(2)}) async-start(), calls=%async_computation.3 | async-start | bytes 7864320 | tf_op jit(solution)/shard_map/reduce_scatter | solution.py:413
  46.9 57.5 %copy-start.10 = (bf16[4,2,192,512]{3,2,1,0:T(8,128)(2,1)}, bf16[4,2,192,512]{3,2,1,0:T(8,128)(2,1)S(1)}, u32[]{:S(2)}) copy-start(bf16[4,2,192,512]{3,2,1,0:T(8,128)(2,1)S(1)} %copy.35.refs_0_) | copy-start | bytes 4718596
  46.9 36.6 %collective-permute-start.4 = (bf16[4,2,192,512]{3,2,1,0:T(8,128)(2,1)S(1)}, bf16[4,2,192,512]{3,2,1,0:T(8,128)(2,1)S(1)}, u32[]{:S(2)}, u32[]{:S(2)}) collective-permute-start(bf16[4,2,192,512]{3,2,1,0:T(8,128)(2,1)S(1)} %copy.35.refs_0_), channel_id=1, source_target_pairs={{3,0},{0,1},{1,2},{2,3},{7,4},{4,5},{5,6},{6,7},{11,8},{8,9},{9,10... | collective-permute-start | bytes 4718600 | tf_op jit(solution)/shard_map/ppermute | solution.py:20
  48.5 36.3 %collective-permute-start.3 = (bf16[4,2,192,512]{3,2,1,0:T(8,128)(2,1)S(1)}, bf16[4,2,192,512]{3,2,1,0:T(8,128)(2,1)S(1)}, u32[]{:S(2)}, u32[]{:S(2)}) collective-permute-start(bf16[4,2,192,512]{3,2,1,0:T(8,128)(2,1)S(1)} %copy.35.refs_0_), channel_id=1, source_target_pairs={{1,0},{2,1},{3,2},{0,3},{5,4},{6,5},{7,6},{4,7},{9,8},{10,9},{11,1... | collective-permute-start | bytes 4718600 | tf_op jit(solution)/shard_map/ppermute | solution.py:20
  84.5 19.1 %collective-permute-start.5 = (bf16[2,2,192,512]{3,2,1,0:T(8,128)(2,1)}, bf16[2,2,192,512]{3,2,1,0:T(8,128)(2,1)S(1)}, u32[]{:S(2)}, u32[]{:S(2)}) collective-permute-start(bf16[2,2,192,512]{3,2,1,0:T(8,128)(2,1)} %slice.88), channel_id=1, source_target_pairs={{3,0},{0,1},{1,2},{2,3},{7,4},{4,5},{5,6},{6,7},{11,8},{8,9},{9,10... | collective-permute-start | bytes 2359304 | tf_op jit(solution)/shard_map/ppermute | solution.py:20
  86.5 17.9 %collective-permute-start.6 = (bf16[2,2,192,512]{3,2,1,0:T(8,128)(2,1)}, bf16[2,2,192,512]{3,2,1,0:T(8,128)(2,1)S(1)}, u32[]{:S(2)}, u32[]{:S(2)}) collective-permute-start(bf16[2,2,192,512]{3,2,1,0:T(8,128)(2,1)} %slice.89), channel_id=1, source_target_pairs={{1,0},{2,1},{3,2},{0,3},{5,4},{6,5},{7,6},{4,7},{9,8},{10,9},{11,1... | collective-permute-start | bytes 2359304 | tf_op jit(solution)/shard_map/ppermute | solution.py:20
  117.7 12.6 %collective-permute-start.7 = (bf16[4,192,2048]{2,1,0:T(8,128)(2,1)}, bf16[4,192,2048]{2,1,0:T(8,128)(2,1)S(1)}, u32[]{:S(2)}, u32[]{:S(2)}) collective-permute-start(bf16[4,192,2048]{2,1,0:T(8,128)(2,1)} %get-tuple-element.63), channel_id=1, source_target_pairs={{16,0},{0,16},{17,1},{1,17},{18,2},{2,18},{19,3},{3,19},{20,4},{4,... | collective-permute-start | bytes 9437192 | tf_op jit(solution)/shard_map/ppermute | solution.py:20
  130.3 8.0 %collective-permute-start.8 = (bf16[4,192,2048]{2,1,0:T(8,128)(2,1)}, bf16[4,192,2048]{2,1,0:T(8,128)(2,1)S(1)}, u32[]{:S(2)}, u32[]{:S(2)}) collective-permute-start(bf16[4,192,2048]{2,1,0:T(8,128)(2,1)} %get-tuple-element.64), channel_id=1, source_target_pairs={{16,0},{0,16},{17,1},{1,17},{18,2},{2,18},{19,3},{3,19},{20,4},{4,... | collective-permute-start | bytes 9437192 | tf_op jit(solution)/shard_map/ppermute | solution.py:20
  155.2 19.9 %collective-permute-start.9 = (bf16[2,2,128,512]{3,2,1,0:T(8,128)(2,1)S(1)}, bf16[2,2,128,512]{3,2,1,0:T(8,128)(2,1)S(1)}, u32[]{:S(2)}, u32[]{:S(2)}) collective-permute-start(bf16[2,2,128,512]{3,2,1,0:T(8,128)(2,1)S(1)} %get-tuple-element.81), channel_id=1, source_target_pairs={{96,0},{0,32},{32,64},{64,96},{97,1},{1,33},{33,65},{65,97},{98,2}... | collective-permute-start | bytes 1572872 | tf_op jit(solution)/shard_map/ppermute | solution.py:20
  156.6 18.7 %collective-permute-start.10 = (bf16[2,2,128,512]{3,2,1,0:T(8,128)(2,1)S(1)}, bf16[2,2,128,512]{3,2,1,0:T(8,128)(2,1)S(1)}, u32[]{:S(2)}, u32[]{:S(2)}) collective-permute-start(bf16[2,2,128,512]{3,2,1,0:T(8,128)(2,1)S(1)} %get-tuple-element.83), channel_id=1, source_target_pairs={{32,0},{64,32},{96,64},{0,96},{33,1},{65,33},{97,65},{1,97},{34,2}... | collective-permute-start | bytes 1572872 | tf_op jit(solution)/shard_map/ppermute | solution.py:20
  171.7 15.0 %collective-permute-start.11 = (bf16[2,2,128,512]{3,2,1,0:T(8,128)(2,1)S(1)}, bf16[2,2,128,512]{3,2,1,0:T(8,128)(2,1)S(1)}, u32[]{:S(2)}, u32[]{:S(2)}) collective-permute-start(bf16[2,2,128,512]{3,2,1,0:T(8,128)(2,1)S(1)} %get-tuple-element.86), channel_id=1, source_target_pairs={{12,0},{0,4},{4,8},{8,12},{13,1},{1,5},{5,9},{9,13},{14,2},{2,6},{... | collective-permute-start | bytes 1572872 | tf_op jit(solution)/shard_map/ppermute | solution.py:20
  173.0 14.1 %collective-permute-start.12 = (bf16[2,2,128,512]{3,2,1,0:T(8,128)(2,1)S(1)}, bf16[2,2,128,512]{3,2,1,0:T(8,128)(2,1)S(1)}, u32[]{:S(2)}, u32[]{:S(2)}) collective-permute-start(bf16[2,2,128,512]{3,2,1,0:T(8,128)(2,1)S(1)} %copy-done.23), channel_id=1, source_target_pairs={{4,0},{8,4},{12,8},{0,12},{5,1},{9,5},{13,9},{1,13},{6,2},{10,6},{... | collective-permute-start | bytes 1572872 | tf_op jit(solution)/shard_map/ppermute | solution.py:20
  187.3 24.3 %collective-permute-start.14 = (bf16[4,2,128,512]{3,2,1,0:T(8,128)(2,1)S(1)}, bf16[4,2,128,512]{3,2,1,0:T(8,128)(2,1)S(1)}, u32[]{:S(2)}, u32[]{:S(2)}) collective-permute-start(bf16[4,2,128,512]{3,2,1,0:T(8,128)(2,1)S(1)} %pad_maximum_fusion.1), channel_id=1, source_target_pairs={{32,0},{64,32},{96,64},{0,96},{33,1},{65,33},{97,65},{1,97},{34,2}... | collective-permute-start | bytes 3145736 | tf_op jit(solution)/shard_map/ppermute | solution.py:20
  187.4 25.5 %collective-permute-start.13 = (bf16[4,2,128,512]{3,2,1,0:T(8,128)(2,1)S(1)}, bf16[4,2,128,512]{3,2,1,0:T(8,128)(2,1)}, u32[]{:S(2)}, u32[]{:S(2)}) collective-permute-start(bf16[4,2,128,512]{3,2,1,0:T(8,128)(2,1)S(1)} %pad_maximum_fusion), channel_id=1, source_target_pairs={{96,0},{0,32},{32,64},{64,96},{97,1},{1,33},{33,65},{65,97},{98,2}... | collective-permute-start | bytes 3145736 | tf_op jit(solution)/shard_map/ppermute | solution.py:20
  189.4 25.3 %collective-permute-start.16 = (bf16[4,2,128,512]{3,2,1,0:T(8,128)(2,1)S(1)}, bf16[4,2,128,512]{3,2,1,0:T(8,128)(2,1)S(1)}, u32[]{:S(2)}, u32[]{:S(2)}) collective-permute-start(bf16[4,2,128,512]{3,2,1,0:T(8,128)(2,1)S(1)} %pad_maximum_fusion.3), channel_id=1, source_target_pairs={{4,0},{8,4},{12,8},{0,12},{5,1},{9,5},{13,9},{1,13},{6,2},{10,6},{... | collective-permute-start | bytes 3145736 | tf_op jit(solution)/shard_map/ppermute | solution.py:20
  192.1 24.3 %collective-permute-start.15 = (bf16[4,2,128,512]{3,2,1,0:T(8,128)(2,1)S(1)}, bf16[4,2,128,512]{3,2,1,0:T(8,128)(2,1)S(1)}, u32[]{:S(2)}, u32[]{:S(2)}) collective-permute-start(bf16[4,2,128,512]{3,2,1,0:T(8,128)(2,1)S(1)} %pad_maximum_fusion.2), channel_id=1, source_target_pairs={{12,0},{0,4},{4,8},{8,12},{13,1},{1,5},{5,9},{9,13},{14,2},{2,6},{... | collective-permute-start | bytes 3145736 | tf_op jit(solution)/shard_map/ppermute | solution.py:20
  216.9 8.3 %collective-permute-start.19 = (bf16[2,128,512]{2,1,0:T(8,128)(2,1)S(1)}, bf16[2,128,512]{2,1,0:T(8,128)(2,1)S(1)}, u32[]{:S(2)}, u32[]{:S(2)}) collective-permute-start(bf16[2,128,512]{2,1,0:T(8,128)(2,1)S(1)} %get-tuple-element.113), channel_id=1, source_target_pairs={{4,0},{8,4},{12,8},{0,12},{5,1},{9,5},{13,9},{1,13},{6,2},{10,6},{... | collective-permute-start | bytes 786440 | tf_op jit(solution)/shard_map/ppermute | solution.py:20
  217.6 10.3 %collective-permute-start.18 = (bf16[2,128,512]{2,1,0:T(8,128)(2,1)S(1)}, bf16[2,128,512]{2,1,0:T(8,128)(2,1)S(1)}, u32[]{:S(2)}, u32[]{:S(2)}) collective-permute-start(bf16[2,128,512]{2,1,0:T(8,128)(2,1)S(1)} %get-tuple-element.114), channel_id=1, source_target_pairs={{8,0},{12,4},{0,8},{4,12},{9,1},{13,5},{1,9},{5,13},{10,2},{14,6},... | collective-permute-start | bytes 786440 | tf_op jit(solution)/shard_map/ppermute | solution.py:20
  218.1 12.3 %collective-permute-start.17 = (bf16[2,128,512]{2,1,0:T(8,128)(2,1)S(1)}, bf16[2,128,512]{2,1,0:T(8,128)(2,1)S(1)}, u32[]{:S(2)}, u32[]{:S(2)}) collective-permute-start(bf16[2,128,512]{2,1,0:T(8,128)(2,1)S(1)} %get-tuple-element.112), channel_id=1, source_target_pairs={{12,0},{0,4},{4,8},{8,12},{13,1},{1,5},{5,9},{9,13},{14,2},{2,6},{... | collective-permute-start | bytes 786440 | tf_op jit(solution)/shard_map/ppermute | solution.py:20
  219.0 11.5 %collective-permute-start.22 = (bf16[2,128,512]{2,1,0:T(8,128)(2,1)S(1)}, bf16[2,128,512]{2,1,0:T(8,128)(2,1)S(1)}, u32[]{:S(2)}, u32[]{:S(2)}) collective-permute-start(bf16[2,128,512]{2,1,0:T(8,128)(2,1)S(1)} %get-tuple-element.110), channel_id=1, source_target_pairs={{32,0},{64,32},{96,64},{0,96},{33,1},{65,33},{97,65},{1,97},{34,2}... | collective-permute-start | bytes 786440 | tf_op jit(solution)/shard_map/ppermute | solution.py:20
  220.7 9.8 %collective-permute-start.21 = (bf16[2,128,512]{2,1,0:T(8,128)(2,1)S(1)}, bf16[2,128,512]{2,1,0:T(8,128)(2,1)S(1)}, u32[]{:S(2)}, u32[]{:S(2)}) collective-permute-start(bf16[2,128,512]{2,1,0:T(8,128)(2,1)S(1)} %get-tuple-element.111), channel_id=1, source_target_pairs={{64,0},{96,32},{0,64},{32,96},{65,1},{97,33},{1,65},{33,97},{66,2}... | collective-permute-start | bytes 786440 | tf_op jit(solution)/shard_map/ppermute | solution.py:20
  225.1 7.6 %collective-permute-start.20 = (bf16[2,128,512]{2,1,0:T(8,128)(2,1)S(1)}, bf16[2,128,512]{2,1,0:T(8,128)(2,1)S(1)}, u32[]{:S(2)}, u32[]{:S(2)}) collective-permute-start(bf16[2,128,512]{2,1,0:T(8,128)(2,1)S(1)} %get-tuple-element.109), channel_id=1, source_target_pairs={{96,0},{0,32},{32,64},{64,96},{97,1},{1,33},{33,65},{65,97},{98,2}... | collective-permute-start | bytes 786440 | tf_op jit(solution)/shard_map/ppermute | solution.py:20
  240.5 28.8 %all-to-all-start.1 = ((bf16[32,48,512]{2,1,0:T(8,128)(2,1)}), bf16[32,48,512]{2,1,0:T(8,128)(2,1)S(1)}, u32[]{:S(2)}, u32[]{:S(2)}) async-start(bf16[32,48,512]{2,1,0:T(8,128)(2,1)} %reshape.73), calls=%async_computation.2 | async-start | bytes 3145728 | tf_op jit(solution)/shard_map/all_to_all | solution.py:387
  246.6 23.8 %copy-start.1 = (bf16[128,512]{1,0:T(8,128)(2,1)S(1)}, bf16[128,512]{1,0:T(8,128)(2,1)}, u32[]{:S(2)}) copy-start(bf16[128,512]{1,0:T(8,128)(2,1)} %param.7) | copy-start | bytes 393220
  246.7 9.9 %collective-permute-start.25 = (bf16[128,512]{1,0:T(8,128)(2,1)S(1)}, bf16[128,512]{1,0:T(8,128)(2,1)S(1)}, u32[]{:S(2)}, u32[]{:S(2)}) collective-permute-start(bf16[128,512]{1,0:T(8,128)(2,1)S(1)} %get-tuple-element.116), channel_id=1, source_target_pairs={{1,0},{2,1},{3,2},{0,3},{5,4},{6,5},{7,6},{4,7},{9,8},{10,9},{11,1... | collective-permute-start | bytes 393224 | tf_op jit(solution)/shard_map/ppermute | solution.py:20
  250.6 7.9 %collective-permute-start.24 = (bf16[128,512]{1,0:T(8,128)(2,1)S(1)}, bf16[128,512]{1,0:T(8,128)(2,1)S(1)}, u32[]{:S(2)}, u32[]{:S(2)}) collective-permute-start(bf16[128,512]{1,0:T(8,128)(2,1)S(1)} %get-tuple-element.115), channel_id=1, source_target_pairs={{2,0},{3,1},{0,2},{1,3},{6,4},{7,5},{4,6},{5,7},{10,8},{11,9},{8,1... | collective-permute-start | bytes 393224 | tf_op jit(solution)/shard_map/ppermute | solution.py:20
  250.7 9.4 %collective-permute-start.23 = (bf16[128,512]{1,0:T(8,128)(2,1)S(1)}, bf16[128,512]{1,0:T(8,128)(2,1)S(1)}, u32[]{:S(2)}, u32[]{:S(2)}) collective-permute-start(bf16[128,512]{1,0:T(8,128)(2,1)S(1)} %slice_bitcast_fusion.8), channel_id=1, source_target_pairs={{3,0},{0,1},{1,2},{2,3},{7,4},{4,5},{5,6},{6,7},{11,8},{8,9},{9,10... | collective-permute-start | bytes 393224 | tf_op jit(solution)/shard_map/ppermute | solution.py:20
  (22 other events, 107.1 us)
Sparse Core Ops, SparseCore 0:
  41.6 70.0 all-gather.2
  155.3 64.5 reduce-scatter.1

commit v4 on v3

--- a/solution.py
+++ b/solution.py
@@ -12,7 +12,7 @@
 F32 = jnp.float32
 CAP = 12
 GROUP = ("y", "c", "z")
-VMEM_LIMIT = 52 * 1024 * 1024
+VMEM_LIMIT = 30 * 1024 * 1024
 
 
 def fetch(a, axis, r):
@@ -61,8 +61,8 @@
         lax.broadcasted_iota(jnp.int32, (slots, both * 4), 0) // CAP
         == lax.broadcasted_iota(jnp.int32, (slots, both * 4), 1)
     ).astype(BF)
-    slot = lax.rem(lax.broadcasted_iota(jnp.int32, (slots, tok), 0), CAP).astype(F32)
-    columns = []
+    slot = lax.rem(lax.broadcasted_iota(jnp.int32, (slots, 1), 0), CAP).astype(F32)
+    places, gates = [], []
     for zz in range(4):
         data = meta[zz].astype(F32)
         named = jnp.zeros((both, tok), F32)
@@ -73,10 +73,11 @@
             gate = jnp.where(same, data[top + k : top + k + 1], gate)
         rank = jnp.where(named > 0, nn(named.astype(BF), earlier), -1.0)
         here = owner == zz
-        rank = jnp.where(here, nn(widen, rank.astype(BF)), -1.0).astype(BF)
-        gate = nn(widen, gate.astype(BF)).astype(BF)
-        columns.append(jnp.where(nn(repeat, rank) == slot, nn(repeat, gate), 0.0).astype(BF))
-    return jnp.concatenate(columns, axis=1)
+        places.append(jnp.where(here, nn(widen, rank.astype(BF)), -1.0).astype(BF))
+        gates.append(nn(widen, gate.astype(BF)).astype(BF))
+    place = nn(repeat, jnp.concatenate(places, axis=1))
+    gate = nn(repeat, jnp.concatenate(gates, axis=1))
+    return jnp.where(place == slot, gate, 0.0).astype(BF)
 
 
 def pick_kernel(ids_ref, whole_ref, own_ref, sib_ref, maps_ref):
@@ -224,22 +225,35 @@
     return [pl.ds(pl.multiple_of(lax.rem(me + r, n) * width, width), width) for r in range(n)]
 
 
+def both_cores(c, ref):
+    return jnp.concatenate([ref[0, c], ref[0, 1 - c]], axis=0)
+
+
+def far_rows(c, lo, hi):
+    return jnp.where(pl.program_id(0) < 2, both_cores(c, lo), both_cores(c, hi))
+
+
 def x_rows_of(c, refs):
     x0, x1, lo, hi, x3 = refs
-    both = lambda ref: jnp.concatenate([ref[0, c], ref[0, 1 - c]], axis=0)
-    far = jnp.where(pl.program_id(0) < 2, both(lo), both(hi))
-    return [both(x0), both(x1), far, both(x3)]
-
-
-def forward_kernel(ids_ref, *refs):
-    x_refs, refs = refs[:5], refs[5:]
-    wg, wu, wd, oo, os, hid_ref, slope_ref, act_ref = refs
+    return [both_cores(c, x0), both_cores(c, x1), far_rows(c, lo, hi), both_cores(c, x3)]
+
+
+def near_kernel(ids_ref, x0, x1, x3, wg, wu, a_ref, b_ref):
+    c = ids_ref[2]
+    n, width = 4, x0.shape[3]
+    moved = moved_columns(ids_ref[3], n, width)
+    blocks = [(0, both_cores(c, x0)), (1, both_cores(c, x1)), (3, both_cores(c, x3))]
+    a_ref[0] = sum(nt(rows, wg[0, :, moved[r]]) for r, rows in blocks)
+    b_ref[0] = sum(nt(rows, wu[0, :, moved[r]]) for r, rows in blocks)
+
+
+def forward_kernel(ids_ref, lo, hi, a_ref, b_ref, wg2, wu2, wd, oo, os, hid_ref, slope_ref, act_ref):
     half, cols = oo.shape[1:]
     n, width = 4, cols // 4
     moved = moved_columns(ids_ref[3], n, width)
-    x_rows = x_rows_of(ids_ref[2], x_refs)
-    a = sum(nt(x_rows[r], wg[0, :, moved[r]]) for r in range(n))
-    b = sum(nt(x_rows[r], wu[0, :, moved[r]]) for r in range(n))
+    far = far_rows(ids_ref[2], lo, hi)
+    a = a_ref[0] + nt(far, wg2[0])
+    b = b_ref[0] + nt(far, wu2[0])
     s = jax.nn.sigmoid(a)
     act = a * s
     hidden = (act * b).astype(BF)
@@ -287,25 +301,28 @@
 
 
 def each(a):
-    return pl.BlockSpec((1,) + a.shape[1:], lambda i: (i,) + (0,) * (a.ndim - 1))
+    return pl.BlockSpec((1,) + a.shape[1:], lambda i, *_: (i,) + (0,) * (len(a.shape) - 1))
+
+
+def each_far(lo, hi):
+    return [
+        pl.BlockSpec((1,) + lo.shape[1:], lambda i, *_: (jnp.minimum(i, 1), 0, 0, 0)),
+        pl.BlockSpec((1,) + hi.shape[1:], lambda i, *_: (jnp.maximum(i - 2, 0), 0, 0, 0)),
+    ]
 
 
 def each_x(blocks):
     specs = [each(a) for a in blocks]
-    lo, hi = blocks[2], blocks[3]
-    specs[2] = pl.BlockSpec((1,) + lo.shape[1:], lambda i: (jnp.minimum(i, 1), 0, 0, 0))
-    specs[3] = pl.BlockSpec((1,) + hi.shape[1:], lambda i: (jnp.maximum(i - 2, 0), 0, 0, 0))
-    return specs
+    return specs[:2] + each_far(blocks[2], blocks[3]) + specs[4:]
 
 
 def per_expert(kernel, ids, in_specs, args, outs, out_specs, products, mebibytes):
-    n_exp = 4
     return pl.pallas_call(
         kernel,
-        grid=(n_exp,),
+        grid_spec=pltpu.PrefetchScalarGridSpec(
+            num_scalar_prefetch=1, grid=(4,), in_specs=in_specs, out_specs=out_specs
+        ),
         out_shape=outs,
-        in_specs=[pl.BlockSpec(memory_space=pltpu.SMEM)] + in_specs,
-        out_specs=out_specs,
         compiler_params=pltpu.CompilerParams(vmem_limit_bytes=VMEM_LIMIT),
         cost_estimate=pl.CostEstimate(
             flops=products * (1536 * 192 * 2048 * 3), bytes_accessed=mebibytes << 20, transcendentals=0
@@ -313,21 +330,35 @@
     )(ids, *args)
 
 
-def forward(ids, x, weights):
-    n_exp, _, rows, width = x[0].shape
-    mid = jax.ShapeDtypeStruct((n_exp, 2 * rows, weights[0].shape[1]), BF)
-    wide = jax.ShapeDtypeStruct(mid.shape, F32)
+def near_products(ids, x, weights):
+    n_exp, _, rows, _ = x[0].shape
+    wide = jax.ShapeDtypeStruct((n_exp, 2 * rows, weights[0].shape[1]), F32)
+    args = tuple(x) + tuple(weights)
+    specs = [each(a) for a in args]
+    return per_expert(near_kernel, ids, specs, args, (wide, wide), (each(wide),) * 2, 2, 14)
+
+
+def forward(ids, far, near, weights):
+    n_exp, _, rows, width = far[0].shape
+    n_exp *= 2
+    wide = near[0]
+    mid = jax.ShapeDtypeStruct(wide.shape, BF)
     out = jax.ShapeDtypeStruct((n_exp, rows, 4 * width), BF)
     outs = (out, out, mid, wide, wide)
-    args = tuple(x) + tuple(weights)
-    specs = each_x(x) + [each(a) for a in weights]
-    return per_expert(forward_kernel, ids, specs, args, outs, tuple(each(a) for a in outs), 3, 26)
+    wg, wu, wd = weights
+    one = pl.BlockSpec(
+        (1, wg.shape[1], width), lambda i, ids: (i, 0, lax.rem(ids[3] + 2, 4))
+    )
+    specs = each_far(*far) + [each(wide), each(wide), one, one, each(wd)]
+    args = tuple(far) + tuple(near) + (wg, wu, wd)
+    outs = tuple(jax.ShapeDtypeStruct(o.shape, o.dtype) for o in outs)
+    return per_expert(forward_kernel, ids, specs, args, outs, tuple(each(a) for a in outs), 2, 18)
 
 
 def backward(ids, g, slope, act, weights, mid, shape):
     outs = (mid, mid, jax.ShapeDtypeStruct((4,) + shape, BF))
     args = tuple(g) + (slope, act) + tuple(weights)
-    spec = pl.BlockSpec((4, 1) + shape[1:], lambda i: (0, i, 0, 0, 0))
+    spec = pl.BlockSpec((4, 1) + shape[1:], lambda i, *_: (0, i, 0, 0, 0))
     out_specs = (each(mid), each(mid), spec)
     return per_expert(back_kernel, ids, [each(a) for a in args], args, outs, out_specs, 3, 26)
 
@@ -339,10 +370,10 @@
     return per_expert(weights_kernel, ids, specs, args, outs, tuple(each(a) for a in outs), 3, 24)
 
 
-def collect_far(parts, axis):
-    own, up, far_lo, far_hi, down = parts
-    half = far_lo.shape[0]
-    got_lo, got_hi = fetch(far_lo, axis, -1), fetch(far_hi, axis, 1)
+def collect_far(parts, got):
+    own, up, down = parts
+    got_lo, got_hi = got
+    half = got_lo.shape[0]
     up = jnp.concatenate([add(up[:half], got_lo), up[half:]])
     down = jnp.concatenate([down[:half], add(down[half:], got_hi)])
     return own, up, down
@@ -398,8 +429,10 @@
     came = came.reshape(n_exp, 2, 16 * CAP, width)
     up, down = fetch(came, "x", 1), fetch(came, "x", -1)
     pair = n_exp // 2
-    x_blocks = (came, up, fetch(down[:pair], "x", -1), fetch(up[pair:], "x", 1), down)
-    out_own, out_sib, hidden, slope, act = forward(ids, x_blocks, weights)
+    near = near_products(ids, (came, up, down), weights[:2])
+    far = (fetch(down[:pair], "x", -1), fetch(up[pair:], "x", 1))
+    x_blocks = (came, up) + far + (down,)
+    out_own, out_sib, hidden, slope, act = forward(ids, far, near, weights)
 
     whole, out_sib = lax.optimization_barrier((whole, out_sib))
     own, sib, maps = pick(ids, whole, n_exp)
@@ -407,6 +440,8 @@
 
     far = sum_tokens(ids, maps, out_own, out_sib, True)
     sib, far = lax.optimization_barrier((fetch(sib, "c", 1), far))
+    got_y = (fetch(far[0], "y", -1), fetch(far[1], "y", 1))
+    got_z = (fetch(far[2], "z", -1), fetch(far[3], "z", 1))
     g_blocks = (own, sib)
     mid = jax.ShapeDtypeStruct(hidden.shape, BF)
     grad_a, grad_b, back = backward(ids, g_blocks, slope, act, weights, mid, came.shape)
@@ -414,8 +449,8 @@
 
     out_sib, grad_a = lax.optimization_barrier((out_sib, grad_a))
     near = sum_tokens(ids, maps, out_own, out_sib, False)
-    ends_y = collect_far((near[0], near[1], far[0], far[1], near[2]), "y")
-    ends_z = collect_far((near[3], near[4], far[2], far[3], near[5]), "z")
+    near, got_y, got_z = lax.optimization_barrier((near, got_y, got_z))
+    ends_y, ends_z = collect_far(near[:3], got_y), collect_far(near[3:], got_z)
     hidden, ends_y, ends_z = lax.optimization_barrier((hidden, ends_y, ends_z))
     grads = weight_grads(ids, x_blocks, g_blocks, (hidden, grad_a, grad_b), w_gate)
     part1, part2 = collect_near(ends_y, "y"), collect_near(ends_z, "z")

time: 279 us -> 259 us (0.928)
  Pallas kernels: 64.3 us -> 46.2 us
  local copies, waits for them, and re-layouts: 26.8 us -> 40.3 us
  waiting for transfers between devices: 116 us -> 103 us
    unnamed x52 -> x100, local copies, waits for them, and re-layouts: 10.4 us -> 26.2 us
    ppermute x26, waiting for transfers between devices: 97.5 us -> 83.7 us  [fetch(): return lax.ppermute(a, axis, [((i + r) % n, i) for i in range(n)])]
    pallas_call x2, Pallas kernels: 17.1 us -> 9.41 us  [call(): pl.pallas_call(kernel, grid_spec=pltpu.PrefetchScalarGridSpec(num_scalar_...]
    pallas_call x3 -> x4, Pallas kernels: 35.7 us -> 29.1 us  [per_expert(): pl.pallas_call(kernel, grid_spec=pltpu.PrefetchScalarGridSpec(num_scalar_...]
    pallas_call x1, Pallas kernels: 11.5 us -> 7.65 us  [pick(): pl.pallas_call(pick_kernel, grid=(4,), out_shape=(rows, rows, maps), in_s...]
  transfers between devices with their start and end apart: 30 -> 30, of which waited for: 19 -> 20; matrix products, arithmetic and copies ran while one was open for 5% -> 4% of each run, Pallas kernels for 18% -> 14%
where the time goes in v4:
time: 259 us; the launch traced here: 258 us
  waiting for transfers between devices  103 us (40%)
  starting transfers between devices  47.1 us (18%)
  Pallas kernels  46.2 us (18%)
  local copies, waits for them, and re-layouts  40.3 us (16%)
  between operations  14.7 us (6%)
  other arithmetic  3.71 us (1%)
  matrix products  3.29 us (1%)
    ppermute x26, waiting for transfers between devices, fetch(): return lax.ppermute(a, axis, [((i + r) % n, i) for i in range(n)])  83.7 us
    ppermute x26, starting transfers between devices, fetch(): return lax.ppermute(a, axis, [((i + r) % n, i) for i in range(n)])  32.4 us
    pallas_call x4, Pallas kernels, per_expert(): pl.pallas_call(kernel, grid_spec=pltpu.PrefetchScalarGridSpec(num_scalar_...  29.1 us
    unnamed x100, local copies, waits for them, and re-layouts  26.2 us
    all_to_all x2, waiting for transfers between devices, exchange(): return lax.all_to_all(a, GROUP, split_axis=0, concat_axis=0, tiled=True)  19.3 us
    all_to_all x2, starting transfers between devices, exchange(): return lax.all_to_all(a, GROUP, split_axis=0, concat_axis=0, tiled=True)  14.6 us
    pallas_call x2, Pallas kernels, call(): pl.pallas_call(kernel, grid_spec=pltpu.PrefetchScalarGridSpec(num_scalar_...  9.41 us
    pallas_call x1, Pallas kernels, pick(): pl.pallas_call(pick_kernel, grid=(4,), out_shape=(rows, rows, maps), in_s...  7.65 us
  transfers between devices with their start and end apart: 30, of which 20 were waited for; matrix products, arithmetic and copies ran while one was open for 4% of the time, Pallas kernels for 14%

profile of v4, /device:TPU:0, one launch (start us, length us, event | category | flops | bytes accessed | tf_op | source)
XLA Modules:
  0.0 258.3 jit_solution(621544526555125972)
XLA Ops:
  10.2 8.5 %all-to-all-start = ((bf16[32,48,512]{2,1,0:T(8,128)(2,1)}), bf16[32,48,512]{2,1,0:T(8,128)(2,1)S(1)}, u32[]{:S(2)}, u32[]{:S(2)}) async-start(bf16[32,48,512]{2,1,0:T(8,128)(2,1)} %bitcast.5), calls=%async_computation | async-start | bytes 3145728 | tf_op jit(solution)/shard_map/all_to_all | solution.py:418
  18.8 2.8 %collective-permute-start = (bf16[128,512]{1,0:T(8,128)(2,1)S(1)}, bf16[128,512]{1,0:T(8,128)(2,1)S(1)}, u32[]{:S(2)}, u32[]{:S(2)}) collective-permute-start(bf16[128,512]{1,0:T(8,128)(2,1)S(1)} %copy-done.45), channel_id=1, source_target_pairs={{1,0},{2,1},{3,2},{0,3},{5,4},{6,5},{7,6},{4,7},{9,8},{10,9},{11,1... | collective-permute-start | bytes 393224 | tf_op jit(solution)/shard_map/ppermute | solution.py:20
  23.4 4.3 %collective-permute-done = bf16[128,512]{1,0:T(8,128)(2,1)S(1)} collective-permute-done((bf16[128,512]{1,0:T(8,128)(2,1)S(1)}, bf16[128,512]{1,0:T(8,128)(2,1)S(1)}, u32[]{:S(2)}, u32[]{:S(2)}) %collective-permute-start) | collective-permute-done | bytes 131104 | tf_op jit(solution)/shard_map/ppermute | solution.py:20
  31.4 10.1 %all-to-all-done = bf16[32,48,512]{2,1,0:T(8,128)(2,1)S(1)} async-done(((bf16[32,48,512]{2,1,0:T(8,128)(2,1)}), bf16[32,48,512]{2,1,0:T(8,128)(2,1)S(1)}, u32[]{:S(2)}, u32[]{:S(2)}) %all-to-all-start) | async-done | bytes 1572896 | tf_op jit(solution)/shard_map/all_to_all | solution.py:418
  42.6 2.4 reshape.65
  51.4 32.2 %collective-permute-done.3.x3.refs_4_ = bf16[4,2,192,512]{3,2,1,0:T(8,128)(2,1)S(1)} collective-permute-done((bf16[4,2,192,512]{3,2,1,0:T(8,128)(2,1)S(1)}, bf16[4,2,192,512]{3,2,1,0:T(8,128)(2,1)S(1)}, u32[]{:S(2)}, u32[]{:S(2)}) %collective-permute-start.3) | collective-permute-done | bytes 1572896 | tf_op jit(solution)/shard_map/ppermute | solution.py:20
  86.4 2.8 %collective-permute-start.6 = (bf16[2,2,192,512]{3,2,1,0:T(8,128)(2,1)}, bf16[2,2,192,512]{3,2,1,0:T(8,128)(2,1)}, u32[]{:S(2)}, u32[]{:S(2)}) collective-permute-start(bf16[2,2,192,512]{3,2,1,0:T(8,128)(2,1)} %slice.89), channel_id=1, source_target_pairs={{1,0},{2,1},{3,2},{0,3},{5,4},{6,5},{7,6},{4,7},{9,8},{10,9},{11,1... | collective-permute-start | bytes 2359304 | tf_op jit(solution)/shard_map/ppermute | solution.py:20
  89.3 2.0 copy-done.9
  95.6 3.8 %shard_map.110 = (f32[4,384,192]{2,1,0:T(8,128)S(1)}, f32[4,384,192]{2,1,0:T(8,128)S(1)}) custom-call(s32[4]{0:T(128)S(1)} %pad_add_fusion.ids_ref, bf16[4,2,192,512]{3,2,1,0:T(8,128)(2,1)S(1)} %copy-done.15, bf16[4,2,192,512]{3,2,1,0:T(8,128)(2,1)S(1)} %copy-done.21, bf16[4,2,192,512]{3,2,1,0:T(8,128)(2,1)S(1)} %copy-done.18, ...), custom_call_target="tpu_custom_call" | custom-call | flops 3623878656 | bytes 14680064 | tf_op jit(solution)/shard_map/pallas_call | solution.py:320
  99.4 4.4 %collective-permute-done.4.lo.refs_2_ = bf16[2,2,192,512]{3,2,1,0:T(8,128)(2,1)} collective-permute-done((bf16[2,2,192,512]{3,2,1,0:T(8,128)(2,1)}, bf16[2,2,192,512]{3,2,1,0:T(8,128)(2,1)}, u32[]{:S(2)}, u32[]{:S(2)}) %collective-permute-start.4) | collective-permute-done | bytes 786464 | tf_op jit(solution)/shard_map/ppermute | solution.py:20
  104.5 5.7 %shard_map.111 = (bf16[4,192,2048]{2,1,0:T(8,128)(2,1)S(1)}, bf16[4,192,2048]{2,1,0:T(8,128)(2,1)S(1)}, bf16[4,384,192]{2,1,0:T(8,128)(2,1)S(1)}, f32[4,384,192]{2,1,0:T(8,128)S(1)}, f32[4,384,192]{2,1,0:T(8,128)S(1)}) custom-call(s32[4]{0:T(128)S(1)} %pad_add_fusion.ids_ref, bf16[2,2,192,512]{3,2,1,0:T(8,128)(2,1)} %collective-permute-done.4.lo.refs_2_, ...), custom_call_target="tpu_custom_call" | custom-call | flops 3623878656 | bytes 18874368 | tf_op jit(solution)/shard_map/pallas_call | solution.py:320
  115.1 3.5 %copy-done.23 = bf16[8448,512]{1,0:T(8,128)(2,1)S(1)} copy-done((bf16[8448,512]{1,0:T(8,128)(2,1)S(1)}, bf16[8448,512]{1,0:T(8,128)(2,1)}, u32[]{:S(2)}) %copy-start.23) | copy-done | bytes 8650776
  118.6 7.6 %shard_map.112 = (bf16[4,192,2048]{2,1,0:T(8,128)(2,1)S(1)}, bf16[4,192,2048]{2,1,0:T(8,128)(2,1)S(1)}, bf16[4,384,512]{2,1,0:T(8,128)(2,1)S(1)}) custom-call(s32[4]{0:T(128)S(1)} %pad_add_fusion.ids_ref, bf16[16,528,512]{2,1,0:T(8,128)(2,1)S(1)} %bitcast.46), custom_call_target="tpu_custom_call" | custom-call | flops 4294967296 | bytes 18874368 | tf_op jit(solution)/shard_map/pallas_call | solution.py:105
  127.1 3.3 %shard_map.113 = (bf16[2,2,128,512]{3,2,1,0:T(8,128)(2,1)S(1)}, bf16[2,2,128,512]{3,2,1,0:T(8,128)(2,1)S(1)}, bf16[2,2,128,512]{3,2,1,0:T(8,128)(2,1)S(1)}, bf16[2,2,128,512]{3,2,1,0:T(8,128)(2,1)S(1)}) custom-call(s32[4]{0:T(128)S(1)} %pad_add_fusion.ids_ref, bf16[4,384,512]{2,1,0:T(8,128)(2,1)S(1)} %get-tuple-element.79.map_ref.map2_ref, ...), custom_call_target="tpu_custom_call" | custom-call | flops 1073741824 | bytes 4194304 | tf_op jit(solution)/shard_map/pallas_call | solution.py:195
  135.4 10.8 %shard_map.114 = (bf16[4,384,192]{2,1,0:T(8,128)(2,1)S(1)}, bf16[4,384,192]{2,1,0:T(8,128)(2,1)S(1)}, bf16[4,4,2,192,512]{4,3,2,1,0:T(8,128)(2,1)}) custom-call(s32[4]{0:T(128)S(1)} %pad_add_fusion.ids_ref, bf16[4,192,2048]{2,1,0:T(8,128)(2,1)S(1)} %get-tuple-element.75.own.refs_5_, bf16[4,192,2048]{2,1,0:T(8,128)(2,1)S(1)} %collective-permute-done.8.sib.refs_6_, ...), custom_call_target="tpu_custom_call" | custom-call | flops 5435817984 | bytes 27262976 | tf_op jit(solution)/shard_map/pallas_call | solution.py:320
  152.7 2.0 collective-permute-start.12
  158.3 6.2 %shard_map.115 = (bf16[4,2,128,512]{3,2,1,0:T(8,128)(2,1)S(1)}, bf16[4,2,128,512]{3,2,1,0:T(8,128)(2,1)S(1)}, bf16[4,2,128,512]{3,2,1,0:T(8,128)(2,1)S(1)}, bf16...) custom-call(s32[4]{0:T(128)S(1)} %pad_add_fusion.ids_ref, ...), custom_call_target="tpu_custom_call" | custom-call | flops 3221225472 | bytes 12582912 | tf_op jit(solution)/shard_map/pallas_call | solution.py:195
  164.5 2.2 collective-permute-done.11
  170.0 3.0 %collective-permute-start.16 = (bf16[4,2,128,512]{3,2,1,0:T(8,128)(2,1)S(1)}, bf16[4,2,128,512]{3,2,1,0:T(8,128)(2,1)S(1)}, u32[]{:S(2)}, u32[]{:S(2)}) collective-permute-start(bf16[4,2,128,512]{3,2,1,0:T(8,128)(2,1)S(1)} %pad_maximum_fusion.3), channel_id=1, source_target_pairs={{4,0},{8,4},{12,8},{0,12},{5,1},{9,5},{13,9},{1,13},{6,2},{10,6},{... | collective-permute-start | bytes 3145736 | tf_op jit(solution)/shard_map/ppermute | solution.py:20
  173.0 8.8 %shard_map.116 = (bf16[4,192,2048]{2,1,0:T(8,128)(2,1)}, bf16[4,192,2048]{2,1,0:T(8,128)(2,1)}, bf16[4,192,2048]{2,1,0:T(8,128)(2,1)}) custom-call(s32[4]{0:T(128)S(1)} %pad_add_fusion.ids_ref, bf16[4,2,192,512]{3,2,1,0:T(8,128)(2,1)S(1)} %copy-done.16, bf16[4,2,192,512]{3,2,1,0:T(8,128)(2,1)S(1)} %copy-done.22, ...), custom_call_target="tpu_custom_call" | custom-call | flops 5435817984 | bytes 25165824 | tf_op jit(solution)/shard_map/pallas_call | solution.py:320
  181.8 10.5 %collective-permute-done.14 = bf16[4,2,128,512]{3,2,1,0:T(8,128)(2,1)S(1)} collective-permute-done((bf16[4,2,128,512]{3,2,1,0:T(8,128)(2,1)S(1)}, bf16[4,2,128,512]{3,2,1,0:T(8,128)(2,1)S(1)}, u32[]{:S(2)}, u32[]{:S(2)}) %collective-permute-start.14) | collective-permute-done | bytes 1048608 | tf_op jit(solution)/shard_map/ppermute | solution.py:20
  194.4 2.9 %collective-permute-done.15 = bf16[4,2,128,512]{3,2,1,0:T(8,128)(2,1)S(1)} collective-permute-done((bf16[4,2,128,512]{3,2,1,0:T(8,128)(2,1)S(1)}, bf16[4,2,128,512]{3,2,1,0:T(8,128)(2,1)S(1)}, u32[]{:S(2)}, u32[]{:S(2)}) %collective-permute-start.15) | collective-permute-done | bytes 1048608 | tf_op jit(solution)/shard_map/ppermute | solution.py:20
  200.1 2.0 collective-permute-start.22
  202.5 3.8 %collective-permute-done.19 = bf16[2,128,512]{2,1,0:T(8,128)(2,1)S(1)} collective-permute-done((bf16[2,128,512]{2,1,0:T(8,128)(2,1)S(1)}, bf16[2,128,512]{2,1,0:T(8,128)(2,1)S(1)}, u32[]{:S(2)}, u32[]{:S(2)}) %collective-permute-start.19) | collective-permute-done | bytes 262176 | tf_op jit(solution)/shard_map/ppermute | solution.py:20
  208.1 2.7 %collective-permute-done.17 = bf16[2,128,512]{2,1,0:T(8,128)(2,1)S(1)} collective-permute-done((bf16[2,128,512]{2,1,0:T(8,128)(2,1)S(1)}, bf16[2,128,512]{2,1,0:T(8,128)(2,1)S(1)}, u32[]{:S(2)}, u32[]{:S(2)}) %collective-permute-start.17) | collective-permute-done | bytes 262176 | tf_op jit(solution)/shard_map/ppermute | solution.py:20
  211.0 2.8 %collective-permute-done.20 = bf16[2,128,512]{2,1,0:T(8,128)(2,1)S(1)} collective-permute-done((bf16[2,128,512]{2,1,0:T(8,128)(2,1)S(1)}, bf16[2,128,512]{2,1,0:T(8,128)(2,1)S(1)}, u32[]{:S(2)}, u32[]{:S(2)}) %collective-permute-start.20) | collective-permute-done | bytes 262176 | tf_op jit(solution)/shard_map/ppermute | solution.py:20
  214.0 2.4 reshape.68
  217.9 3.6 %reshape.73 = bf16[32,48,512]{2,1,0:T(8,128)(2,1)} reshape(bf16[4,2,4,4,12,512]{5,4,3,2,1,0:T(8,128)(2,1)} %copy.39) | data formatting | bytes 3145728 | tf_op jit(solution)/shard_map/all_to_all | solution.py:418
  221.6 6.1 %all-to-all-start.1 = ((bf16[32,48,512]{2,1,0:T(8,128)(2,1)}), bf16[32,48,512]{2,1,0:T(8,128)(2,1)S(1)}, u32[]{:S(2)}, u32[]{:S(2)}) async-start(bf16[32,48,512]{2,1,0:T(8,128)(2,1)} %reshape.73), calls=%async_computation.2 | async-start | bytes 3145728 | tf_op jit(solution)/shard_map/all_to_all | solution.py:418
  227.7 3.2 %collective-permute-start.25 = (bf16[128,512]{1,0:T(8,128)(2,1)S(1)}, bf16[128,512]{1,0:T(8,128)(2,1)S(1)}, u32[]{:S(2)}, u32[]{:S(2)}) collective-permute-start(bf16[128,512]{1,0:T(8,128)(2,1)S(1)} %get-tuple-element.140), channel_id=1, source_target_pairs={{1,0},{2,1},{3,2},{0,3},{5,4},{6,5},{7,6},{4,7},{9,8},{10,9},{11,1... | collective-permute-start | bytes 393224 | tf_op jit(solution)/shard_map/ppermute | solution.py:20
  231.9 5.0 %collective-permute-done.25 = bf16[128,512]{1,0:T(8,128)(2,1)S(1)} collective-permute-done((bf16[128,512]{1,0:T(8,128)(2,1)S(1)}, bf16[128,512]{1,0:T(8,128)(2,1)S(1)}, u32[]{:S(2)}, u32[]{:S(2)}) %collective-permute-start.25) | collective-permute-done | bytes 131104 | tf_op jit(solution)/shard_map/ppermute | solution.py:20
  241.1 9.3 %all-to-all-done.1 = bf16[32,48,512]{2,1,0:T(8,128)(2,1)S(1)} async-done(((bf16[32,48,512]{2,1,0:T(8,128)(2,1)}), bf16[32,48,512]{2,1,0:T(8,128)(2,1)S(1)}, u32[]{:S(2)}, u32[]{:S(2)}) %all-to-all-start.1) | async-done | bytes 1572896 | tf_op jit(solution)/shard_map/all_to_all | solution.py:418
  (174 shorter events, 63.2 us)
Async XLA Ops:
  10.2 31.3 %all-to-all-start = ((bf16[32,48,512]{2,1,0:T(8,128)(2,1)}), bf16[32,48,512]{2,1,0:T(8,128)(2,1)S(1)}, u32[]{:S(2)}, u32[]{:S(2)}) async-start(bf16[32,48,512]{2,1,0:T(8,128)(2,1)} %bitcast.5), calls=%async_computation | async-start | bytes 3145728 | tf_op jit(solution)/shard_map/all_to_all | solution.py:418
  18.8 96.3 %all-gather.3.cloned.1.call-start = ((), (), s32[]{:S(2)}) async-start(), calls=%async_computation.4 | async-start | bytes 9191424 | tf_op jit(solution)/shard_map/all_gather | solution.py:426
  18.8 8.9 %collective-permute-start = (bf16[128,512]{1,0:T(8,128)(2,1)S(1)}, bf16[128,512]{1,0:T(8,128)(2,1)S(1)}, u32[]{:S(2)}, u32[]{:S(2)}) collective-permute-start(bf16[128,512]{1,0:T(8,128)(2,1)S(1)} %copy-done.45), channel_id=1, source_target_pairs={{1,0},{2,1},{3,2},{0,3},{5,4},{6,5},{7,6},{4,7},{9,8},{10,9},{11,1... | collective-permute-start | bytes 393224 | tf_op jit(solution)/shard_map/ppermute | solution.py:20
  21.7 7.9 %collective-permute-start.1 = (bf16[128,512]{1,0:T(8,128)(2,1)S(1)}, bf16[128,512]{1,0:T(8,128)(2,1)S(1)}, u32[]{:S(2)}, u32[]{:S(2)}) collective-permute-start(bf16[128,512]{1,0:T(8,128)(2,1)S(1)} %copy-done.45), channel_id=1, source_target_pairs={{2,0},{3,1},{0,2},{1,3},{6,4},{7,5},{4,6},{5,7},{10,8},{11,9},{8,1... | collective-permute-start | bytes 393224 | tf_op jit(solution)/shard_map/ppermute | solution.py:20
  22.5 8.9 %collective-permute-start.2 = (bf16[128,512]{1,0:T(8,128)(2,1)S(1)}, bf16[128,512]{1,0:T(8,128)(2,1)S(1)}, u32[]{:S(2)}, u32[]{:S(2)}) collective-permute-start(bf16[128,512]{1,0:T(8,128)(2,1)S(1)} %copy-done.45), channel_id=1, source_target_pairs={{3,0},{0,1},{1,2},{2,3},{7,4},{4,5},{5,6},{6,7},{11,8},{8,9},{9,10... | collective-permute-start | bytes 393224 | tf_op jit(solution)/shard_map/ppermute | solution.py:20
  42.6 171.4 %reduce-scatter.2.cloned.1.call-start = ((), (), s32[]{:S(2)}) async-start(), calls=%async_computation.3 | async-start | bytes 7864320 | tf_op jit(solution)/shard_map/reduce_scatter | solution.py:448
  46.9 42.4 %copy-start.6 = (bf16[4,192,2048]{2,1,0:T(8,128)(2,1)S(1)}, bf16[4,192,2048]{2,1,0:T(8,128)(2,1)}, u32[]{:S(2)}) copy-start(bf16[4,192,2048]{2,1,0:T(8,128)(2,1)} %wg.3) | copy-start | bytes 9437188
  46.9 36.6 %collective-permute-start.3 = (bf16[4,2,192,512]{3,2,1,0:T(8,128)(2,1)S(1)}, bf16[4,2,192,512]{3,2,1,0:T(8,128)(2,1)S(1)}, u32[]{:S(2)}, u32[]{:S(2)}) collective-permute-start(bf16[4,2,192,512]{3,2,1,0:T(8,128)(2,1)S(1)} %copy.33.x0.refs_0_), channel_id=1, source_target_pairs={{3,0},{0,1},{1,2},{2,3},{7,4},{4,5},{5,6},{6,7},{11,8},{8,9},{9,10... | collective-permute-start | bytes 4718600 | tf_op jit(solution)/shard_map/ppermute | solution.py:20
  48.5 36.4 %collective-permute-start.5 = (bf16[4,2,192,512]{3,2,1,0:T(8,128)(2,1)S(1)}, bf16[4,2,192,512]{3,2,1,0:T(8,128)(2,1)S(1)}, u32[]{:S(2)}, u32[]{:S(2)}) collective-permute-start(bf16[4,2,192,512]{3,2,1,0:T(8,128)(2,1)S(1)} %copy.33.x0.refs_0_), channel_id=1, source_target_pairs={{1,0},{2,1},{3,2},{0,3},{5,4},{6,5},{7,6},{4,7},{9,8},{10,9},{11,1... | collective-permute-start | bytes 4718600 | tf_op jit(solution)/shard_map/ppermute | solution.py:20
  84.6 19.2 %collective-permute-start.4 = (bf16[2,2,192,512]{3,2,1,0:T(8,128)(2,1)}, bf16[2,2,192,512]{3,2,1,0:T(8,128)(2,1)}, u32[]{:S(2)}, u32[]{:S(2)}) collective-permute-start(bf16[2,2,192,512]{3,2,1,0:T(8,128)(2,1)} %slice.88), channel_id=1, source_target_pairs={{3,0},{0,1},{1,2},{2,3},{7,4},{4,5},{5,6},{6,7},{11,8},{8,9},{9,10... | collective-permute-start | bytes 2359304 | tf_op jit(solution)/shard_map/ppermute | solution.py:20
  86.4 18.1 %collective-permute-start.6 = (bf16[2,2,192,512]{3,2,1,0:T(8,128)(2,1)}, bf16[2,2,192,512]{3,2,1,0:T(8,128)(2,1)}, u32[]{:S(2)}, u32[]{:S(2)}) collective-permute-start(bf16[2,2,192,512]{3,2,1,0:T(8,128)(2,1)} %slice.89), channel_id=1, source_target_pairs={{1,0},{2,1},{3,2},{0,3},{5,4},{6,5},{7,6},{4,7},{9,8},{10,9},{11,1... | collective-permute-start | bytes 2359304 | tf_op jit(solution)/shard_map/ppermute | solution.py:20
  115.1 11.1 %collective-permute-start.7 = (bf16[4,192,2048]{2,1,0:T(8,128)(2,1)}, bf16[4,192,2048]{2,1,0:T(8,128)(2,1)S(1)}, u32[]{:S(2)}, u32[]{:S(2)}) collective-permute-start(bf16[4,192,2048]{2,1,0:T(8,128)(2,1)} %copy-done.26), channel_id=1, source_target_pairs={{16,0},{0,16},{17,1},{1,17},{18,2},{2,18},{19,3},{3,19},{20,4},{4,... | collective-permute-start | bytes 9437192 | tf_op jit(solution)/shard_map/ppermute | solution.py:20
  126.3 6.1 %collective-permute-start.8 = (bf16[4,192,2048]{2,1,0:T(8,128)(2,1)S(1)}, bf16[4,192,2048]{2,1,0:T(8,128)(2,1)S(1)}, u32[]{:S(2)}, u32[]{:S(2)}) collective-permute-start(bf16[4,192,2048]{2,1,0:T(8,128)(2,1)S(1)} %get-tuple-element.78), channel_id=1, source_target_pairs={{16,0},{0,16},{17,1},{1,17},{18,2},{2,18},{19,3},{3,19},{20,4},{4,... | collective-permute-start | bytes 9437192 | tf_op jit(solution)/shard_map/ppermute | solution.py:20
  148.1 16.4 %collective-permute-start.9 = (bf16[2,2,128,512]{3,2,1,0:T(8,128)(2,1)}, bf16[2,2,128,512]{3,2,1,0:T(8,128)(2,1)S(1)}, u32[]{:S(2)}, u32[]{:S(2)}) collective-permute-start(bf16[2,2,128,512]{3,2,1,0:T(8,128)(2,1)} %copy-done.36), channel_id=1, source_target_pairs={{96,0},{0,32},{32,64},{64,96},{97,1},{1,33},{33,65},{65,97},{98,2}... | collective-permute-start | bytes 1572872 | tf_op jit(solution)/shard_map/ppermute | solution.py:20
  149.5 15.0 %collective-permute-start.10 = (bf16[2,2,128,512]{3,2,1,0:T(8,128)(2,1)}, bf16[2,2,128,512]{3,2,1,0:T(8,128)(2,1)S(1)}, u32[]{:S(2)}, u32[]{:S(2)}) collective-permute-start(bf16[2,2,128,512]{3,2,1,0:T(8,128)(2,1)} %copy-done.35), channel_id=1, source_target_pairs={{32,0},{64,32},{96,64},{0,96},{33,1},{65,33},{97,65},{1,97},{34,2}... | collective-permute-start | bytes 1572872 | tf_op jit(solution)/shard_map/ppermute | solution.py:20
  151.4 15.2 %collective-permute-start.11 = (bf16[2,2,128,512]{3,2,1,0:T(8,128)(2,1)}, bf16[2,2,128,512]{3,2,1,0:T(8,128)(2,1)S(1)}, u32[]{:S(2)}, u32[]{:S(2)}) collective-permute-start(bf16[2,2,128,512]{3,2,1,0:T(8,128)(2,1)} %copy-done.34), channel_id=1, source_target_pairs={{12,0},{0,4},{4,8},{8,12},{13,1},{1,5},{5,9},{9,13},{14,2},{2,6},{... | collective-permute-start | bytes 1572872 | tf_op jit(solution)/shard_map/ppermute | solution.py:20
  152.7 14.0 %collective-permute-start.12 = (bf16[2,2,128,512]{3,2,1,0:T(8,128)(2,1)}, bf16[2,2,128,512]{3,2,1,0:T(8,128)(2,1)S(1)}, u32[]{:S(2)}, u32[]{:S(2)}) collective-permute-start(bf16[2,2,128,512]{3,2,1,0:T(8,128)(2,1)} %copy-done.33), channel_id=1, source_target_pairs={{4,0},{8,4},{12,8},{0,12},{5,1},{9,5},{13,9},{1,13},{6,2},{10,6},{... | collective-permute-start | bytes 1572872 | tf_op jit(solution)/shard_map/ppermute | solution.py:20
  167.9 24.4 %collective-permute-start.14 = (bf16[4,2,128,512]{3,2,1,0:T(8,128)(2,1)S(1)}, bf16[4,2,128,512]{3,2,1,0:T(8,128)(2,1)S(1)}, u32[]{:S(2)}, u32[]{:S(2)}) collective-permute-start(bf16[4,2,128,512]{3,2,1,0:T(8,128)(2,1)S(1)} %pad_maximum_fusion.1), channel_id=1, source_target_pairs={{32,0},{64,32},{96,64},{0,96},{33,1},{65,33},{97,65},{1,97},{34,2}... | collective-permute-start | bytes 3145736 | tf_op jit(solution)/shard_map/ppermute | solution.py:20
  168.7 25.2 %collective-permute-start.13 = (bf16[4,2,128,512]{3,2,1,0:T(8,128)(2,1)S(1)}, bf16[4,2,128,512]{3,2,1,0:T(8,128)(2,1)S(1)}, u32[]{:S(2)}, u32[]{:S(2)}) collective-permute-start(bf16[4,2,128,512]{3,2,1,0:T(8,128)(2,1)S(1)} %pad_maximum_fusion), channel_id=1, source_target_pairs={{96,0},{0,32},{32,64},{64,96},{97,1},{1,33},{33,65},{65,97},{98,2}... | collective-permute-start | bytes 3145736 | tf_op jit(solution)/shard_map/ppermute | solution.py:20
  170.0 24.4 %collective-permute-start.16 = (bf16[4,2,128,512]{3,2,1,0:T(8,128)(2,1)S(1)}, bf16[4,2,128,512]{3,2,1,0:T(8,128)(2,1)S(1)}, u32[]{:S(2)}, u32[]{:S(2)}) collective-permute-start(bf16[4,2,128,512]{3,2,1,0:T(8,128)(2,1)S(1)} %pad_maximum_fusion.3), channel_id=1, source_target_pairs={{4,0},{8,4},{12,8},{0,12},{5,1},{9,5},{13,9},{1,13},{6,2},{10,6},{... | collective-permute-start | bytes 3145736 | tf_op jit(solution)/shard_map/ppermute | solution.py:20
  173.0 24.4 %collective-permute-start.15 = (bf16[4,2,128,512]{3,2,1,0:T(8,128)(2,1)S(1)}, bf16[4,2,128,512]{3,2,1,0:T(8,128)(2,1)S(1)}, u32[]{:S(2)}, u32[]{:S(2)}) collective-permute-start(bf16[4,2,128,512]{3,2,1,0:T(8,128)(2,1)S(1)} %pad_maximum_fusion.2), channel_id=1, source_target_pairs={{12,0},{0,4},{4,8},{8,12},{13,1},{1,5},{5,9},{9,13},{14,2},{2,6},{... | collective-permute-start | bytes 3145736 | tf_op jit(solution)/shard_map/ppermute | solution.py:20
  197.9 8.4 %collective-permute-start.19 = (bf16[2,128,512]{2,1,0:T(8,128)(2,1)S(1)}, bf16[2,128,512]{2,1,0:T(8,128)(2,1)S(1)}, u32[]{:S(2)}, u32[]{:S(2)}) collective-permute-start(bf16[2,128,512]{2,1,0:T(8,128)(2,1)S(1)} %get-tuple-element.137), channel_id=1, source_target_pairs={{4,0},{8,4},{12,8},{0,12},{5,1},{9,5},{13,9},{1,13},{6,2},{10,6},{... | collective-permute-start | bytes 786440 | tf_op jit(solution)/shard_map/ppermute | solution.py:20
  198.2 9.9 %collective-permute-start.18 = (bf16[2,128,512]{2,1,0:T(8,128)(2,1)S(1)}, bf16[2,128,512]{2,1,0:T(8,128)(2,1)S(1)}, u32[]{:S(2)}, u32[]{:S(2)}) collective-permute-start(bf16[2,128,512]{2,1,0:T(8,128)(2,1)S(1)} %get-tuple-element.138), channel_id=1, source_target_pairs={{8,0},{12,4},{0,8},{4,12},{9,1},{13,5},{1,9},{5,13},{10,2},{14,6},... | collective-permute-start | bytes 786440 | tf_op jit(solution)/shard_map/ppermute | solution.py:20
  199.1 11.8 %collective-permute-start.17 = (bf16[2,128,512]{2,1,0:T(8,128)(2,1)S(1)}, bf16[2,128,512]{2,1,0:T(8,128)(2,1)S(1)}, u32[]{:S(2)}, u32[]{:S(2)}) collective-permute-start(bf16[2,128,512]{2,1,0:T(8,128)(2,1)S(1)} %get-tuple-element.136), channel_id=1, source_target_pairs={{12,0},{0,4},{4,8},{8,12},{13,1},{1,5},{5,9},{9,13},{14,2},{2,6},{... | collective-permute-start | bytes 786440 | tf_op jit(solution)/shard_map/ppermute | solution.py:20
  200.1 10.9 %collective-permute-start.22 = (bf16[2,128,512]{2,1,0:T(8,128)(2,1)S(1)}, bf16[2,128,512]{2,1,0:T(8,128)(2,1)S(1)}, u32[]{:S(2)}, u32[]{:S(2)}) collective-permute-start(bf16[2,128,512]{2,1,0:T(8,128)(2,1)S(1)} %get-tuple-element.134), channel_id=1, source_target_pairs={{32,0},{64,32},{96,64},{0,96},{33,1},{65,33},{97,65},{1,97},{34,2}... | collective-permute-start | bytes 786440 | tf_op jit(solution)/shard_map/ppermute | solution.py:20
  202.1 9.0 %collective-permute-start.21 = (bf16[2,128,512]{2,1,0:T(8,128)(2,1)S(1)}, bf16[2,128,512]{2,1,0:T(8,128)(2,1)S(1)}, u32[]{:S(2)}, u32[]{:S(2)}) collective-permute-start(bf16[2,128,512]{2,1,0:T(8,128)(2,1)S(1)} %get-tuple-element.135), channel_id=1, source_target_pairs={{64,0},{96,32},{0,64},{32,96},{65,1},{97,33},{1,65},{33,97},{66,2}... | collective-permute-start | bytes 786440 | tf_op jit(solution)/shard_map/ppermute | solution.py:20
  206.3 7.6 %collective-permute-start.20 = (bf16[2,128,512]{2,1,0:T(8,128)(2,1)S(1)}, bf16[2,128,512]{2,1,0:T(8,128)(2,1)S(1)}, u32[]{:S(2)}, u32[]{:S(2)}) collective-permute-start(bf16[2,128,512]{2,1,0:T(8,128)(2,1)S(1)} %get-tuple-element.133), channel_id=1, source_target_pairs={{96,0},{0,32},{32,64},{64,96},{97,1},{1,33},{33,65},{65,97},{98,2}... | collective-permute-start | bytes 786440 | tf_op jit(solution)/shard_map/ppermute | solution.py:20
  221.6 28.8 %all-to-all-start.1 = ((bf16[32,48,512]{2,1,0:T(8,128)(2,1)}), bf16[32,48,512]{2,1,0:T(8,128)(2,1)S(1)}, u32[]{:S(2)}, u32[]{:S(2)}) async-start(bf16[32,48,512]{2,1,0:T(8,128)(2,1)} %reshape.73), calls=%async_computation.2 | async-start | bytes 3145728 | tf_op jit(solution)/shard_map/all_to_all | solution.py:418
  227.7 23.8 %copy-start.1 = (bf16[128,512]{1,0:T(8,128)(2,1)S(1)}, bf16[128,512]{1,0:T(8,128)(2,1)}, u32[]{:S(2)}) copy-start(bf16[128,512]{1,0:T(8,128)(2,1)} %param.7) | copy-start | bytes 393220
  227.7 9.2 %collective-permute-start.25 = (bf16[128,512]{1,0:T(8,128)(2,1)S(1)}, bf16[128,512]{1,0:T(8,128)(2,1)S(1)}, u32[]{:S(2)}, u32[]{:S(2)}) collective-permute-start(bf16[128,512]{1,0:T(8,128)(2,1)S(1)} %get-tuple-element.140), channel_id=1, source_target_pairs={{1,0},{2,1},{3,2},{0,3},{5,4},{6,5},{7,6},{4,7},{9,8},{10,9},{11,1... | collective-permute-start | bytes 393224 | tf_op jit(solution)/shard_map/ppermute | solution.py:20
  230.9 7.9 %collective-permute-start.24 = (bf16[128,512]{1,0:T(8,128)(2,1)S(1)}, bf16[128,512]{1,0:T(8,128)(2,1)S(1)}, u32[]{:S(2)}, u32[]{:S(2)}) collective-permute-start(bf16[128,512]{1,0:T(8,128)(2,1)S(1)} %get-tuple-element.139), channel_id=1, source_target_pairs={{2,0},{3,1},{0,2},{1,3},{6,4},{7,5},{4,6},{5,7},{10,8},{11,9},{8,1... | collective-permute-start | bytes 393224 | tf_op jit(solution)/shard_map/ppermute | solution.py:20
  230.9 9.5 %collective-permute-start.23 = (bf16[128,512]{1,0:T(8,128)(2,1)S(1)}, bf16[128,512]{1,0:T(8,128)(2,1)S(1)}, u32[]{:S(2)}, u32[]{:S(2)}) collective-permute-start(bf16[128,512]{1,0:T(8,128)(2,1)S(1)} %slice_bitcast_fusion.8), channel_id=1, source_target_pairs={{3,0},{0,1},{1,2},{2,3},{7,4},{4,5},{5,6},{6,7},{11,8},{8,9},{9,10... | collective-permute-start | bytes 393224 | tf_op jit(solution)/shard_map/ppermute | solution.py:20
  (46 other events, 280.1 us)
Sparse Core Ops, SparseCore 0:
  41.6 70.0 all-gather.2
  148.2 64.5 reduce-scatter.1

commit v5 on v4

--- a/solution.py
+++ b/solution.py
@@ -370,6 +370,47 @@
     return per_expert(weights_kernel, ids, specs, args, outs, tuple(each(a) for a in outs), 3, 24)
 
 
+def regroup_matrix(span):
+    n = 4 * span
+    line = lax.broadcasted_iota(jnp.int32, (n, 1), 0)
+    col = lax.broadcasted_iota(jnp.int32, (n, n), 1)
+    swapped = (lax.rem(line // CAP, 4) * 4 + line // span) * CAP + lax.rem(line, CAP)
+    return (swapped == col).astype(BF)
+
+
+def by_expert_kernel(rows_ref, out_ref):
+    span = out_ref.shape[2] // 4
+    matrix = regroup_matrix(span)
+    for i in range(rows_ref.shape[0]):
+        rows = nn(matrix, rows_ref[i]).astype(BF)
+        y, c = i // 2, i % 2
+        for e in range(out_ref.shape[0]):
+            out_ref[e, c, y * span : (y + 1) * span] = rows[e * span : (e + 1) * span]
+
+
+def by_group_kernel(rows_ref, out_ref):
+    span = rows_ref.shape[2] // 4
+    matrix = regroup_matrix(span)
+    for i in range(out_ref.shape[0]):
+        y, c = i // 2, i % 2
+        rows = [rows_ref[e, c, y * span : (y + 1) * span] for e in range(rows_ref.shape[0])]
+        out_ref[i] = tn(matrix, jnp.concatenate(rows, axis=0)).astype(BF)
+
+
+def regroup(rows, n_exp, to_experts):
+    width = rows.shape[-1]
+    flat, deep = (8, 4 * n_exp * CAP, width), (n_exp, 2, 16 * CAP, width)
+    vmem = pl.BlockSpec(memory_space=pltpu.VMEM)
+    return pl.pallas_call(
+        by_expert_kernel if to_experts else by_group_kernel,
+        out_shape=jax.ShapeDtypeStruct(deep if to_experts else flat, BF),
+        in_specs=[vmem],
+        out_specs=vmem,
+        compiler_params=pltpu.CompilerParams(vmem_limit_bytes=VMEM_LIMIT),
+        cost_estimate=pl.CostEstimate(flops=1 << 29, bytes_accessed=3 << 20, transcendentals=0),
+    )(rows.reshape(flat if to_experts else deep))
+
+
 def collect_far(parts, got):
     own, up, down = parts
     got_lo, got_hi = got
@@ -425,8 +466,7 @@
     came, whole = lax.optimization_barrier((came, whole))
     whole = lax.all_gather(whole, ("y", "z"))
 
-    came = came.reshape(4, 2, 4, n_exp, CAP, width).transpose(3, 1, 0, 2, 4, 5)
-    came = came.reshape(n_exp, 2, 16 * CAP, width)
+    came = regroup(came, n_exp, True)
     up, down = fetch(came, "x", 1), fetch(came, "x", -1)
     pair = n_exp // 2
     near = near_products(ids, (came, up, down), weights[:2])
@@ -458,8 +498,7 @@
     part1, part2 = collect_small(part1, "z"), collect_small(part2, "y")
 
     back, part1, part2 = lax.optimization_barrier((back, part1, part2))
-    back = back.reshape(n_exp, 2, 4, 4, CAP, width).transpose(2, 1, 3, 0, 4, 5)
-    back = exchange(back.reshape(slots, width))
+    back = exchange(regroup(back, n_exp, False).reshape(slots, width))
     mixed = collect_small((part1[0], part1[1], part2[0], part2[1]), "x")
     grad_tokens = tn(own_map, back).astype(BF)
     return (mixed, grad_tokens) + tuple(grads)

time: 259 us -> 252 us (0.973)
  local copies, waits for them, and re-layouts: 40.3 us -> 29 us
    all_to_all x2 -> x0, local copies, waits for them, and re-layouts: 5.2 us -> none  [exchange(): return lax.all_to_all(a, GROUP, split_axis=0, concat_axis=0, tiled=True)]
    reshape x3 -> x0, local copies, waits for them, and re-layouts: 4.99 us -> none  [the longest x1 2.36 us: body(): back = back.reshape(n_exp, 2, 4, 4, CAP, width).transpose(2, 1, 3, 0, 4, 5)]
  transfers between devices with their start and end apart: 30 -> 30, of which waited for: 20 -> 22; matrix products, arithmetic and copies ran while one was open for 4% -> 2% of each run, Pallas kernels for 14% -> 14%
where the time goes in v5:
time: 252 us; the launch traced here: 251 us
  waiting for transfers between devices  105 us (42%)
  Pallas kernels  48.6 us (19%)
  starting transfers between devices  46.8 us (19%)
  local copies, waits for them, and re-layouts  29 us (12%)
  between operations  14.7 us (6%)
  other arithmetic  3.71 us (1%)
  matrix products  3.29 us (1%)
    ppermute x26, waiting for transfers between devices, fetch(): return lax.ppermute(a, axis, [((i + r) % n, i) for i in range(n)])  83.8 us
    ppermute x26, starting transfers between devices, fetch(): return lax.ppermute(a, axis, [((i + r) % n, i) for i in range(n)])  32.5 us
    pallas_call x4, Pallas kernels, per_expert(): pl.pallas_call(kernel, grid_spec=pltpu.PrefetchScalarGridSpec(num_scalar_...  29.2 us
    unnamed x100, local copies, waits for them, and re-layouts  26.7 us
    all_to_all x2, waiting for transfers between devices, exchange(): return lax.all_to_all(a, GROUP, split_axis=0, concat_axis=0, tiled=True)  19.6 us
    all_to_all x2, starting transfers between devices, exchange(): return lax.all_to_all(a, GROUP, split_axis=0, concat_axis=0, tiled=True)  14.1 us
    pallas_call x2, Pallas kernels, call(): pl.pallas_call(kernel, grid_spec=pltpu.PrefetchScalarGridSpec(num_scalar_...  9.41 us
    pallas_call x1, Pallas kernels, pick(): pl.pallas_call(pick_kernel, grid=(4,), out_shape=(rows, rows, maps), in_s...  7.65 us
  transfers between devices with their start and end apart: 30, of which 22 were waited for; matrix products, arithmetic and copies ran while one was open for 2% of the time, Pallas kernels for 14%

profile of v5, /device:TPU:0, one launch (start us, length us, event | category | flops | bytes accessed | tf_op | source)
XLA Modules:
  0.0 250.9 jit_solution(283522701655910856)
XLA Ops:
  10.2 8.5 %all-to-all-start = ((bf16[32,48,512]{2,1,0:T(8,128)(2,1)}), bf16[32,48,512]{2,1,0:T(8,128)(2,1)S(1)}, u32[]{:S(2)}, u32[]{:S(2)}) async-start(bf16[32,48,512]{2,1,0:T(8,128)(2,1)} %bitcast.5), calls=%async_computation | async-start | bytes 3145728 | tf_op jit(solution)/shard_map/all_to_all | solution.py:459
  18.8 2.8 %collective-permute-start = (bf16[128,512]{1,0:T(8,128)(2,1)S(1)}, bf16[128,512]{1,0:T(8,128)(2,1)S(1)}, u32[]{:S(2)}, u32[]{:S(2)}) collective-permute-start(bf16[128,512]{1,0:T(8,128)(2,1)S(1)} %copy-done.45), channel_id=1, source_target_pairs={{1,0},{2,1},{3,2},{0,3},{5,4},{6,5},{7,6},{4,7},{9,8},{10,9},{11,1... | collective-permute-start | bytes 393224 | tf_op jit(solution)/shard_map/ppermute | solution.py:20
  23.4 4.3 %collective-permute-done = bf16[128,512]{1,0:T(8,128)(2,1)S(1)} collective-permute-done((bf16[128,512]{1,0:T(8,128)(2,1)S(1)}, bf16[128,512]{1,0:T(8,128)(2,1)S(1)}, u32[]{:S(2)}, u32[]{:S(2)}) %collective-permute-start) | collective-permute-done | bytes 131104 | tf_op jit(solution)/shard_map/ppermute | solution.py:20
  31.4 10.1 %all-to-all-done = bf16[32,48,512]{2,1,0:T(8,128)(2,1)S(1)} async-done(((bf16[32,48,512]{2,1,0:T(8,128)(2,1)}), bf16[32,48,512]{2,1,0:T(8,128)(2,1)S(1)}, u32[]{:S(2)}, u32[]{:S(2)}) %all-to-all-start) | async-done | bytes 1572896 | tf_op jit(solution)/shard_map/all_to_all | solution.py:459
  46.6 32.2 %collective-permute-done.3.x3.refs_4_ = bf16[4,2,192,512]{3,2,1,0:T(8,128)(2,1)S(1)} collective-permute-done((bf16[4,2,192,512]{3,2,1,0:T(8,128)(2,1)S(1)}, bf16[4,2,192,512]{3,2,1,0:T(8,128)(2,1)S(1)}, u32[]{:S(2)}, u32[]{:S(2)}) %collective-permute-start.3) | collective-permute-done | bytes 1572896 | tf_op jit(solution)/shard_map/ppermute | solution.py:20
  81.6 2.8 %collective-permute-start.6 = (bf16[2,2,192,512]{3,2,1,0:T(8,128)(2,1)}, bf16[2,2,192,512]{3,2,1,0:T(8,128)(2,1)}, u32[]{:S(2)}, u32[]{:S(2)}) collective-permute-start(bf16[2,2,192,512]{3,2,1,0:T(8,128)(2,1)} %slice.89), channel_id=1, source_target_pairs={{1,0},{2,1},{3,2},{0,3},{5,4},{6,5},{7,6},{4,7},{9,8},{10,9},{11,1... | collective-permute-start | bytes 2359304 | tf_op jit(solution)/shard_map/ppermute | solution.py:20
  84.5 1.9 copy-done.9
  90.8 3.8 %shard_map.111 = (f32[4,384,192]{2,1,0:T(8,128)S(1)}, f32[4,384,192]{2,1,0:T(8,128)S(1)}) custom-call(s32[4]{0:T(128)S(1)} %pad_add_fusion.ids_ref, bf16[4,2,192,512]{3,2,1,0:T(8,128)(2,1)S(1)} %copy-done.15, bf16[4,2,192,512]{3,2,1,0:T(8,128)(2,1)S(1)} %copy-done.22, bf16[4,2,192,512]{3,2,1,0:T(8,128)(2,1)S(1)} %copy-done.19, ...), custom_call_target="tpu_custom_call" | custom-call | flops 3623878656 | bytes 14680064 | tf_op jit(solution)/shard_map/pallas_call | solution.py:320
  94.6 4.4 %collective-permute-done.4.lo.refs_2_ = bf16[2,2,192,512]{3,2,1,0:T(8,128)(2,1)} collective-permute-done((bf16[2,2,192,512]{3,2,1,0:T(8,128)(2,1)}, bf16[2,2,192,512]{3,2,1,0:T(8,128)(2,1)}, u32[]{:S(2)}, u32[]{:S(2)}) %collective-permute-start.4) | collective-permute-done | bytes 786464 | tf_op jit(solution)/shard_map/ppermute | solution.py:20
  99.7 5.8 %shard_map.112 = (bf16[4,192,2048]{2,1,0:T(8,128)(2,1)S(1)}, bf16[4,192,2048]{2,1,0:T(8,128)(2,1)S(1)}, bf16[4,384,192]{2,1,0:T(8,128)(2,1)S(1)}, f32[4,384,192]{2,1,0:T(8,128)S(1)}, f32[4,384,192]{2,1,0:T(8,128)S(1)}) custom-call(s32[4]{0:T(128)S(1)} %pad_add_fusion.ids_ref, bf16[2,2,192,512]{3,2,1,0:T(8,128)(2,1)} %collective-permute-done.4.lo.refs_2_, ...), custom_call_target="tpu_custom_call" | custom-call | flops 3623878656 | bytes 18874368 | tf_op jit(solution)/shard_map/pallas_call | solution.py:320
  111.7 3.5 %copy-done.24 = bf16[8448,512]{1,0:T(8,128)(2,1)S(1)} copy-done((bf16[8448,512]{1,0:T(8,128)(2,1)S(1)}, bf16[8448,512]{1,0:T(8,128)(2,1)}, u32[]{:S(2)}) %copy-start.24) | copy-done | bytes 8650776
  115.2 7.6 %shard_map.113 = (bf16[4,192,2048]{2,1,0:T(8,128)(2,1)S(1)}, bf16[4,192,2048]{2,1,0:T(8,128)(2,1)S(1)}, bf16[4,384,512]{2,1,0:T(8,128)(2,1)S(1)}) custom-call(s32[4]{0:T(128)S(1)} %pad_add_fusion.ids_ref, bf16[16,528,512]{2,1,0:T(8,128)(2,1)S(1)} %bitcast.48), custom_call_target="tpu_custom_call" | custom-call | flops 4294967296 | bytes 18874368 | tf_op jit(solution)/shard_map/pallas_call | solution.py:105
  123.5 3.3 %shard_map.114 = (bf16[2,2,128,512]{3,2,1,0:T(8,128)(2,1)S(1)}, bf16[2,2,128,512]{3,2,1,0:T(8,128)(2,1)S(1)}, bf16[2,2,128,512]{3,2,1,0:T(8,128)(2,1)S(1)}, bf16[2,2,128,512]{3,2,1,0:T(8,128)(2,1)S(1)}) custom-call(s32[4]{0:T(128)S(1)} %pad_add_fusion.ids_ref, bf16[4,384,512]{2,1,0:T(8,128)(2,1)S(1)} %get-tuple-element.79.map_ref.map2_ref, ...), custom_call_target="tpu_custom_call" | custom-call | flops 1073741824 | bytes 4194304 | tf_op jit(solution)/shard_map/pallas_call | solution.py:195
  126.8 1.9 collective-permute-done.8.sib.refs_6_
  132.0 10.8 %shard_map.115 = (bf16[4,384,192]{2,1,0:T(8,128)(2,1)S(1)}, bf16[4,384,192]{2,1,0:T(8,128)(2,1)S(1)}, bf16[4,4,2,192,512]{4,3,2,1,0:T(8,128)(2,1)}) custom-call(s32[4]{0:T(128)S(1)} %pad_add_fusion.ids_ref, bf16[4,192,2048]{2,1,0:T(8,128)(2,1)S(1)} %get-tuple-element.75.own.refs_5_, bf16[4,192,2048]{2,1,0:T(8,128)(2,1)S(1)} %collective-permute-done.8.sib.refs_6_, ...), custom_call_target="tpu_custom_call" | custom-call | flops 5435817984 | bytes 27262976 | tf_op jit(solution)/shard_map/pallas_call | solution.py:320
  149.4 1.9 collective-permute-start.12
  155.0 6.2 %shard_map.116 = (bf16[4,2,128,512]{3,2,1,0:T(8,128)(2,1)S(1)}, bf16[4,2,128,512]{3,2,1,0:T(8,128)(2,1)S(1)}, bf16[4,2,128,512]{3,2,1,0:T(8,128)(2,1)S(1)}, bf16...) custom-call(s32[4]{0:T(128)S(1)} %pad_add_fusion.ids_ref, ...), custom_call_target="tpu_custom_call" | custom-call | flops 3221225472 | bytes 12582912 | tf_op jit(solution)/shard_map/pallas_call | solution.py:195
  161.2 2.1 collective-permute-done.11
  166.6 3.0 %collective-permute-start.16 = (bf16[4,2,128,512]{3,2,1,0:T(8,128)(2,1)S(1)}, bf16[4,2,128,512]{3,2,1,0:T(8,128)(2,1)S(1)}, u32[]{:S(2)}, u32[]{:S(2)}) collective-permute-start(bf16[4,2,128,512]{3,2,1,0:T(8,128)(2,1)S(1)} %pad_maximum_fusion.3), channel_id=1, source_target_pairs={{4,0},{8,4},{12,8},{0,12},{5,1},{9,5},{13,9},{1,13},{6,2},{10,6},{... | collective-permute-start | bytes 3145736 | tf_op jit(solution)/shard_map/ppermute | solution.py:20
  169.6 8.8 %shard_map.117 = (bf16[4,192,2048]{2,1,0:T(8,128)(2,1)}, bf16[4,192,2048]{2,1,0:T(8,128)(2,1)}, bf16[4,192,2048]{2,1,0:T(8,128)(2,1)}) custom-call(s32[4]{0:T(128)S(1)} %pad_add_fusion.ids_ref, bf16[4,2,192,512]{3,2,1,0:T(8,128)(2,1)S(1)} %copy-done.16, bf16[4,2,192,512]{3,2,1,0:T(8,128)(2,1)S(1)} %copy-done.23, ...), custom_call_target="tpu_custom_call" | custom-call | flops 5435817984 | bytes 25165824 | tf_op jit(solution)/shard_map/pallas_call | solution.py:320
  178.5 10.4 %collective-permute-done.14 = bf16[4,2,128,512]{3,2,1,0:T(8,128)(2,1)S(1)} collective-permute-done((bf16[4,2,128,512]{3,2,1,0:T(8,128)(2,1)S(1)}, bf16[4,2,128,512]{3,2,1,0:T(8,128)(2,1)S(1)}, u32[]{:S(2)}, u32[]{:S(2)}) %collective-permute-start.14) | collective-permute-done | bytes 1048608 | tf_op jit(solution)/shard_map/ppermute | solution.py:20
  188.9 2.5 collective-permute-done.13
  191.9 2.1 collective-permute-done.15
  196.7 2.8 %collective-permute-start.22 = (bf16[2,128,512]{2,1,0:T(8,128)(2,1)S(1)}, bf16[2,128,512]{2,1,0:T(8,128)(2,1)S(1)}, u32[]{:S(2)}, u32[]{:S(2)}) collective-permute-start(bf16[2,128,512]{2,1,0:T(8,128)(2,1)S(1)} %get-tuple-element.134), channel_id=1, source_target_pairs={{32,0},{64,32},{96,64},{0,96},{33,1},{65,33},{97,65},{1,97},{34,2}... | collective-permute-start | bytes 786440 | tf_op jit(solution)/shard_map/ppermute | solution.py:20
  199.5 3.4 %collective-permute-done.19 = bf16[2,128,512]{2,1,0:T(8,128)(2,1)S(1)} collective-permute-done((bf16[2,128,512]{2,1,0:T(8,128)(2,1)S(1)}, bf16[2,128,512]{2,1,0:T(8,128)(2,1)S(1)}, u32[]{:S(2)}, u32[]{:S(2)}) %collective-permute-start.19) | collective-permute-done | bytes 262176 | tf_op jit(solution)/shard_map/ppermute | solution.py:20
  203.2 2.1 collective-permute-done.18
  205.3 2.7 %collective-permute-done.17 = bf16[2,128,512]{2,1,0:T(8,128)(2,1)S(1)} collective-permute-done((bf16[2,128,512]{2,1,0:T(8,128)(2,1)S(1)}, bf16[2,128,512]{2,1,0:T(8,128)(2,1)S(1)}, u32[]{:S(2)}, u32[]{:S(2)}) %collective-permute-start.17) | collective-permute-done | bytes 262176 | tf_op jit(solution)/shard_map/ppermute | solution.py:20
  208.6 2.7 %collective-permute-done.20 = bf16[2,128,512]{2,1,0:T(8,128)(2,1)S(1)} collective-permute-done((bf16[2,128,512]{2,1,0:T(8,128)(2,1)S(1)}, bf16[2,128,512]{2,1,0:T(8,128)(2,1)S(1)}, u32[]{:S(2)}, u32[]{:S(2)}) %collective-permute-start.20) | collective-permute-done | bytes 262176 | tf_op jit(solution)/shard_map/ppermute | solution.py:20
  214.6 5.6 %all-to-all-start.1 = ((bf16[32,48,512]{2,1,0:T(8,128)(2,1)}), bf16[32,48,512]{2,1,0:T(8,128)(2,1)S(1)}, u32[]{:S(2)}, u32[]{:S(2)}) async-start(bf16[32,48,512]{2,1,0:T(8,128)(2,1)} %bitcast.24), calls=%async_computation.2 | async-start | bytes 3145728 | tf_op jit(solution)/shard_map/all_to_all | solution.py:459
  220.3 2.7 %collective-permute-start.25 = (bf16[128,512]{1,0:T(8,128)(2,1)S(1)}, bf16[128,512]{1,0:T(8,128)(2,1)S(1)}, u32[]{:S(2)}, u32[]{:S(2)}) collective-permute-start(bf16[128,512]{1,0:T(8,128)(2,1)S(1)} %get-tuple-element.140), channel_id=1, source_target_pairs={{1,0},{2,1},{3,2},{0,3},{5,4},{6,5},{7,6},{4,7},{9,8},{10,9},{11,1... | collective-permute-start | bytes 393224 | tf_op jit(solution)/shard_map/ppermute | solution.py:20
  224.5 4.5 %collective-permute-done.25 = bf16[128,512]{1,0:T(8,128)(2,1)S(1)} collective-permute-done((bf16[128,512]{1,0:T(8,128)(2,1)S(1)}, bf16[128,512]{1,0:T(8,128)(2,1)S(1)}, u32[]{:S(2)}, u32[]{:S(2)}) %collective-permute-start.25) | collective-permute-done | bytes 131104 | tf_op jit(solution)/shard_map/ppermute | solution.py:20
  233.5 9.5 %all-to-all-done.1 = bf16[32,48,512]{2,1,0:T(8,128)(2,1)S(1)} async-done(((bf16[32,48,512]{2,1,0:T(8,128)(2,1)}), bf16[32,48,512]{2,1,0:T(8,128)(2,1)S(1)}, u32[]{:S(2)}, u32[]{:S(2)}) %all-to-all-start.1) | async-done | bytes 1572896 | tf_op jit(solution)/shard_map/all_to_all | solution.py:459
  (170 shorter events, 59.4 us)
Async XLA Ops:
  10.2 31.3 %all-to-all-start = ((bf16[32,48,512]{2,1,0:T(8,128)(2,1)}), bf16[32,48,512]{2,1,0:T(8,128)(2,1)S(1)}, u32[]{:S(2)}, u32[]{:S(2)}) async-start(bf16[32,48,512]{2,1,0:T(8,128)(2,1)} %bitcast.5), calls=%async_computation | async-start | bytes 3145728 | tf_op jit(solution)/shard_map/all_to_all | solution.py:459
  18.8 92.9 %all-gather.3.cloned.1.call-start = ((), (), s32[]{:S(2)}) async-start(), calls=%async_computation.4 | async-start | bytes 9191424 | tf_op jit(solution)/shard_map/all_gather | solution.py:467
  18.8 8.9 %collective-permute-start = (bf16[128,512]{1,0:T(8,128)(2,1)S(1)}, bf16[128,512]{1,0:T(8,128)(2,1)S(1)}, u32[]{:S(2)}, u32[]{:S(2)}) collective-permute-start(bf16[128,512]{1,0:T(8,128)(2,1)S(1)} %copy-done.45), channel_id=1, source_target_pairs={{1,0},{2,1},{3,2},{0,3},{5,4},{6,5},{7,6},{4,7},{9,8},{10,9},{11,1... | collective-permute-start | bytes 393224 | tf_op jit(solution)/shard_map/ppermute | solution.py:20
  21.7 7.9 %collective-permute-start.1 = (bf16[128,512]{1,0:T(8,128)(2,1)S(1)}, bf16[128,512]{1,0:T(8,128)(2,1)S(1)}, u32[]{:S(2)}, u32[]{:S(2)}) collective-permute-start(bf16[128,512]{1,0:T(8,128)(2,1)S(1)} %copy-done.45), channel_id=1, source_target_pairs={{2,0},{3,1},{0,2},{1,3},{6,4},{7,5},{4,6},{5,7},{10,8},{11,9},{8,1... | collective-permute-start | bytes 393224 | tf_op jit(solution)/shard_map/ppermute | solution.py:20
  22.5 8.9 %collective-permute-start.2 = (bf16[128,512]{1,0:T(8,128)(2,1)S(1)}, bf16[128,512]{1,0:T(8,128)(2,1)S(1)}, u32[]{:S(2)}, u32[]{:S(2)}) collective-permute-start(bf16[128,512]{1,0:T(8,128)(2,1)S(1)} %copy-done.45), channel_id=1, source_target_pairs={{3,0},{0,1},{1,2},{2,3},{7,4},{4,5},{5,6},{6,7},{11,8},{8,9},{9,10... | collective-permute-start | bytes 393224 | tf_op jit(solution)/shard_map/ppermute | solution.py:20
  41.5 169.9 %reduce-scatter.2.cloned.1.call-start = ((), (), s32[]{:S(2)}) async-start(), calls=%async_computation.3 | async-start | bytes 7864320 | tf_op jit(solution)/shard_map/reduce_scatter | solution.py:488
  42.2 42.4 %copy-start.6 = (bf16[4,192,2048]{2,1,0:T(8,128)(2,1)S(1)}, bf16[4,192,2048]{2,1,0:T(8,128)(2,1)}, u32[]{:S(2)}) copy-start(bf16[4,192,2048]{2,1,0:T(8,128)(2,1)} %wg.3) | copy-start | bytes 9437188
  42.2 36.6 %collective-permute-start.3 = (bf16[4,2,192,512]{3,2,1,0:T(8,128)(2,1)S(1)}, bf16[4,2,192,512]{3,2,1,0:T(8,128)(2,1)S(1)}, u32[]{:S(2)}, u32[]{:S(2)}) collective-permute-start(bf16[4,2,192,512]{3,2,1,0:T(8,128)(2,1)S(1)} %shard_map.110.x0.refs_0_), channel_id=1, source_target_pairs={{3,0},{0,1},{1,2},{2,3},{7,4},{4,5},{5,6},{6,7},{11,8},{8,9},{9,10... | collective-permute-start | bytes 4718600 | tf_op jit(solution)/shard_map/ppermute | solution.py:20
  43.7 36.4 %collective-permute-start.5 = (bf16[4,2,192,512]{3,2,1,0:T(8,128)(2,1)S(1)}, bf16[4,2,192,512]{3,2,1,0:T(8,128)(2,1)S(1)}, u32[]{:S(2)}, u32[]{:S(2)}) collective-permute-start(bf16[4,2,192,512]{3,2,1,0:T(8,128)(2,1)S(1)} %shard_map.110.x0.refs_0_), channel_id=1, source_target_pairs={{1,0},{2,1},{3,2},{0,3},{5,4},{6,5},{7,6},{4,7},{9,8},{10,9},{11,1... | collective-permute-start | bytes 4718600 | tf_op jit(solution)/shard_map/ppermute | solution.py:20
  79.8 19.2 %collective-permute-start.4 = (bf16[2,2,192,512]{3,2,1,0:T(8,128)(2,1)}, bf16[2,2,192,512]{3,2,1,0:T(8,128)(2,1)}, u32[]{:S(2)}, u32[]{:S(2)}) collective-permute-start(bf16[2,2,192,512]{3,2,1,0:T(8,128)(2,1)} %slice.88), channel_id=1, source_target_pairs={{3,0},{0,1},{1,2},{2,3},{7,4},{4,5},{5,6},{6,7},{11,8},{8,9},{9,10... | collective-permute-start | bytes 2359304 | tf_op jit(solution)/shard_map/ppermute | solution.py:20
  81.6 18.1 %collective-permute-start.6 = (bf16[2,2,192,512]{3,2,1,0:T(8,128)(2,1)}, bf16[2,2,192,512]{3,2,1,0:T(8,128)(2,1)}, u32[]{:S(2)}, u32[]{:S(2)}) collective-permute-start(bf16[2,2,192,512]{3,2,1,0:T(8,128)(2,1)} %slice.89), channel_id=1, source_target_pairs={{1,0},{2,1},{3,2},{0,3},{5,4},{6,5},{7,6},{4,7},{9,8},{10,9},{11,1... | collective-permute-start | bytes 2359304 | tf_op jit(solution)/shard_map/ppermute | solution.py:20
  111.7 11.1 %collective-permute-start.7 = (bf16[4,192,2048]{2,1,0:T(8,128)(2,1)}, bf16[4,192,2048]{2,1,0:T(8,128)(2,1)S(1)}, u32[]{:S(2)}, u32[]{:S(2)}) collective-permute-start(bf16[4,192,2048]{2,1,0:T(8,128)(2,1)} %copy-done.27), channel_id=1, source_target_pairs={{16,0},{0,16},{17,1},{1,17},{18,2},{2,18},{19,3},{3,19},{20,4},{4,... | collective-permute-start | bytes 9437192 | tf_op jit(solution)/shard_map/ppermute | solution.py:20
  122.9 5.9 %collective-permute-start.8 = (bf16[4,192,2048]{2,1,0:T(8,128)(2,1)S(1)}, bf16[4,192,2048]{2,1,0:T(8,128)(2,1)S(1)}, u32[]{:S(2)}, u32[]{:S(2)}) collective-permute-start(bf16[4,192,2048]{2,1,0:T(8,128)(2,1)S(1)} %get-tuple-element.78), channel_id=1, source_target_pairs={{16,0},{0,16},{17,1},{1,17},{18,2},{2,18},{19,3},{3,19},{20,4},{4,... | collective-permute-start | bytes 9437192 | tf_op jit(solution)/shard_map/ppermute | solution.py:20
  144.7 16.5 %collective-permute-start.9 = (bf16[2,2,128,512]{3,2,1,0:T(8,128)(2,1)}, bf16[2,2,128,512]{3,2,1,0:T(8,128)(2,1)S(1)}, u32[]{:S(2)}, u32[]{:S(2)}) collective-permute-start(bf16[2,2,128,512]{3,2,1,0:T(8,128)(2,1)} %copy-done.37), channel_id=1, source_target_pairs={{96,0},{0,32},{32,64},{64,96},{97,1},{1,33},{33,65},{65,97},{98,2}... | collective-permute-start | bytes 1572872 | tf_op jit(solution)/shard_map/ppermute | solution.py:20
  146.3 14.9 %collective-permute-start.10 = (bf16[2,2,128,512]{3,2,1,0:T(8,128)(2,1)}, bf16[2,2,128,512]{3,2,1,0:T(8,128)(2,1)S(1)}, u32[]{:S(2)}, u32[]{:S(2)}) collective-permute-start(bf16[2,2,128,512]{3,2,1,0:T(8,128)(2,1)} %copy-done.36), channel_id=1, source_target_pairs={{32,0},{64,32},{96,64},{0,96},{33,1},{65,33},{97,65},{1,97},{34,2}... | collective-permute-start | bytes 1572872 | tf_op jit(solution)/shard_map/ppermute | solution.py:20
  148.0 15.2 %collective-permute-start.11 = (bf16[2,2,128,512]{3,2,1,0:T(8,128)(2,1)}, bf16[2,2,128,512]{3,2,1,0:T(8,128)(2,1)S(1)}, u32[]{:S(2)}, u32[]{:S(2)}) collective-permute-start(bf16[2,2,128,512]{3,2,1,0:T(8,128)(2,1)} %copy-done.35), channel_id=1, source_target_pairs={{12,0},{0,4},{4,8},{8,12},{13,1},{1,5},{5,9},{9,13},{14,2},{2,6},{... | collective-permute-start | bytes 1572872 | tf_op jit(solution)/shard_map/ppermute | solution.py:20
  149.4 13.9 %collective-permute-start.12 = (bf16[2,2,128,512]{3,2,1,0:T(8,128)(2,1)}, bf16[2,2,128,512]{3,2,1,0:T(8,128)(2,1)S(1)}, u32[]{:S(2)}, u32[]{:S(2)}) collective-permute-start(bf16[2,2,128,512]{3,2,1,0:T(8,128)(2,1)} %copy-done.34), channel_id=1, source_target_pairs={{4,0},{8,4},{12,8},{0,12},{5,1},{9,5},{13,9},{1,13},{6,2},{10,6},{... | collective-permute-start | bytes 1572872 | tf_op jit(solution)/shard_map/ppermute | solution.py:20
  164.5 24.4 %collective-permute-start.14 = (bf16[4,2,128,512]{3,2,1,0:T(8,128)(2,1)S(1)}, bf16[4,2,128,512]{3,2,1,0:T(8,128)(2,1)S(1)}, u32[]{:S(2)}, u32[]{:S(2)}) collective-permute-start(bf16[4,2,128,512]{3,2,1,0:T(8,128)(2,1)S(1)} %pad_maximum_fusion.1), channel_id=1, source_target_pairs={{32,0},{64,32},{96,64},{0,96},{33,1},{65,33},{97,65},{1,97},{34,2}... | collective-permute-start | bytes 3145736 | tf_op jit(solution)/shard_map/ppermute | solution.py:20
  166.1 25.2 %collective-permute-start.13 = (bf16[4,2,128,512]{3,2,1,0:T(8,128)(2,1)S(1)}, bf16[4,2,128,512]{3,2,1,0:T(8,128)(2,1)S(1)}, u32[]{:S(2)}, u32[]{:S(2)}) collective-permute-start(bf16[4,2,128,512]{3,2,1,0:T(8,128)(2,1)S(1)} %pad_maximum_fusion), channel_id=1, source_target_pairs={{96,0},{0,32},{32,64},{64,96},{97,1},{1,33},{33,65},{65,97},{98,2}... | collective-permute-start | bytes 3145736 | tf_op jit(solution)/shard_map/ppermute | solution.py:20
  166.6 25.2 %collective-permute-start.16 = (bf16[4,2,128,512]{3,2,1,0:T(8,128)(2,1)S(1)}, bf16[4,2,128,512]{3,2,1,0:T(8,128)(2,1)S(1)}, u32[]{:S(2)}, u32[]{:S(2)}) collective-permute-start(bf16[4,2,128,512]{3,2,1,0:T(8,128)(2,1)S(1)} %pad_maximum_fusion.3), channel_id=1, source_target_pairs={{4,0},{8,4},{12,8},{0,12},{5,1},{9,5},{13,9},{1,13},{6,2},{10,6},{... | collective-permute-start | bytes 3145736 | tf_op jit(solution)/shard_map/ppermute | solution.py:20
  169.6 24.4 %collective-permute-start.15 = (bf16[4,2,128,512]{3,2,1,0:T(8,128)(2,1)S(1)}, bf16[4,2,128,512]{3,2,1,0:T(8,128)(2,1)S(1)}, u32[]{:S(2)}, u32[]{:S(2)}) collective-permute-start(bf16[4,2,128,512]{3,2,1,0:T(8,128)(2,1)S(1)} %pad_maximum_fusion.2), channel_id=1, source_target_pairs={{12,0},{0,4},{4,8},{8,12},{13,1},{1,5},{5,9},{9,13},{14,2},{2,6},{... | collective-permute-start | bytes 3145736 | tf_op jit(solution)/shard_map/ppermute | solution.py:20
  194.5 8.4 %collective-permute-start.19 = (bf16[2,128,512]{2,1,0:T(8,128)(2,1)S(1)}, bf16[2,128,512]{2,1,0:T(8,128)(2,1)S(1)}, u32[]{:S(2)}, u32[]{:S(2)}) collective-permute-start(bf16[2,128,512]{2,1,0:T(8,128)(2,1)S(1)} %get-tuple-element.137), channel_id=1, source_target_pairs={{4,0},{8,4},{12,8},{0,12},{5,1},{9,5},{13,9},{1,13},{6,2},{10,6},{... | collective-permute-start | bytes 786440 | tf_op jit(solution)/shard_map/ppermute | solution.py:20
  195.1 10.2 %collective-permute-start.18 = (bf16[2,128,512]{2,1,0:T(8,128)(2,1)S(1)}, bf16[2,128,512]{2,1,0:T(8,128)(2,1)S(1)}, u32[]{:S(2)}, u32[]{:S(2)}) collective-permute-start(bf16[2,128,512]{2,1,0:T(8,128)(2,1)S(1)} %get-tuple-element.138), channel_id=1, source_target_pairs={{8,0},{12,4},{0,8},{4,12},{9,1},{13,5},{1,9},{5,13},{10,2},{14,6},... | collective-permute-start | bytes 786440 | tf_op jit(solution)/shard_map/ppermute | solution.py:20
  195.7 12.3 %collective-permute-start.17 = (bf16[2,128,512]{2,1,0:T(8,128)(2,1)S(1)}, bf16[2,128,512]{2,1,0:T(8,128)(2,1)S(1)}, u32[]{:S(2)}, u32[]{:S(2)}) collective-permute-start(bf16[2,128,512]{2,1,0:T(8,128)(2,1)S(1)} %get-tuple-element.136), channel_id=1, source_target_pairs={{12,0},{0,4},{4,8},{8,12},{13,1},{1,5},{5,9},{9,13},{14,2},{2,6},{... | collective-permute-start | bytes 786440 | tf_op jit(solution)/shard_map/ppermute | solution.py:20
  196.7 11.5 %collective-permute-start.22 = (bf16[2,128,512]{2,1,0:T(8,128)(2,1)S(1)}, bf16[2,128,512]{2,1,0:T(8,128)(2,1)S(1)}, u32[]{:S(2)}, u32[]{:S(2)}) collective-permute-start(bf16[2,128,512]{2,1,0:T(8,128)(2,1)S(1)} %get-tuple-element.134), channel_id=1, source_target_pairs={{32,0},{64,32},{96,64},{0,96},{33,1},{65,33},{97,65},{1,97},{34,2}... | collective-permute-start | bytes 786440 | tf_op jit(solution)/shard_map/ppermute | solution.py:20
  199.5 9.1 %collective-permute-start.21 = (bf16[2,128,512]{2,1,0:T(8,128)(2,1)S(1)}, bf16[2,128,512]{2,1,0:T(8,128)(2,1)S(1)}, u32[]{:S(2)}, u32[]{:S(2)}) collective-permute-start(bf16[2,128,512]{2,1,0:T(8,128)(2,1)S(1)} %get-tuple-element.135), channel_id=1, source_target_pairs={{64,0},{96,32},{0,64},{32,96},{65,1},{97,33},{1,65},{33,97},{66,2}... | collective-permute-start | bytes 786440 | tf_op jit(solution)/shard_map/ppermute | solution.py:20
  202.9 8.4 %collective-permute-start.20 = (bf16[2,128,512]{2,1,0:T(8,128)(2,1)S(1)}, bf16[2,128,512]{2,1,0:T(8,128)(2,1)S(1)}, u32[]{:S(2)}, u32[]{:S(2)}) collective-permute-start(bf16[2,128,512]{2,1,0:T(8,128)(2,1)S(1)} %get-tuple-element.133), channel_id=1, source_target_pairs={{96,0},{0,32},{32,64},{64,96},{97,1},{1,33},{33,65},{65,97},{98,2}... | collective-permute-start | bytes 786440 | tf_op jit(solution)/shard_map/ppermute | solution.py:20
  214.6 28.3 %all-to-all-start.1 = ((bf16[32,48,512]{2,1,0:T(8,128)(2,1)}), bf16[32,48,512]{2,1,0:T(8,128)(2,1)S(1)}, u32[]{:S(2)}, u32[]{:S(2)}) async-start(bf16[32,48,512]{2,1,0:T(8,128)(2,1)} %bitcast.24), calls=%async_computation.2 | async-start | bytes 3145728 | tf_op jit(solution)/shard_map/all_to_all | solution.py:459
  220.2 23.8 %copy-start.1 = (bf16[128,512]{1,0:T(8,128)(2,1)S(1)}, bf16[128,512]{1,0:T(8,128)(2,1)}, u32[]{:S(2)}) copy-start(bf16[128,512]{1,0:T(8,128)(2,1)} %param.7) | copy-start | bytes 393220
  220.3 8.8 %collective-permute-start.25 = (bf16[128,512]{1,0:T(8,128)(2,1)S(1)}, bf16[128,512]{1,0:T(8,128)(2,1)S(1)}, u32[]{:S(2)}, u32[]{:S(2)}) collective-permute-start(bf16[128,512]{1,0:T(8,128)(2,1)S(1)} %get-tuple-element.140), channel_id=1, source_target_pairs={{1,0},{2,1},{3,2},{0,3},{5,4},{6,5},{7,6},{4,7},{9,8},{10,9},{11,1... | collective-permute-start | bytes 393224 | tf_op jit(solution)/shard_map/ppermute | solution.py:20
  223.0 7.9 %collective-permute-start.24 = (bf16[128,512]{1,0:T(8,128)(2,1)S(1)}, bf16[128,512]{1,0:T(8,128)(2,1)S(1)}, u32[]{:S(2)}, u32[]{:S(2)}) collective-permute-start(bf16[128,512]{1,0:T(8,128)(2,1)S(1)} %get-tuple-element.139), channel_id=1, source_target_pairs={{2,0},{3,1},{0,2},{1,3},{6,4},{7,5},{4,6},{5,7},{10,8},{11,9},{8,1... | collective-permute-start | bytes 393224 | tf_op jit(solution)/shard_map/ppermute | solution.py:20
  223.6 9.2 %collective-permute-start.23 = (bf16[128,512]{1,0:T(8,128)(2,1)S(1)}, bf16[128,512]{1,0:T(8,128)(2,1)S(1)}, u32[]{:S(2)}, u32[]{:S(2)}) collective-permute-start(bf16[128,512]{1,0:T(8,128)(2,1)S(1)} %slice_bitcast_fusion.8), channel_id=1, source_target_pairs={{3,0},{0,1},{1,2},{2,3},{7,4},{4,5},{5,6},{6,7},{11,8},{8,9},{9,10... | collective-permute-start | bytes 393224 | tf_op jit(solution)/shard_map/ppermute | solution.py:20
  (46 other events, 282.3 us)
Sparse Core Ops, SparseCore 0:
  41.6 70.0 all-gather.2
  144.9 63.6 reduce-scatter.1

commit v6 on v5

--- a/solution.py
+++ b/solution.py
@@ -12,7 +12,7 @@
 F32 = jnp.float32
 CAP = 12
 GROUP = ("y", "c", "z")
-VMEM_LIMIT = 30 * 1024 * 1024
+VMEM_LIMIT = 20 * 1024 * 1024
 
 
 def fetch(a, axis, r):

time: 252 us -> 256 us (1.016)
  local copies, waits for them, and re-layouts: 29 us -> 32.2 us
    unnamed x100, local copies, waits for them, and re-layouts: 26.7 us -> 29.9 us
  transfers between devices with their start and end apart: 30 -> 30, of which waited for: 22 -> 23; matrix products, arithmetic and copies ran while one was open for 2% -> 2% of each run, Pallas kernels for 14% -> 14%
where the time goes in v6:
time: 256 us; the launch traced here: 255 us
  waiting for transfers between devices  107 us (42%)
  Pallas kernels  47.9 us (19%)
  starting transfers between devices  46.9 us (18%)
  local copies, waits for them, and re-layouts  32.2 us (13%)
  between operations  14.7 us (6%)
  other arithmetic  3.66 us (1%)
  matrix products  3.29 us (1%)
    ppermute x26, waiting for transfers between devices, fetch(): return lax.ppermute(a, axis, [((i + r) % n, i) for i in range(n)])  85.5 us
    ppermute x26, starting transfers between devices, fetch(): return lax.ppermute(a, axis, [((i + r) % n, i) for i in range(n)])  32.7 us
    unnamed x100, local copies, waits for them, and re-layouts  29.9 us
    pallas_call x4, Pallas kernels, per_expert(): pl.pallas_call(kernel, grid_spec=pltpu.PrefetchScalarGridSpec(num_scalar_...  28.5 us
    all_to_all x2, waiting for transfers between devices, exchange(): return lax.all_to_all(a, GROUP, split_axis=0, concat_axis=0, tiled=True)  19.6 us
    all_to_all x2, starting transfers between devices, exchange(): return lax.all_to_all(a, GROUP, split_axis=0, concat_axis=0, tiled=True)  14.1 us
    pallas_call x2, Pallas kernels, call(): pl.pallas_call(kernel, grid_spec=pltpu.PrefetchScalarGridSpec(num_scalar_...  9.42 us
    pallas_call x1, Pallas kernels, pick(): pl.pallas_call(pick_kernel, grid=(4,), out_shape=(rows, rows, maps), in_s...  7.65 us
  transfers between devices with their start and end apart: 30, of which 23 were waited for; matrix products, arithmetic and copies ran while one was open for 2% of the time, Pallas kernels for 14%

profile of v6, /device:TPU:0, one launch (start us, length us, event | category | flops | bytes accessed | tf_op | source)
XLA Modules:
  0.0 255.1 jit_solution(10401246681619028818)
XLA Ops:
  10.2 8.5 %all-to-all-start = ((bf16[32,48,512]{2,1,0:T(8,128)(2,1)}), bf16[32,48,512]{2,1,0:T(8,128)(2,1)S(1)}, u32[]{:S(2)}, u32[]{:S(2)}) async-start(bf16[32,48,512]{2,1,0:T(8,128)(2,1)} %bitcast.5), calls=%async_computation | async-start | bytes 3145728 | tf_op jit(solution)/shard_map/all_to_all | solution.py:459
  18.8 2.8 %collective-permute-start = (bf16[128,512]{1,0:T(8,128)(2,1)S(1)}, bf16[128,512]{1,0:T(8,128)(2,1)S(1)}, u32[]{:S(2)}, u32[]{:S(2)}) collective-permute-start(bf16[128,512]{1,0:T(8,128)(2,1)S(1)} %copy-done.45), channel_id=1, source_target_pairs={{1,0},{2,1},{3,2},{0,3},{5,4},{6,5},{7,6},{4,7},{9,8},{10,9},{11,1... | collective-permute-start | bytes 393224 | tf_op jit(solution)/shard_map/ppermute | solution.py:20
  23.4 4.3 %collective-permute-done = bf16[128,512]{1,0:T(8,128)(2,1)S(1)} collective-permute-done((bf16[128,512]{1,0:T(8,128)(2,1)S(1)}, bf16[128,512]{1,0:T(8,128)(2,1)S(1)}, u32[]{:S(2)}, u32[]{:S(2)}) %collective-permute-start) | collective-permute-done | bytes 131104 | tf_op jit(solution)/shard_map/ppermute | solution.py:20
  31.4 10.1 %all-to-all-done = bf16[32,48,512]{2,1,0:T(8,128)(2,1)S(1)} async-done(((bf16[32,48,512]{2,1,0:T(8,128)(2,1)}), bf16[32,48,512]{2,1,0:T(8,128)(2,1)S(1)}, u32[]{:S(2)}, u32[]{:S(2)}) %all-to-all-start) | async-done | bytes 1572896 | tf_op jit(solution)/shard_map/all_to_all | solution.py:459
  46.6 32.2 %collective-permute-done.3.x3.refs_4_ = bf16[4,2,192,512]{3,2,1,0:T(8,128)(2,1)S(1)} collective-permute-done((bf16[4,2,192,512]{3,2,1,0:T(8,128)(2,1)S(1)}, bf16[4,2,192,512]{3,2,1,0:T(8,128)(2,1)S(1)}, u32[]{:S(2)}, u32[]{:S(2)}) %collective-permute-start.3) | collective-permute-done | bytes 1572896 | tf_op jit(solution)/shard_map/ppermute | solution.py:20
  81.6 2.8 %collective-permute-start.6 = (bf16[2,2,192,512]{3,2,1,0:T(8,128)(2,1)}, bf16[2,2,192,512]{3,2,1,0:T(8,128)(2,1)}, u32[]{:S(2)}, u32[]{:S(2)}) collective-permute-start(bf16[2,2,192,512]{3,2,1,0:T(8,128)(2,1)} %slice.89), channel_id=1, source_target_pairs={{1,0},{2,1},{3,2},{0,3},{5,4},{6,5},{7,6},{4,7},{9,8},{10,9},{11,1... | collective-permute-start | bytes 2359304 | tf_op jit(solution)/shard_map/ppermute | solution.py:20
  84.5 1.9 copy-done.10
  90.8 3.8 %shard_map.111 = (f32[4,384,192]{2,1,0:T(8,128)S(1)}, f32[4,384,192]{2,1,0:T(8,128)S(1)}) custom-call(s32[4]{0:T(128)S(1)} %pad_add_fusion.ids_ref, bf16[4,2,192,512]{3,2,1,0:T(8,128)(2,1)S(1)} %copy-done.15, bf16[4,2,192,512]{3,2,1,0:T(8,128)(2,1)S(1)} %copy-done.22, bf16[4,2,192,512]{3,2,1,0:T(8,128)(2,1)S(1)} %copy-done.19, ...), custom_call_target="tpu_custom_call" | custom-call | flops 3623878656 | bytes 14680064 | tf_op jit(solution)/shard_map/pallas_call | solution.py:320
  94.6 4.4 %collective-permute-done.4.lo.refs_2_ = bf16[2,2,192,512]{3,2,1,0:T(8,128)(2,1)} collective-permute-done((bf16[2,2,192,512]{3,2,1,0:T(8,128)(2,1)}, bf16[2,2,192,512]{3,2,1,0:T(8,128)(2,1)}, u32[]{:S(2)}, u32[]{:S(2)}) %collective-permute-start.4) | collective-permute-done | bytes 786464 | tf_op jit(solution)/shard_map/ppermute | solution.py:20
  99.7 5.8 %shard_map.112 = (bf16[4,192,2048]{2,1,0:T(8,128)(2,1)S(1)}, bf16[4,192,2048]{2,1,0:T(8,128)(2,1)S(1)}, bf16[4,384,192]{2,1,0:T(8,128)(2,1)S(1)}, f32[4,384,192]{2,1,0:T(8,128)S(1)}, f32[4,384,192]{2,1,0:T(8,128)S(1)}) custom-call(s32[4]{0:T(128)S(1)} %pad_add_fusion.ids_ref, bf16[2,2,192,512]{3,2,1,0:T(8,128)(2,1)} %collective-permute-done.4.lo.refs_2_, ...), custom_call_target="tpu_custom_call" | custom-call | flops 3623878656 | bytes 18874368 | tf_op jit(solution)/shard_map/pallas_call | solution.py:320
  111.7 3.5 %copy-done.24 = bf16[8448,512]{1,0:T(8,128)(2,1)S(1)} copy-done((bf16[8448,512]{1,0:T(8,128)(2,1)S(1)}, bf16[8448,512]{1,0:T(8,128)(2,1)}, u32[]{:S(2)}) %copy-start.24) | copy-done | bytes 8650776
  115.2 7.6 %shard_map.113 = (bf16[4,192,2048]{2,1,0:T(8,128)(2,1)S(1)}, bf16[4,192,2048]{2,1,0:T(8,128)(2,1)S(1)}, bf16[4,384,512]{2,1,0:T(8,128)(2,1)S(1)}) custom-call(s32[4]{0:T(128)S(1)} %pad_add_fusion.ids_ref, bf16[16,528,512]{2,1,0:T(8,128)(2,1)S(1)} %bitcast.49), custom_call_target="tpu_custom_call" | custom-call | flops 4294967296 | bytes 18874368 | tf_op jit(solution)/shard_map/pallas_call | solution.py:105
  123.5 3.3 %shard_map.114 = (bf16[2,2,128,512]{3,2,1,0:T(8,128)(2,1)S(1)}, bf16[2,2,128,512]{3,2,1,0:T(8,128)(2,1)S(1)}, bf16[2,2,128,512]{3,2,1,0:T(8,128)(2,1)S(1)}, bf16[2,2,128,512]{3,2,1,0:T(8,128)(2,1)S(1)}) custom-call(s32[4]{0:T(128)S(1)} %pad_add_fusion.ids_ref, bf16[4,384,512]{2,1,0:T(8,128)(2,1)S(1)} %get-tuple-element.79.map_ref.map2_ref, ...), custom_call_target="tpu_custom_call" | custom-call | flops 1073741824 | bytes 4194304 | tf_op jit(solution)/shard_map/pallas_call | solution.py:195
  130.9 10.1 %shard_map.115 = (bf16[4,384,192]{2,1,0:T(8,128)(2,1)S(1)}, bf16[4,384,192]{2,1,0:T(8,128)(2,1)S(1)}, bf16[4,4,2,192,512]{4,3,2,1,0:T(8,128)(2,1)S(1)}) custom-call(s32[4]{0:T(128)S(1)} %pad_add_fusion.ids_ref, bf16[4,192,2048]{2,1,0:T(8,128)(2,1)S(1)} %get-tuple-element.75.own.refs_5_, bf16[4,192,2048]{2,1,0:T(8,128)(2,1)S(1)} %collective-permute-done.8.sib.refs_6_, ...), custom_call_target="tpu_custom_call" | custom-call | flops 5435817984 | bytes 27262976 | tf_op jit(solution)/shard_map/pallas_call | solution.py:320
  141.0 2.7 %copy-done.6 = bf16[4,4,2,192,512]{4,3,2,1,0:T(8,128)(2,1)} copy-done((bf16[4,4,2,192,512]{4,3,2,1,0:T(8,128)(2,1)}, bf16[4,4,2,192,512]{4,3,2,1,0:T(8,128)(2,1)S(1)}, u32[]{:S(2)}) %copy-start.6) | copy-done | bytes 6291480
  150.2 1.9 collective-permute-start.12
  152.1 1.9 copy-done.3
  155.5 6.2 %shard_map.116 = (bf16[4,2,128,512]{3,2,1,0:T(8,128)(2,1)S(1)}, bf16[4,2,128,512]{3,2,1,0:T(8,128)(2,1)S(1)}, bf16[4,2,128,512]{3,2,1,0:T(8,128)(2,1)S(1)}, bf16...) custom-call(s32[4]{0:T(128)S(1)} %pad_add_fusion.ids_ref, ...), custom_call_target="tpu_custom_call" | custom-call | flops 3221225472 | bytes 12582912 | tf_op jit(solution)/shard_map/pallas_call | solution.py:195
  161.8 3.2 %collective-permute-done.11 = bf16[2,2,128,512]{3,2,1,0:T(8,128)(2,1)S(1)} collective-permute-done((bf16[2,2,128,512]{3,2,1,0:T(8,128)(2,1)}, bf16[2,2,128,512]{3,2,1,0:T(8,128)(2,1)S(1)}, u32[]{:S(2)}, u32[]{:S(2)}) %collective-permute-start.11) | collective-permute-done | bytes 524320 | tf_op jit(solution)/shard_map/ppermute | solution.py:20
  168.4 3.1 %collective-permute-start.16 = (bf16[4,2,128,512]{3,2,1,0:T(8,128)(2,1)S(1)}, bf16[4,2,128,512]{3,2,1,0:T(8,128)(2,1)S(1)}, u32[]{:S(2)}, u32[]{:S(2)}) collective-permute-start(bf16[4,2,128,512]{3,2,1,0:T(8,128)(2,1)S(1)} %pad_maximum_fusion.3), channel_id=1, source_target_pairs={{4,0},{8,4},{12,8},{0,12},{5,1},{9,5},{13,9},{1,13},{6,2},{10,6},{... | collective-permute-start | bytes 3145736 | tf_op jit(solution)/shard_map/ppermute | solution.py:20
  171.6 8.8 %shard_map.117 = (bf16[4,192,2048]{2,1,0:T(8,128)(2,1)}, bf16[4,192,2048]{2,1,0:T(8,128)(2,1)}, bf16[4,192,2048]{2,1,0:T(8,128)(2,1)}) custom-call(s32[4]{0:T(128)S(1)} %pad_add_fusion.ids_ref, bf16[4,2,192,512]{3,2,1,0:T(8,128)(2,1)S(1)} %copy-done.16, bf16[4,2,192,512]{3,2,1,0:T(8,128)(2,1)S(1)} %copy-done.23, ...), custom_call_target="tpu_custom_call" | custom-call | flops 5435817984 | bytes 25165824 | tf_op jit(solution)/shard_map/pallas_call | solution.py:320
  180.4 11.2 %collective-permute-done.14 = bf16[4,2,128,512]{3,2,1,0:T(8,128)(2,1)S(1)} collective-permute-done((bf16[4,2,128,512]{3,2,1,0:T(8,128)(2,1)S(1)}, bf16[4,2,128,512]{3,2,1,0:T(8,128)(2,1)S(1)}, u32[]{:S(2)}, u32[]{:S(2)}) %collective-permute-start.14) | collective-permute-done | bytes 1048608 | tf_op jit(solution)/shard_map/ppermute | solution.py:20
  191.7 2.5 collective-permute-done.13
  194.6 2.5 collective-permute-done.15
  199.8 2.8 %collective-permute-start.22 = (bf16[2,128,512]{2,1,0:T(8,128)(2,1)S(1)}, bf16[2,128,512]{2,1,0:T(8,128)(2,1)S(1)}, u32[]{:S(2)}, u32[]{:S(2)}) collective-permute-start(bf16[2,128,512]{2,1,0:T(8,128)(2,1)S(1)} %get-tuple-element.134), channel_id=1, source_target_pairs={{32,0},{64,32},{96,64},{0,96},{33,1},{65,33},{97,65},{1,97},{34,2}... | collective-permute-start | bytes 786440 | tf_op jit(solution)/shard_map/ppermute | solution.py:20
  202.6 4.3 %collective-permute-done.19 = bf16[2,128,512]{2,1,0:T(8,128)(2,1)S(1)} collective-permute-done((bf16[2,128,512]{2,1,0:T(8,128)(2,1)S(1)}, bf16[2,128,512]{2,1,0:T(8,128)(2,1)S(1)}, u32[]{:S(2)}, u32[]{:S(2)}) %collective-permute-start.19) | collective-permute-done | bytes 262176 | tf_op jit(solution)/shard_map/ppermute | solution.py:20
  208.9 3.4 %collective-permute-done.17 = bf16[2,128,512]{2,1,0:T(8,128)(2,1)S(1)} collective-permute-done((bf16[2,128,512]{2,1,0:T(8,128)(2,1)S(1)}, bf16[2,128,512]{2,1,0:T(8,128)(2,1)S(1)}, u32[]{:S(2)}, u32[]{:S(2)}) %collective-permute-start.17) | collective-permute-done | bytes 262176 | tf_op jit(solution)/shard_map/ppermute | solution.py:20
  212.8 2.7 %collective-permute-done.20 = bf16[2,128,512]{2,1,0:T(8,128)(2,1)S(1)} collective-permute-done((bf16[2,128,512]{2,1,0:T(8,128)(2,1)S(1)}, bf16[2,128,512]{2,1,0:T(8,128)(2,1)S(1)}, u32[]{:S(2)}, u32[]{:S(2)}) %collective-permute-start.20) | collective-permute-done | bytes 262176 | tf_op jit(solution)/shard_map/ppermute | solution.py:20
  218.9 5.6 %all-to-all-start.1 = ((bf16[32,48,512]{2,1,0:T(8,128)(2,1)}), bf16[32,48,512]{2,1,0:T(8,128)(2,1)S(1)}, u32[]{:S(2)}, u32[]{:S(2)}) async-start(bf16[32,48,512]{2,1,0:T(8,128)(2,1)} %bitcast.24), calls=%async_computation.2 | async-start | bytes 3145728 | tf_op jit(solution)/shard_map/all_to_all | solution.py:459
  224.5 2.7 %collective-permute-start.25 = (bf16[128,512]{1,0:T(8,128)(2,1)S(1)}, bf16[128,512]{1,0:T(8,128)(2,1)S(1)}, u32[]{:S(2)}, u32[]{:S(2)}) collective-permute-start(bf16[128,512]{1,0:T(8,128)(2,1)S(1)} %get-tuple-element.140), channel_id=1, source_target_pairs={{1,0},{2,1},{3,2},{0,3},{5,4},{6,5},{7,6},{4,7},{9,8},{10,9},{11,1... | collective-permute-start | bytes 393224 | tf_op jit(solution)/shard_map/ppermute | solution.py:20
  228.7 4.5 %collective-permute-done.25 = bf16[128,512]{1,0:T(8,128)(2,1)S(1)} collective-permute-done((bf16[128,512]{1,0:T(8,128)(2,1)S(1)}, bf16[128,512]{1,0:T(8,128)(2,1)S(1)}, u32[]{:S(2)}, u32[]{:S(2)}) %collective-permute-start.25) | collective-permute-done | bytes 131104 | tf_op jit(solution)/shard_map/ppermute | solution.py:20
  237.6 9.6 %all-to-all-done.1 = bf16[32,48,512]{2,1,0:T(8,128)(2,1)S(1)} async-done(((bf16[32,48,512]{2,1,0:T(8,128)(2,1)}), bf16[32,48,512]{2,1,0:T(8,128)(2,1)S(1)}, u32[]{:S(2)}, u32[]{:S(2)}) %all-to-all-start.1) | async-done | bytes 1572896 | tf_op jit(solution)/shard_map/all_to_all | solution.py:459
  (170 shorter events, 59.9 us)
Async XLA Ops:
  10.2 31.3 %all-to-all-start = ((bf16[32,48,512]{2,1,0:T(8,128)(2,1)}), bf16[32,48,512]{2,1,0:T(8,128)(2,1)S(1)}, u32[]{:S(2)}, u32[]{:S(2)}) async-start(bf16[32,48,512]{2,1,0:T(8,128)(2,1)} %bitcast.5), calls=%async_computation | async-start | bytes 3145728 | tf_op jit(solution)/shard_map/all_to_all | solution.py:459
  18.8 92.9 %all-gather.3.cloned.1.call-start = ((), (), s32[]{:S(2)}) async-start(), calls=%async_computation.4 | async-start | bytes 9191424 | tf_op jit(solution)/shard_map/all_gather | solution.py:467
  18.8 8.9 %collective-permute-start = (bf16[128,512]{1,0:T(8,128)(2,1)S(1)}, bf16[128,512]{1,0:T(8,128)(2,1)S(1)}, u32[]{:S(2)}, u32[]{:S(2)}) collective-permute-start(bf16[128,512]{1,0:T(8,128)(2,1)S(1)} %copy-done.45), channel_id=1, source_target_pairs={{1,0},{2,1},{3,2},{0,3},{5,4},{6,5},{7,6},{4,7},{9,8},{10,9},{11,1... | collective-permute-start | bytes 393224 | tf_op jit(solution)/shard_map/ppermute | solution.py:20
  21.7 7.9 %collective-permute-start.1 = (bf16[128,512]{1,0:T(8,128)(2,1)S(1)}, bf16[128,512]{1,0:T(8,128)(2,1)S(1)}, u32[]{:S(2)}, u32[]{:S(2)}) collective-permute-start(bf16[128,512]{1,0:T(8,128)(2,1)S(1)} %copy-done.45), channel_id=1, source_target_pairs={{2,0},{3,1},{0,2},{1,3},{6,4},{7,5},{4,6},{5,7},{10,8},{11,9},{8,1... | collective-permute-start | bytes 393224 | tf_op jit(solution)/shard_map/ppermute | solution.py:20
  22.5 8.9 %collective-permute-start.2 = (bf16[128,512]{1,0:T(8,128)(2,1)S(1)}, bf16[128,512]{1,0:T(8,128)(2,1)S(1)}, u32[]{:S(2)}, u32[]{:S(2)}) collective-permute-start(bf16[128,512]{1,0:T(8,128)(2,1)S(1)} %copy-done.45), channel_id=1, source_target_pairs={{3,0},{0,1},{1,2},{2,3},{7,4},{4,5},{5,6},{6,7},{11,8},{8,9},{9,10... | collective-permute-start | bytes 393224 | tf_op jit(solution)/shard_map/ppermute | solution.py:20
  41.5 174.2 %reduce-scatter.2.cloned.1.call-start = ((), (), s32[]{:S(2)}) async-start(), calls=%async_computation.3 | async-start | bytes 7864320 | tf_op jit(solution)/shard_map/reduce_scatter | solution.py:488
  42.2 42.4 %copy-start.7 = (bf16[4,192,2048]{2,1,0:T(8,128)(2,1)S(1)}, bf16[4,192,2048]{2,1,0:T(8,128)(2,1)}, u32[]{:S(2)}) copy-start(bf16[4,192,2048]{2,1,0:T(8,128)(2,1)} %wg.3) | copy-start | bytes 9437188
  42.2 36.6 %collective-permute-start.3 = (bf16[4,2,192,512]{3,2,1,0:T(8,128)(2,1)S(1)}, bf16[4,2,192,512]{3,2,1,0:T(8,128)(2,1)S(1)}, u32[]{:S(2)}, u32[]{:S(2)}) collective-permute-start(bf16[4,2,192,512]{3,2,1,0:T(8,128)(2,1)S(1)} %shard_map.110.x0.refs_0_), channel_id=1, source_target_pairs={{3,0},{0,1},{1,2},{2,3},{7,4},{4,5},{5,6},{6,7},{11,8},{8,9},{9,10... | collective-permute-start | bytes 4718600 | tf_op jit(solution)/shard_map/ppermute | solution.py:20
  43.7 36.4 %collective-permute-start.5 = (bf16[4,2,192,512]{3,2,1,0:T(8,128)(2,1)S(1)}, bf16[4,2,192,512]{3,2,1,0:T(8,128)(2,1)S(1)}, u32[]{:S(2)}, u32[]{:S(2)}) collective-permute-start(bf16[4,2,192,512]{3,2,1,0:T(8,128)(2,1)S(1)} %shard_map.110.x0.refs_0_), channel_id=1, source_target_pairs={{1,0},{2,1},{3,2},{0,3},{5,4},{6,5},{7,6},{4,7},{9,8},{10,9},{11,1... | collective-permute-start | bytes 4718600 | tf_op jit(solution)/shard_map/ppermute | solution.py:20
  79.8 19.2 %collective-permute-start.4 = (bf16[2,2,192,512]{3,2,1,0:T(8,128)(2,1)}, bf16[2,2,192,512]{3,2,1,0:T(8,128)(2,1)}, u32[]{:S(2)}, u32[]{:S(2)}) collective-permute-start(bf16[2,2,192,512]{3,2,1,0:T(8,128)(2,1)} %slice.88), channel_id=1, source_target_pairs={{3,0},{0,1},{1,2},{2,3},{7,4},{4,5},{5,6},{6,7},{11,8},{8,9},{9,10... | collective-permute-start | bytes 2359304 | tf_op jit(solution)/shard_map/ppermute | solution.py:20
  81.6 18.1 %collective-permute-start.6 = (bf16[2,2,192,512]{3,2,1,0:T(8,128)(2,1)}, bf16[2,2,192,512]{3,2,1,0:T(8,128)(2,1)}, u32[]{:S(2)}, u32[]{:S(2)}) collective-permute-start(bf16[2,2,192,512]{3,2,1,0:T(8,128)(2,1)} %slice.89), channel_id=1, source_target_pairs={{1,0},{2,1},{3,2},{0,3},{5,4},{6,5},{7,6},{4,7},{9,8},{10,9},{11,1... | collective-permute-start | bytes 2359304 | tf_op jit(solution)/shard_map/ppermute | solution.py:20
  111.7 11.1 %collective-permute-start.7 = (bf16[4,192,2048]{2,1,0:T(8,128)(2,1)}, bf16[4,192,2048]{2,1,0:T(8,128)(2,1)S(1)}, u32[]{:S(2)}, u32[]{:S(2)}) collective-permute-start(bf16[4,192,2048]{2,1,0:T(8,128)(2,1)} %copy-done.27), channel_id=1, source_target_pairs={{16,0},{0,16},{17,1},{1,17},{18,2},{2,18},{19,3},{3,19},{20,4},{4,... | collective-permute-start | bytes 9437192 | tf_op jit(solution)/shard_map/ppermute | solution.py:20
  122.9 7.1 %collective-permute-start.8 = (bf16[4,192,2048]{2,1,0:T(8,128)(2,1)S(1)}, bf16[4,192,2048]{2,1,0:T(8,128)(2,1)S(1)}, u32[]{:S(2)}, u32[]{:S(2)}) collective-permute-start(bf16[4,192,2048]{2,1,0:T(8,128)(2,1)S(1)} %get-tuple-element.78), channel_id=1, source_target_pairs={{16,0},{0,16},{17,1},{1,17},{18,2},{2,18},{19,3},{3,19},{20,4},{4,... | collective-permute-start | bytes 9437192 | tf_op jit(solution)/shard_map/ppermute | solution.py:20
  145.6 16.1 %collective-permute-start.9 = (bf16[2,2,128,512]{3,2,1,0:T(8,128)(2,1)}, bf16[2,2,128,512]{3,2,1,0:T(8,128)(2,1)S(1)}, u32[]{:S(2)}, u32[]{:S(2)}) collective-permute-start(bf16[2,2,128,512]{3,2,1,0:T(8,128)(2,1)} %copy-done.37), channel_id=1, source_target_pairs={{96,0},{0,32},{32,64},{64,96},{97,1},{1,33},{33,65},{65,97},{98,2}... | collective-permute-start | bytes 1572872 | tf_op jit(solution)/shard_map/ppermute | solution.py:20
  147.1 14.6 %collective-permute-start.10 = (bf16[2,2,128,512]{3,2,1,0:T(8,128)(2,1)}, bf16[2,2,128,512]{3,2,1,0:T(8,128)(2,1)S(1)}, u32[]{:S(2)}, u32[]{:S(2)}) collective-permute-start(bf16[2,2,128,512]{3,2,1,0:T(8,128)(2,1)} %copy-done.36), channel_id=1, source_target_pairs={{32,0},{64,32},{96,64},{0,96},{33,1},{65,33},{97,65},{1,97},{34,2}... | collective-permute-start | bytes 1572872 | tf_op jit(solution)/shard_map/ppermute | solution.py:20
  148.9 16.1 %collective-permute-start.11 = (bf16[2,2,128,512]{3,2,1,0:T(8,128)(2,1)}, bf16[2,2,128,512]{3,2,1,0:T(8,128)(2,1)S(1)}, u32[]{:S(2)}, u32[]{:S(2)}) collective-permute-start(bf16[2,2,128,512]{3,2,1,0:T(8,128)(2,1)} %copy-done.35), channel_id=1, source_target_pairs={{12,0},{0,4},{4,8},{8,12},{13,1},{1,5},{5,9},{9,13},{14,2},{2,6},{... | collective-permute-start | bytes 1572872 | tf_op jit(solution)/shard_map/ppermute | solution.py:20
  150.2 14.9 %collective-permute-start.12 = (bf16[2,2,128,512]{3,2,1,0:T(8,128)(2,1)}, bf16[2,2,128,512]{3,2,1,0:T(8,128)(2,1)S(1)}, u32[]{:S(2)}, u32[]{:S(2)}) collective-permute-start(bf16[2,2,128,512]{3,2,1,0:T(8,128)(2,1)} %copy-done.34), channel_id=1, source_target_pairs={{4,0},{8,4},{12,8},{0,12},{5,1},{9,5},{13,9},{1,13},{6,2},{10,6},{... | collective-permute-start | bytes 1572872 | tf_op jit(solution)/shard_map/ppermute | solution.py:20
  166.3 25.4 %collective-permute-start.14 = (bf16[4,2,128,512]{3,2,1,0:T(8,128)(2,1)S(1)}, bf16[4,2,128,512]{3,2,1,0:T(8,128)(2,1)S(1)}, u32[]{:S(2)}, u32[]{:S(2)}) collective-permute-start(bf16[4,2,128,512]{3,2,1,0:T(8,128)(2,1)S(1)} %pad_maximum_fusion.1), channel_id=1, source_target_pairs={{32,0},{64,32},{96,64},{0,96},{33,1},{65,33},{97,65},{1,97},{34,2}... | collective-permute-start | bytes 3145736 | tf_op jit(solution)/shard_map/ppermute | solution.py:20
  167.8 26.4 %collective-permute-start.13 = (bf16[4,2,128,512]{3,2,1,0:T(8,128)(2,1)S(1)}, bf16[4,2,128,512]{3,2,1,0:T(8,128)(2,1)S(1)}, u32[]{:S(2)}, u32[]{:S(2)}) collective-permute-start(bf16[4,2,128,512]{3,2,1,0:T(8,128)(2,1)S(1)} %pad_maximum_fusion), channel_id=1, source_target_pairs={{96,0},{0,32},{32,64},{64,96},{97,1},{1,33},{33,65},{65,97},{98,2}... | collective-permute-start | bytes 3145736 | tf_op jit(solution)/shard_map/ppermute | solution.py:20
  168.4 26.2 %collective-permute-start.16 = (bf16[4,2,128,512]{3,2,1,0:T(8,128)(2,1)S(1)}, bf16[4,2,128,512]{3,2,1,0:T(8,128)(2,1)S(1)}, u32[]{:S(2)}, u32[]{:S(2)}) collective-permute-start(bf16[4,2,128,512]{3,2,1,0:T(8,128)(2,1)S(1)} %pad_maximum_fusion.3), channel_id=1, source_target_pairs={{4,0},{8,4},{12,8},{0,12},{5,1},{9,5},{13,9},{1,13},{6,2},{10,6},{... | collective-permute-start | bytes 3145736 | tf_op jit(solution)/shard_map/ppermute | solution.py:20
  171.5 25.5 %collective-permute-start.15 = (bf16[4,2,128,512]{3,2,1,0:T(8,128)(2,1)S(1)}, bf16[4,2,128,512]{3,2,1,0:T(8,128)(2,1)S(1)}, u32[]{:S(2)}, u32[]{:S(2)}) collective-permute-start(bf16[4,2,128,512]{3,2,1,0:T(8,128)(2,1)S(1)} %pad_maximum_fusion.2), channel_id=1, source_target_pairs={{12,0},{0,4},{4,8},{8,12},{13,1},{1,5},{5,9},{9,13},{14,2},{2,6},{... | collective-permute-start | bytes 3145736 | tf_op jit(solution)/shard_map/ppermute | solution.py:20
  197.6 9.3 %collective-permute-start.19 = (bf16[2,128,512]{2,1,0:T(8,128)(2,1)S(1)}, bf16[2,128,512]{2,1,0:T(8,128)(2,1)S(1)}, u32[]{:S(2)}, u32[]{:S(2)}) collective-permute-start(bf16[2,128,512]{2,1,0:T(8,128)(2,1)S(1)} %get-tuple-element.137), channel_id=1, source_target_pairs={{4,0},{8,4},{12,8},{0,12},{5,1},{9,5},{13,9},{1,13},{6,2},{10,6},{... | collective-permute-start | bytes 786440 | tf_op jit(solution)/shard_map/ppermute | solution.py:20
  198.2 10.7 %collective-permute-start.18 = (bf16[2,128,512]{2,1,0:T(8,128)(2,1)S(1)}, bf16[2,128,512]{2,1,0:T(8,128)(2,1)S(1)}, u32[]{:S(2)}, u32[]{:S(2)}) collective-permute-start(bf16[2,128,512]{2,1,0:T(8,128)(2,1)S(1)} %get-tuple-element.138), channel_id=1, source_target_pairs={{8,0},{12,4},{0,8},{4,12},{9,1},{13,5},{1,9},{5,13},{10,2},{14,6},... | collective-permute-start | bytes 786440 | tf_op jit(solution)/shard_map/ppermute | solution.py:20
  198.8 13.5 %collective-permute-start.17 = (bf16[2,128,512]{2,1,0:T(8,128)(2,1)S(1)}, bf16[2,128,512]{2,1,0:T(8,128)(2,1)S(1)}, u32[]{:S(2)}, u32[]{:S(2)}) collective-permute-start(bf16[2,128,512]{2,1,0:T(8,128)(2,1)S(1)} %get-tuple-element.136), channel_id=1, source_target_pairs={{12,0},{0,4},{4,8},{8,12},{13,1},{1,5},{5,9},{9,13},{14,2},{2,6},{... | collective-permute-start | bytes 786440 | tf_op jit(solution)/shard_map/ppermute | solution.py:20
  199.8 12.7 %collective-permute-start.22 = (bf16[2,128,512]{2,1,0:T(8,128)(2,1)S(1)}, bf16[2,128,512]{2,1,0:T(8,128)(2,1)S(1)}, u32[]{:S(2)}, u32[]{:S(2)}) collective-permute-start(bf16[2,128,512]{2,1,0:T(8,128)(2,1)S(1)} %get-tuple-element.134), channel_id=1, source_target_pairs={{32,0},{64,32},{96,64},{0,96},{33,1},{65,33},{97,65},{1,97},{34,2}... | collective-permute-start | bytes 786440 | tf_op jit(solution)/shard_map/ppermute | solution.py:20
  202.6 10.2 %collective-permute-start.21 = (bf16[2,128,512]{2,1,0:T(8,128)(2,1)S(1)}, bf16[2,128,512]{2,1,0:T(8,128)(2,1)S(1)}, u32[]{:S(2)}, u32[]{:S(2)}) collective-permute-start(bf16[2,128,512]{2,1,0:T(8,128)(2,1)S(1)} %get-tuple-element.135), channel_id=1, source_target_pairs={{64,0},{96,32},{0,64},{32,96},{65,1},{97,33},{1,65},{33,97},{66,2}... | collective-permute-start | bytes 786440 | tf_op jit(solution)/shard_map/ppermute | solution.py:20
  206.9 8.6 %collective-permute-start.20 = (bf16[2,128,512]{2,1,0:T(8,128)(2,1)S(1)}, bf16[2,128,512]{2,1,0:T(8,128)(2,1)S(1)}, u32[]{:S(2)}, u32[]{:S(2)}) collective-permute-start(bf16[2,128,512]{2,1,0:T(8,128)(2,1)S(1)} %get-tuple-element.133), channel_id=1, source_target_pairs={{96,0},{0,32},{32,64},{64,96},{97,1},{1,33},{33,65},{65,97},{98,2}... | collective-permute-start | bytes 786440 | tf_op jit(solution)/shard_map/ppermute | solution.py:20
  218.9 28.3 %all-to-all-start.1 = ((bf16[32,48,512]{2,1,0:T(8,128)(2,1)}), bf16[32,48,512]{2,1,0:T(8,128)(2,1)S(1)}, u32[]{:S(2)}, u32[]{:S(2)}) async-start(bf16[32,48,512]{2,1,0:T(8,128)(2,1)} %bitcast.24), calls=%async_computation.2 | async-start | bytes 3145728 | tf_op jit(solution)/shard_map/all_to_all | solution.py:459
  224.5 23.8 %copy-start.1 = (bf16[128,512]{1,0:T(8,128)(2,1)S(1)}, bf16[128,512]{1,0:T(8,128)(2,1)}, u32[]{:S(2)}) copy-start(bf16[128,512]{1,0:T(8,128)(2,1)} %param.7) | copy-start | bytes 393220
  224.5 8.7 %collective-permute-start.25 = (bf16[128,512]{1,0:T(8,128)(2,1)S(1)}, bf16[128,512]{1,0:T(8,128)(2,1)S(1)}, u32[]{:S(2)}, u32[]{:S(2)}) collective-permute-start(bf16[128,512]{1,0:T(8,128)(2,1)S(1)} %get-tuple-element.140), channel_id=1, source_target_pairs={{1,0},{2,1},{3,2},{0,3},{5,4},{6,5},{7,6},{4,7},{9,8},{10,9},{11,1... | collective-permute-start | bytes 393224 | tf_op jit(solution)/shard_map/ppermute | solution.py:20
  227.2 7.9 %collective-permute-start.24 = (bf16[128,512]{1,0:T(8,128)(2,1)S(1)}, bf16[128,512]{1,0:T(8,128)(2,1)S(1)}, u32[]{:S(2)}, u32[]{:S(2)}) collective-permute-start(bf16[128,512]{1,0:T(8,128)(2,1)S(1)} %get-tuple-element.139), channel_id=1, source_target_pairs={{2,0},{3,1},{0,2},{1,3},{6,4},{7,5},{4,6},{5,7},{10,8},{11,9},{8,1... | collective-permute-start | bytes 393224 | tf_op jit(solution)/shard_map/ppermute | solution.py:20
  227.8 9.1 %collective-permute-start.23 = (bf16[128,512]{1,0:T(8,128)(2,1)S(1)}, bf16[128,512]{1,0:T(8,128)(2,1)S(1)}, u32[]{:S(2)}, u32[]{:S(2)}) collective-permute-start(bf16[128,512]{1,0:T(8,128)(2,1)S(1)} %slice_bitcast_fusion.8), channel_id=1, source_target_pairs={{3,0},{0,1},{1,2},{2,3},{7,4},{4,5},{5,6},{6,7},{11,8},{8,9},{9,10... | collective-permute-start | bytes 393224 | tf_op jit(solution)/shard_map/ppermute | solution.py:20
  (46 other events, 213.1 us)
Sparse Core Ops, SparseCore 0:
  41.6 70.0 all-gather.2
  145.7 64.8 reduce-scatter.1

commit v7 on v6

--- a/solution.py
+++ b/solution.py
@@ -12,7 +12,7 @@
 F32 = jnp.float32
 CAP = 12
 GROUP = ("y", "c", "z")
-VMEM_LIMIT = 20 * 1024 * 1024
+VMEM_LIMIT = 36 * 1024 * 1024
 
 
 def fetch(a, axis, r):

time: 256 us -> 254 us (level)
  waiting for transfers between devices: 107 us -> 101 us
  Pallas kernels: 47.9 us -> 51.1 us
    ppermute x26, waiting for transfers between devices: 85.5 us -> 80.3 us  [fetch(): return lax.ppermute(a, axis, [((i + r) % n, i) for i in range(n)])]
    unnamed x100 -> x96, local copies, waits for them, and re-layouts: 29.9 us -> 30.1 us
  transfers between devices with their start and end apart: 30 -> 30, of which waited for: 23 -> 21; matrix products, arithmetic and copies ran while one was open for 2% -> 2% of each run, Pallas kernels for 14% -> 15%
where the time goes in v7:
time: 254 us; the launch traced here: 253 us
  waiting for transfers between devices  101 us (40%)
  Pallas kernels  51.1 us (20%)
  starting transfers between devices  46.8 us (18%)
  local copies, waits for them, and re-layouts  32.4 us (13%)
  between operations  14.6 us (6%)
  other arithmetic  3.71 us (1%)
  matrix products  3.29 us (1%)
    ppermute x26, waiting for transfers between devices, fetch(): return lax.ppermute(a, axis, [((i + r) % n, i) for i in range(n)])  80.3 us
    ppermute x26, starting transfers between devices, fetch(): return lax.ppermute(a, axis, [((i + r) % n, i) for i in range(n)])  32.1 us
    pallas_call x4, Pallas kernels, per_expert(): pl.pallas_call(kernel, grid_spec=pltpu.PrefetchScalarGridSpec(num_scalar_...  31 us
    unnamed x96, local copies, waits for them, and re-layouts  30.1 us
    all_to_all x2, waiting for transfers between devices, exchange(): return lax.all_to_all(a, GROUP, split_axis=0, concat_axis=0, tiled=True)  20 us
    all_to_all x2, starting transfers between devices, exchange(): return lax.all_to_all(a, GROUP, split_axis=0, concat_axis=0, tiled=True)  14.5 us
    pallas_call x2, Pallas kernels, call(): pl.pallas_call(kernel, grid_spec=pltpu.PrefetchScalarGridSpec(num_scalar_...  9.42 us
    pallas_call x1, Pallas kernels, pick(): pl.pallas_call(pick_kernel, grid=(4,), out_shape=(rows, rows, maps), in_s...  8.33 us
  transfers between devices with their start and end apart: 30, of which 21 were waited for; matrix products, arithmetic and copies ran while one was open for 2% of the time, Pallas kernels for 15%

profile of v7, /device:TPU:0, one launch (start us, length us, event | category | flops | bytes accessed | tf_op | source)
XLA Modules:
  0.0 252.9 jit_solution(16633062033994536424)
XLA Ops:
  10.2 8.5 %all-to-all-start = ((bf16[32,48,512]{2,1,0:T(8,128)(2,1)}), bf16[32,48,512]{2,1,0:T(8,128)(2,1)S(1)}, u32[]{:S(2)}, u32[]{:S(2)}) async-start(bf16[32,48,512]{2,1,0:T(8,128)(2,1)} %bitcast.5), calls=%async_computation | async-start | bytes 3145728 | tf_op jit(solution)/shard_map/all_to_all | solution.py:459
  18.8 2.8 %collective-permute-start = (bf16[128,512]{1,0:T(8,128)(2,1)S(1)}, bf16[128,512]{1,0:T(8,128)(2,1)S(1)}, u32[]{:S(2)}, u32[]{:S(2)}) collective-permute-start(bf16[128,512]{1,0:T(8,128)(2,1)S(1)} %copy-done.43), channel_id=1, source_target_pairs={{1,0},{2,1},{3,2},{0,3},{5,4},{6,5},{7,6},{4,7},{9,8},{10,9},{11,1... | collective-permute-start | bytes 393224 | tf_op jit(solution)/shard_map/ppermute | solution.py:20
  23.4 4.3 %collective-permute-done = bf16[128,512]{1,0:T(8,128)(2,1)S(1)} collective-permute-done((bf16[128,512]{1,0:T(8,128)(2,1)S(1)}, bf16[128,512]{1,0:T(8,128)(2,1)S(1)}, u32[]{:S(2)}, u32[]{:S(2)}) %collective-permute-start) | collective-permute-done | bytes 131104 | tf_op jit(solution)/shard_map/ppermute | solution.py:20
  31.4 10.1 %all-to-all-done = bf16[32,48,512]{2,1,0:T(8,128)(2,1)S(1)} async-done(((bf16[32,48,512]{2,1,0:T(8,128)(2,1)}), bf16[32,48,512]{2,1,0:T(8,128)(2,1)S(1)}, u32[]{:S(2)}, u32[]{:S(2)}) %all-to-all-start) | async-done | bytes 1572896 | tf_op jit(solution)/shard_map/all_to_all | solution.py:459
  46.6 32.2 %collective-permute-done.3.x3.refs_4_ = bf16[4,2,192,512]{3,2,1,0:T(8,128)(2,1)S(1)} collective-permute-done((bf16[4,2,192,512]{3,2,1,0:T(8,128)(2,1)S(1)}, bf16[4,2,192,512]{3,2,1,0:T(8,128)(2,1)S(1)}, u32[]{:S(2)}, u32[]{:S(2)}) %collective-permute-start.3) | collective-permute-done | bytes 1572896 | tf_op jit(solution)/shard_map/ppermute | solution.py:20
  81.6 2.8 %collective-permute-start.6 = (bf16[2,2,192,512]{3,2,1,0:T(8,128)(2,1)}, bf16[2,2,192,512]{3,2,1,0:T(8,128)(2,1)}, u32[]{:S(2)}, u32[]{:S(2)}) collective-permute-start(bf16[2,2,192,512]{3,2,1,0:T(8,128)(2,1)} %slice.89), channel_id=1, source_target_pairs={{1,0},{2,1},{3,2},{0,3},{5,4},{6,5},{7,6},{4,7},{9,8},{10,9},{11,1... | collective-permute-start | bytes 2359304 | tf_op jit(solution)/shard_map/ppermute | solution.py:20
  84.5 1.9 copy-done.9
  90.8 3.8 %shard_map.111 = (f32[4,384,192]{2,1,0:T(8,128)S(1)}, f32[4,384,192]{2,1,0:T(8,128)S(1)}) custom-call(s32[4]{0:T(128)S(1)} %pad_add_fusion.ids_ref, bf16[4,2,192,512]{3,2,1,0:T(8,128)(2,1)S(1)} %copy-done.12, bf16[4,2,192,512]{3,2,1,0:T(8,128)(2,1)S(1)} %copy-done.19, bf16[4,2,192,512]{3,2,1,0:T(8,128)(2,1)S(1)} %copy-done.16, ...), custom_call_target="tpu_custom_call" | custom-call | flops 3623878656 | bytes 14680064 | tf_op jit(solution)/shard_map/pallas_call | solution.py:320
  94.6 4.4 %collective-permute-done.4.lo.refs_2_ = bf16[2,2,192,512]{3,2,1,0:T(8,128)(2,1)} collective-permute-done((bf16[2,2,192,512]{3,2,1,0:T(8,128)(2,1)}, bf16[2,2,192,512]{3,2,1,0:T(8,128)(2,1)}, u32[]{:S(2)}, u32[]{:S(2)}) %collective-permute-start.4) | collective-permute-done | bytes 786464 | tf_op jit(solution)/shard_map/ppermute | solution.py:20
  99.7 6.4 %shard_map.112 = (bf16[4,192,2048]{2,1,0:T(8,128)(2,1)S(1)}, bf16[4,192,2048]{2,1,0:T(8,128)(2,1)S(1)}, bf16[4,384,192]{2,1,0:T(8,128)(2,1)S(1)}, f32[4,384,192]{2,1,0:T(8,128)S(1)}, f32[4,384,192]{2,1,0:T(8,128)S(1)}) custom-call(s32[4]{0:T(128)S(1)} %pad_add_fusion.ids_ref, bf16[2,2,192,512]{3,2,1,0:T(8,128)(2,1)} %collective-permute-done.4.lo.refs_2_, ...), custom_call_target="tpu_custom_call" | custom-call | flops 3623878656 | bytes 18874368 | tf_op jit(solution)/shard_map/pallas_call | solution.py:320
  111.7 3.5 %copy-done.21 = bf16[8448,512]{1,0:T(8,128)(2,1)S(1)} copy-done((bf16[8448,512]{1,0:T(8,128)(2,1)S(1)}, bf16[8448,512]{1,0:T(8,128)(2,1)}, u32[]{:S(2)}) %copy-start.21) | copy-done | bytes 8650776
  115.2 8.3 %shard_map.113 = (bf16[4,192,2048]{2,1,0:T(8,128)(2,1)S(1)}, bf16[4,192,2048]{2,1,0:T(8,128)(2,1)}, bf16[4,384,512]{2,1,0:T(8,128)(2,1)S(1)}) custom-call(s32[4]{0:T(128)S(1)} %pad_add_fusion.ids_ref, bf16[16,528,512]{2,1,0:T(8,128)(2,1)S(1)} %bitcast.48), custom_call_target="tpu_custom_call" | custom-call | flops 4294967296 | bytes 18874368 | tf_op jit(solution)/shard_map/pallas_call | solution.py:105
  124.1 3.3 %shard_map.114 = (bf16[2,2,128,512]{3,2,1,0:T(8,128)(2,1)S(1)}, bf16[2,2,128,512]{3,2,1,0:T(8,128)(2,1)S(1)}, bf16[2,2,128,512]{3,2,1,0:T(8,128)(2,1)S(1)}, bf16[2,2,128,512]{3,2,1,0:T(8,128)(2,1)S(1)}) custom-call(s32[4]{0:T(128)S(1)} %pad_add_fusion.ids_ref, bf16[4,384,512]{2,1,0:T(8,128)(2,1)S(1)} %get-tuple-element.79.map_ref.map2_ref, ...), custom_call_target="tpu_custom_call" | custom-call | flops 1073741824 | bytes 4194304 | tf_op jit(solution)/shard_map/pallas_call | solution.py:195
  132.3 1.9 copy-done.23
  134.2 12.0 %shard_map.115 = (bf16[4,384,192]{2,1,0:T(8,128)(2,1)S(1)}, bf16[4,384,192]{2,1,0:T(8,128)(2,1)S(1)}, bf16[4,4,2,192,512]{4,3,2,1,0:T(8,128)(2,1)}) custom-call(s32[4]{0:T(128)S(1)} %pad_add_fusion.ids_ref, bf16[4,192,2048]{2,1,0:T(8,128)(2,1)S(1)} %get-tuple-element.75.own.refs_5_, bf16[4,192,2048]{2,1,0:T(8,128)(2,1)S(1)} %copy-done.23, ...), custom_call_target="tpu_custom_call" | custom-call | flops 5435817984 | bytes 27262976 | tf_op jit(solution)/shard_map/pallas_call | solution.py:320
  152.6 1.9 collective-permute-start.12
  154.5 1.9 copy-done.3
  158.3 6.2 %shard_map.116 = (bf16[4,2,128,512]{3,2,1,0:T(8,128)(2,1)S(1)}, bf16[4,2,128,512]{3,2,1,0:T(8,128)(2,1)S(1)}, bf16[4,2,128,512]{3,2,1,0:T(8,128)(2,1)S(1)}, bf16...) custom-call(s32[4]{0:T(128)S(1)} %pad_add_fusion.ids_ref, ...), custom_call_target="tpu_custom_call" | custom-call | flops 3221225472 | bytes 12582912 | tf_op jit(solution)/shard_map/pallas_call | solution.py:195
  169.4 3.0 %collective-permute-start.16 = (bf16[4,2,128,512]{3,2,1,0:T(8,128)(2,1)S(1)}, bf16[4,2,128,512]{3,2,1,0:T(8,128)(2,1)S(1)}, u32[]{:S(2)}, u32[]{:S(2)}) collective-permute-start(bf16[4,2,128,512]{3,2,1,0:T(8,128)(2,1)S(1)} %pad_maximum_fusion.3), channel_id=1, source_target_pairs={{4,0},{8,4},{12,8},{0,12},{5,1},{9,5},{13,9},{1,13},{6,2},{10,6},{... | collective-permute-start | bytes 3145736 | tf_op jit(solution)/shard_map/ppermute | solution.py:20
  172.4 8.8 %shard_map.117 = (bf16[4,192,2048]{2,1,0:T(8,128)(2,1)}, bf16[4,192,2048]{2,1,0:T(8,128)(2,1)}, bf16[4,192,2048]{2,1,0:T(8,128)(2,1)}) custom-call(s32[4]{0:T(128)S(1)} %pad_add_fusion.ids_ref, bf16[4,2,192,512]{3,2,1,0:T(8,128)(2,1)S(1)} %copy-done.13, bf16[4,2,192,512]{3,2,1,0:T(8,128)(2,1)S(1)} %copy-done.20, ...), custom_call_target="tpu_custom_call" | custom-call | flops 5435817984 | bytes 25165824 | tf_op jit(solution)/shard_map/pallas_call | solution.py:320
  181.2 9.9 %collective-permute-done.14 = bf16[4,2,128,512]{3,2,1,0:T(8,128)(2,1)S(1)} collective-permute-done((bf16[4,2,128,512]{3,2,1,0:T(8,128)(2,1)S(1)}, bf16[4,2,128,512]{3,2,1,0:T(8,128)(2,1)S(1)}, u32[]{:S(2)}, u32[]{:S(2)}) %collective-permute-start.14) | collective-permute-done | bytes 1048608 | tf_op jit(solution)/shard_map/ppermute | solution.py:20
  191.1 2.5 collective-permute-done.13
  194.0 2.1 collective-permute-done.15
  198.9 2.8 %collective-permute-start.22 = (bf16[2,128,512]{2,1,0:T(8,128)(2,1)S(1)}, bf16[2,128,512]{2,1,0:T(8,128)(2,1)S(1)}, u32[]{:S(2)}, u32[]{:S(2)}) collective-permute-start(bf16[2,128,512]{2,1,0:T(8,128)(2,1)S(1)} %get-tuple-element.134), channel_id=1, source_target_pairs={{32,0},{64,32},{96,64},{0,96},{33,1},{65,33},{97,65},{1,97},{34,2}... | collective-permute-start | bytes 786440 | tf_op jit(solution)/shard_map/ppermute | solution.py:20
  201.7 2.8 %collective-permute-done.19 = bf16[2,128,512]{2,1,0:T(8,128)(2,1)S(1)} collective-permute-done((bf16[2,128,512]{2,1,0:T(8,128)(2,1)S(1)}, bf16[2,128,512]{2,1,0:T(8,128)(2,1)S(1)}, u32[]{:S(2)}, u32[]{:S(2)}) %collective-permute-start.19) | collective-permute-done | bytes 262176 | tf_op jit(solution)/shard_map/ppermute | solution.py:20
  204.8 2.2 collective-permute-done.18
  207.0 2.7 %collective-permute-done.17 = bf16[2,128,512]{2,1,0:T(8,128)(2,1)S(1)} collective-permute-done((bf16[2,128,512]{2,1,0:T(8,128)(2,1)S(1)}, bf16[2,128,512]{2,1,0:T(8,128)(2,1)S(1)}, u32[]{:S(2)}, u32[]{:S(2)}) %collective-permute-start.17) | collective-permute-done | bytes 262176 | tf_op jit(solution)/shard_map/ppermute | solution.py:20
  210.2 2.7 %collective-permute-done.20 = bf16[2,128,512]{2,1,0:T(8,128)(2,1)S(1)} collective-permute-done((bf16[2,128,512]{2,1,0:T(8,128)(2,1)S(1)}, bf16[2,128,512]{2,1,0:T(8,128)(2,1)S(1)}, u32[]{:S(2)}, u32[]{:S(2)}) %collective-permute-start.20) | collective-permute-done | bytes 262176 | tf_op jit(solution)/shard_map/ppermute | solution.py:20
  216.3 6.0 %all-to-all-start.1 = ((bf16[32,48,512]{2,1,0:T(8,128)(2,1)}), bf16[32,48,512]{2,1,0:T(8,128)(2,1)S(1)}, u32[]{:S(2)}, u32[]{:S(2)}) async-start(bf16[32,48,512]{2,1,0:T(8,128)(2,1)} %bitcast.24), calls=%async_computation.2 | async-start | bytes 3145728 | tf_op jit(solution)/shard_map/all_to_all | solution.py:459
  222.3 2.3 collective-permute-start.25
  226.1 4.5 %collective-permute-done.25 = bf16[128,512]{1,0:T(8,128)(2,1)S(1)} collective-permute-done((bf16[128,512]{1,0:T(8,128)(2,1)S(1)}, bf16[128,512]{1,0:T(8,128)(2,1)S(1)}, u32[]{:S(2)}, u32[]{:S(2)}) %collective-permute-start.25) | collective-permute-done | bytes 131104 | tf_op jit(solution)/shard_map/ppermute | solution.py:20
  235.1 9.9 %all-to-all-done.1 = bf16[32,48,512]{2,1,0:T(8,128)(2,1)S(1)} async-done(((bf16[32,48,512]{2,1,0:T(8,128)(2,1)}), bf16[32,48,512]{2,1,0:T(8,128)(2,1)S(1)}, u32[]{:S(2)}, u32[]{:S(2)}) %all-to-all-start.1) | async-done | bytes 1572896 | tf_op jit(solution)/shard_map/all_to_all | solution.py:459
  (166 shorter events, 59.9 us)
Async XLA Ops:
  10.2 31.3 %all-to-all-start = ((bf16[32,48,512]{2,1,0:T(8,128)(2,1)}), bf16[32,48,512]{2,1,0:T(8,128)(2,1)S(1)}, u32[]{:S(2)}, u32[]{:S(2)}) async-start(bf16[32,48,512]{2,1,0:T(8,128)(2,1)} %bitcast.5), calls=%async_computation | async-start | bytes 3145728 | tf_op jit(solution)/shard_map/all_to_all | solution.py:459
  18.8 92.9 %all-gather.3.cloned.1.call-start = ((), (), s32[]{:S(2)}) async-start(), calls=%async_computation.4 | async-start | bytes 9191424 | tf_op jit(solution)/shard_map/all_gather | solution.py:467
  18.8 8.9 %collective-permute-start = (bf16[128,512]{1,0:T(8,128)(2,1)S(1)}, bf16[128,512]{1,0:T(8,128)(2,1)S(1)}, u32[]{:S(2)}, u32[]{:S(2)}) collective-permute-start(bf16[128,512]{1,0:T(8,128)(2,1)S(1)} %copy-done.43), channel_id=1, source_target_pairs={{1,0},{2,1},{3,2},{0,3},{5,4},{6,5},{7,6},{4,7},{9,8},{10,9},{11,1... | collective-permute-start | bytes 393224 | tf_op jit(solution)/shard_map/ppermute | solution.py:20
  21.7 7.9 %collective-permute-start.1 = (bf16[128,512]{1,0:T(8,128)(2,1)S(1)}, bf16[128,512]{1,0:T(8,128)(2,1)S(1)}, u32[]{:S(2)}, u32[]{:S(2)}) collective-permute-start(bf16[128,512]{1,0:T(8,128)(2,1)S(1)} %copy-done.43), channel_id=1, source_target_pairs={{2,0},{3,1},{0,2},{1,3},{6,4},{7,5},{4,6},{5,7},{10,8},{11,9},{8,1... | collective-permute-start | bytes 393224 | tf_op jit(solution)/shard_map/ppermute | solution.py:20
  22.5 8.9 %collective-permute-start.2 = (bf16[128,512]{1,0:T(8,128)(2,1)S(1)}, bf16[128,512]{1,0:T(8,128)(2,1)S(1)}, u32[]{:S(2)}, u32[]{:S(2)}) collective-permute-start(bf16[128,512]{1,0:T(8,128)(2,1)S(1)} %copy-done.43), channel_id=1, source_target_pairs={{3,0},{0,1},{1,2},{2,3},{7,4},{4,5},{5,6},{6,7},{11,8},{8,9},{9,10... | collective-permute-start | bytes 393224 | tf_op jit(solution)/shard_map/ppermute | solution.py:20
  41.5 171.5 %reduce-scatter.2.cloned.1.call-start = ((), (), s32[]{:S(2)}) async-start(), calls=%async_computation.3 | async-start | bytes 7864320 | tf_op jit(solution)/shard_map/reduce_scatter | solution.py:488
  42.2 42.4 %copy-start.6 = (bf16[4,192,2048]{2,1,0:T(8,128)(2,1)S(1)}, bf16[4,192,2048]{2,1,0:T(8,128)(2,1)}, u32[]{:S(2)}) copy-start(bf16[4,192,2048]{2,1,0:T(8,128)(2,1)} %wg.3) | copy-start | bytes 9437188
  42.2 36.6 %collective-permute-start.3 = (bf16[4,2,192,512]{3,2,1,0:T(8,128)(2,1)S(1)}, bf16[4,2,192,512]{3,2,1,0:T(8,128)(2,1)S(1)}, u32[]{:S(2)}, u32[]{:S(2)}) collective-permute-start(bf16[4,2,192,512]{3,2,1,0:T(8,128)(2,1)S(1)} %shard_map.110.x0.refs_0_), channel_id=1, source_target_pairs={{3,0},{0,1},{1,2},{2,3},{7,4},{4,5},{5,6},{6,7},{11,8},{8,9},{9,10... | collective-permute-start | bytes 4718600 | tf_op jit(solution)/shard_map/ppermute | solution.py:20
  43.7 36.3 %collective-permute-start.5 = (bf16[4,2,192,512]{3,2,1,0:T(8,128)(2,1)S(1)}, bf16[4,2,192,512]{3,2,1,0:T(8,128)(2,1)S(1)}, u32[]{:S(2)}, u32[]{:S(2)}) collective-permute-start(bf16[4,2,192,512]{3,2,1,0:T(8,128)(2,1)S(1)} %shard_map.110.x0.refs_0_), channel_id=1, source_target_pairs={{1,0},{2,1},{3,2},{0,3},{5,4},{6,5},{7,6},{4,7},{9,8},{10,9},{11,1... | collective-permute-start | bytes 4718600 | tf_op jit(solution)/shard_map/ppermute | solution.py:20
  79.8 19.2 %collective-permute-start.4 = (bf16[2,2,192,512]{3,2,1,0:T(8,128)(2,1)}, bf16[2,2,192,512]{3,2,1,0:T(8,128)(2,1)}, u32[]{:S(2)}, u32[]{:S(2)}) collective-permute-start(bf16[2,2,192,512]{3,2,1,0:T(8,128)(2,1)} %slice.88), channel_id=1, source_target_pairs={{3,0},{0,1},{1,2},{2,3},{7,4},{4,5},{5,6},{6,7},{11,8},{8,9},{9,10... | collective-permute-start | bytes 2359304 | tf_op jit(solution)/shard_map/ppermute | solution.py:20
  81.6 18.1 %collective-permute-start.6 = (bf16[2,2,192,512]{3,2,1,0:T(8,128)(2,1)}, bf16[2,2,192,512]{3,2,1,0:T(8,128)(2,1)}, u32[]{:S(2)}, u32[]{:S(2)}) collective-permute-start(bf16[2,2,192,512]{3,2,1,0:T(8,128)(2,1)} %slice.89), channel_id=1, source_target_pairs={{1,0},{2,1},{3,2},{0,3},{5,4},{6,5},{7,6},{4,7},{9,8},{10,9},{11,1... | collective-permute-start | bytes 2359304 | tf_op jit(solution)/shard_map/ppermute | solution.py:20
  111.7 11.8 %collective-permute-start.7 = (bf16[4,192,2048]{2,1,0:T(8,128)(2,1)}, bf16[4,192,2048]{2,1,0:T(8,128)(2,1)S(1)}, u32[]{:S(2)}, u32[]{:S(2)}) collective-permute-start(bf16[4,192,2048]{2,1,0:T(8,128)(2,1)} %copy-done.25), channel_id=1, source_target_pairs={{16,0},{0,16},{17,1},{1,17},{18,2},{2,18},{19,3},{3,19},{20,4},{4,... | collective-permute-start | bytes 9437192 | tf_op jit(solution)/shard_map/ppermute | solution.py:20
  123.5 7.1 %collective-permute-start.8 = (bf16[4,192,2048]{2,1,0:T(8,128)(2,1)}, bf16[4,192,2048]{2,1,0:T(8,128)(2,1)S(1)}, u32[]{:S(2)}, u32[]{:S(2)}) collective-permute-start(bf16[4,192,2048]{2,1,0:T(8,128)(2,1)} %get-tuple-element.78), channel_id=1, source_target_pairs={{16,0},{0,16},{17,1},{1,17},{18,2},{2,18},{19,3},{3,19},{20,4},{4,... | collective-permute-start | bytes 9437192 | tf_op jit(solution)/shard_map/ppermute | solution.py:20
  148.0 16.5 %collective-permute-start.9 = (bf16[2,2,128,512]{3,2,1,0:T(8,128)(2,1)}, bf16[2,2,128,512]{3,2,1,0:T(8,128)(2,1)S(1)}, u32[]{:S(2)}, u32[]{:S(2)}) collective-permute-start(bf16[2,2,128,512]{3,2,1,0:T(8,128)(2,1)} %copy-done.35), channel_id=1, source_target_pairs={{96,0},{0,32},{32,64},{64,96},{97,1},{1,33},{33,65},{65,97},{98,2}... | collective-permute-start | bytes 1572872 | tf_op jit(solution)/shard_map/ppermute | solution.py:20
  149.5 14.9 %collective-permute-start.10 = (bf16[2,2,128,512]{3,2,1,0:T(8,128)(2,1)}, bf16[2,2,128,512]{3,2,1,0:T(8,128)(2,1)S(1)}, u32[]{:S(2)}, u32[]{:S(2)}) collective-permute-start(bf16[2,2,128,512]{3,2,1,0:T(8,128)(2,1)} %copy-done.34), channel_id=1, source_target_pairs={{32,0},{64,32},{96,64},{0,96},{33,1},{65,33},{97,65},{1,97},{34,2}... | collective-permute-start | bytes 1572872 | tf_op jit(solution)/shard_map/ppermute | solution.py:20
  151.3 14.7 %collective-permute-start.11 = (bf16[2,2,128,512]{3,2,1,0:T(8,128)(2,1)}, bf16[2,2,128,512]{3,2,1,0:T(8,128)(2,1)S(1)}, u32[]{:S(2)}, u32[]{:S(2)}) collective-permute-start(bf16[2,2,128,512]{3,2,1,0:T(8,128)(2,1)} %copy-done.33), channel_id=1, source_target_pairs={{12,0},{0,4},{4,8},{8,12},{13,1},{1,5},{5,9},{9,13},{14,2},{2,6},{... | collective-permute-start | bytes 1572872 | tf_op jit(solution)/shard_map/ppermute | solution.py:20
  152.6 13.4 %collective-permute-start.12 = (bf16[2,2,128,512]{3,2,1,0:T(8,128)(2,1)}, bf16[2,2,128,512]{3,2,1,0:T(8,128)(2,1)S(1)}, u32[]{:S(2)}, u32[]{:S(2)}) collective-permute-start(bf16[2,2,128,512]{3,2,1,0:T(8,128)(2,1)} %copy-done.32), channel_id=1, source_target_pairs={{4,0},{8,4},{12,8},{0,12},{5,1},{9,5},{13,9},{1,13},{6,2},{10,6},{... | collective-permute-start | bytes 1572872 | tf_op jit(solution)/shard_map/ppermute | solution.py:20
  167.3 23.8 %collective-permute-start.14 = (bf16[4,2,128,512]{3,2,1,0:T(8,128)(2,1)S(1)}, bf16[4,2,128,512]{3,2,1,0:T(8,128)(2,1)S(1)}, u32[]{:S(2)}, u32[]{:S(2)}) collective-permute-start(bf16[4,2,128,512]{3,2,1,0:T(8,128)(2,1)S(1)} %pad_maximum_fusion.1), channel_id=1, source_target_pairs={{32,0},{64,32},{96,64},{0,96},{33,1},{65,33},{97,65},{1,97},{34,2}... | collective-permute-start | bytes 3145736 | tf_op jit(solution)/shard_map/ppermute | solution.py:20
  168.9 24.7 %collective-permute-start.13 = (bf16[4,2,128,512]{3,2,1,0:T(8,128)(2,1)S(1)}, bf16[4,2,128,512]{3,2,1,0:T(8,128)(2,1)S(1)}, u32[]{:S(2)}, u32[]{:S(2)}) collective-permute-start(bf16[4,2,128,512]{3,2,1,0:T(8,128)(2,1)S(1)} %pad_maximum_fusion), channel_id=1, source_target_pairs={{96,0},{0,32},{32,64},{64,96},{97,1},{1,33},{33,65},{65,97},{98,2}... | collective-permute-start | bytes 3145736 | tf_op jit(solution)/shard_map/ppermute | solution.py:20
  169.4 24.6 %collective-permute-start.16 = (bf16[4,2,128,512]{3,2,1,0:T(8,128)(2,1)S(1)}, bf16[4,2,128,512]{3,2,1,0:T(8,128)(2,1)S(1)}, u32[]{:S(2)}, u32[]{:S(2)}) collective-permute-start(bf16[4,2,128,512]{3,2,1,0:T(8,128)(2,1)S(1)} %pad_maximum_fusion.3), channel_id=1, source_target_pairs={{4,0},{8,4},{12,8},{0,12},{5,1},{9,5},{13,9},{1,13},{6,2},{10,6},{... | collective-permute-start | bytes 3145736 | tf_op jit(solution)/shard_map/ppermute | solution.py:20
  172.3 23.8 %collective-permute-start.15 = (bf16[4,2,128,512]{3,2,1,0:T(8,128)(2,1)S(1)}, bf16[4,2,128,512]{3,2,1,0:T(8,128)(2,1)S(1)}, u32[]{:S(2)}, u32[]{:S(2)}) collective-permute-start(bf16[4,2,128,512]{3,2,1,0:T(8,128)(2,1)S(1)} %pad_maximum_fusion.2), channel_id=1, source_target_pairs={{12,0},{0,4},{4,8},{8,12},{13,1},{1,5},{5,9},{9,13},{14,2},{2,6},{... | collective-permute-start | bytes 3145736 | tf_op jit(solution)/shard_map/ppermute | solution.py:20
  196.7 7.8 %collective-permute-start.19 = (bf16[2,128,512]{2,1,0:T(8,128)(2,1)S(1)}, bf16[2,128,512]{2,1,0:T(8,128)(2,1)S(1)}, u32[]{:S(2)}, u32[]{:S(2)}) collective-permute-start(bf16[2,128,512]{2,1,0:T(8,128)(2,1)S(1)} %get-tuple-element.137), channel_id=1, source_target_pairs={{4,0},{8,4},{12,8},{0,12},{5,1},{9,5},{13,9},{1,13},{6,2},{10,6},{... | collective-permute-start | bytes 786440 | tf_op jit(solution)/shard_map/ppermute | solution.py:20
  197.3 9.7 %collective-permute-start.18 = (bf16[2,128,512]{2,1,0:T(8,128)(2,1)S(1)}, bf16[2,128,512]{2,1,0:T(8,128)(2,1)S(1)}, u32[]{:S(2)}, u32[]{:S(2)}) collective-permute-start(bf16[2,128,512]{2,1,0:T(8,128)(2,1)S(1)} %get-tuple-element.138), channel_id=1, source_target_pairs={{8,0},{12,4},{0,8},{4,12},{9,1},{13,5},{1,9},{5,13},{10,2},{14,6},... | collective-permute-start | bytes 786440 | tf_op jit(solution)/shard_map/ppermute | solution.py:20
  197.9 11.8 %collective-permute-start.17 = (bf16[2,128,512]{2,1,0:T(8,128)(2,1)S(1)}, bf16[2,128,512]{2,1,0:T(8,128)(2,1)S(1)}, u32[]{:S(2)}, u32[]{:S(2)}) collective-permute-start(bf16[2,128,512]{2,1,0:T(8,128)(2,1)S(1)} %get-tuple-element.136), channel_id=1, source_target_pairs={{12,0},{0,4},{4,8},{8,12},{13,1},{1,5},{5,9},{9,13},{14,2},{2,6},{... | collective-permute-start | bytes 786440 | tf_op jit(solution)/shard_map/ppermute | solution.py:20
  198.9 10.9 %collective-permute-start.22 = (bf16[2,128,512]{2,1,0:T(8,128)(2,1)S(1)}, bf16[2,128,512]{2,1,0:T(8,128)(2,1)S(1)}, u32[]{:S(2)}, u32[]{:S(2)}) collective-permute-start(bf16[2,128,512]{2,1,0:T(8,128)(2,1)S(1)} %get-tuple-element.134), channel_id=1, source_target_pairs={{32,0},{64,32},{96,64},{0,96},{33,1},{65,33},{97,65},{1,97},{34,2}... | collective-permute-start | bytes 786440 | tf_op jit(solution)/shard_map/ppermute | solution.py:20
  201.7 8.5 %collective-permute-start.21 = (bf16[2,128,512]{2,1,0:T(8,128)(2,1)S(1)}, bf16[2,128,512]{2,1,0:T(8,128)(2,1)S(1)}, u32[]{:S(2)}, u32[]{:S(2)}) collective-permute-start(bf16[2,128,512]{2,1,0:T(8,128)(2,1)S(1)} %get-tuple-element.135), channel_id=1, source_target_pairs={{64,0},{96,32},{0,64},{32,96},{65,1},{97,33},{1,65},{33,97},{66,2}... | collective-permute-start | bytes 786440 | tf_op jit(solution)/shard_map/ppermute | solution.py:20
  204.5 8.4 %collective-permute-start.20 = (bf16[2,128,512]{2,1,0:T(8,128)(2,1)S(1)}, bf16[2,128,512]{2,1,0:T(8,128)(2,1)S(1)}, u32[]{:S(2)}, u32[]{:S(2)}) collective-permute-start(bf16[2,128,512]{2,1,0:T(8,128)(2,1)S(1)} %get-tuple-element.133), channel_id=1, source_target_pairs={{96,0},{0,32},{32,64},{64,96},{97,1},{1,33},{33,65},{65,97},{98,2}... | collective-permute-start | bytes 786440 | tf_op jit(solution)/shard_map/ppermute | solution.py:20
  216.3 28.7 %all-to-all-start.1 = ((bf16[32,48,512]{2,1,0:T(8,128)(2,1)}), bf16[32,48,512]{2,1,0:T(8,128)(2,1)S(1)}, u32[]{:S(2)}, u32[]{:S(2)}) async-start(bf16[32,48,512]{2,1,0:T(8,128)(2,1)} %bitcast.24), calls=%async_computation.2 | async-start | bytes 3145728 | tf_op jit(solution)/shard_map/all_to_all | solution.py:459
  222.3 23.8 %copy-start.1 = (bf16[128,512]{1,0:T(8,128)(2,1)S(1)}, bf16[128,512]{1,0:T(8,128)(2,1)}, u32[]{:S(2)}) copy-start(bf16[128,512]{1,0:T(8,128)(2,1)} %param.7) | copy-start | bytes 393220
  222.3 8.4 %collective-permute-start.25 = (bf16[128,512]{1,0:T(8,128)(2,1)S(1)}, bf16[128,512]{1,0:T(8,128)(2,1)S(1)}, u32[]{:S(2)}, u32[]{:S(2)}) collective-permute-start(bf16[128,512]{1,0:T(8,128)(2,1)S(1)} %get-tuple-element.140), channel_id=1, source_target_pairs={{1,0},{2,1},{3,2},{0,3},{5,4},{6,5},{7,6},{4,7},{9,8},{10,9},{11,1... | collective-permute-start | bytes 393224 | tf_op jit(solution)/shard_map/ppermute | solution.py:20
  224.6 7.9 %collective-permute-start.24 = (bf16[128,512]{1,0:T(8,128)(2,1)S(1)}, bf16[128,512]{1,0:T(8,128)(2,1)S(1)}, u32[]{:S(2)}, u32[]{:S(2)}) collective-permute-start(bf16[128,512]{1,0:T(8,128)(2,1)S(1)} %get-tuple-element.139), channel_id=1, source_target_pairs={{2,0},{3,1},{0,2},{1,3},{6,4},{7,5},{4,6},{5,7},{10,8},{11,9},{8,1... | collective-permute-start | bytes 393224 | tf_op jit(solution)/shard_map/ppermute | solution.py:20
  225.2 9.2 %collective-permute-start.23 = (bf16[128,512]{1,0:T(8,128)(2,1)S(1)}, bf16[128,512]{1,0:T(8,128)(2,1)S(1)}, u32[]{:S(2)}, u32[]{:S(2)}) collective-permute-start(bf16[128,512]{1,0:T(8,128)(2,1)S(1)} %slice_bitcast_fusion.8), channel_id=1, source_target_pairs={{3,0},{0,1},{1,2},{2,3},{7,4},{4,5},{5,6},{6,7},{11,8},{8,9},{9,10... | collective-permute-start | bytes 393224 | tf_op jit(solution)/shard_map/ppermute | solution.py:20
  (44 other events, 193.2 us)
Sparse Core Ops, SparseCore 0:
  41.6 70.0 all-gather.2
  148.1 63.6 reduce-scatter.1
